TPU v7x, 128 devices: a whole 4x4x4 slice. The times are simulated.
128 devices in a mesh: group: 4 (over z_hi, core), dp: 2 (over z_lo), expert: 16 (over x, y).
Axes of the slice: x: 4, y: 4, z: 4 (z_hi: 2, z_lo: 2; z = z_hi * 2 + z_lo), core: 2. Of those that a mesh axis runs over, the one named last changes fastest.
Arguments:
- tokens: bfloat16 [2, 16384, 768], P(None, ('group', 'dp', 'expert')), may hold values from -24 to 24
- out_grad: bfloat16 [2, 16384, 768], P(None, ('group', 'dp', 'expert')), may hold values from -6 to 6
- expert_ids: int32 [2, 16384, 2], P(None, ('group', 'dp', 'expert')), may hold values from 0 to 16, all different within a row; in each aligned block of 128 rows (0 to 127, 128 to 255, ..., all dimensions but the last counted through in order) at most 22 rows name the same one
- replay: int32 [2, 16384], P(None, ('group', 'dp', 'expert')), may hold values 0 or 1
- frozen_in: bfloat16 [1, 768, 3072], replicated, may hold values from -0.21875 to 0.21875
- frozen_out: bfloat16 [1, 3072, 768], replicated, may hold values from -0.109375 to 0.109375
- gains: float32 [2, 768], P(None, ('dp', 'expert')), may hold values from 0.5 to 1.5
- w_qkv: float32 [768, 2304], P(('dp', 'expert')), may hold values from -0.21875 to 0.21875
- w_proj: float32 [768, 768], P(('dp', 'expert')), may hold values from -1.75 to 1.75
- router: float32 [768, 17], P(('dp', 'expert')), may hold values from -0.15625 to 0.15625
- exp_in: float32 [16, 768, 3072], P('expert', 'group', 'dp'), may hold values from -0.21875 to 0.21875
- exp_out: float32 [16, 3072, 768], P('expert', 'dp', 'group'), may hold values from -0.109375 to 0.109375
- mom_gains: float32 [2, 768], P(None, ('dp', 'expert')), may hold values from -1.5 to 1.5
- mom_qkv: float32 [768, 2304], P(('dp', 'expert')), may hold values from -0.046875 to 0.046875
- mom_proj: float32 [768, 768], P(('dp', 'expert')), may hold values from -0.3125 to 0.3125
- mom_router: float32 [768, 17], P(('dp', 'expert')), may hold values from -0.03125 to 0.03125
- mom_in: float32 [16, 768, 3072], P('expert', 'group', 'dp'), may hold values from -0.046875 to 0.046875
- mom_out: float32 [16, 3072, 768], P('expert', 'dp', 'group'), may hold values from -0.0234375 to 0.0234375
- state_gains: float32 [4, 2, 2, 768], P('group', None, None, ('dp', 'expert'))
- state_qkv: float32 [4, 2, 768, 2304], P('group', None, ('dp', 'expert'))
- state_proj: float32 [4, 2, 768, 768], P('group', None, ('dp', 'expert'))
- state_router: float32 [4, 2, 768, 17], P('group', None, ('dp', 'expert'))
- state_in: float32 [4, 2, 16, 768, 3072], P('group', None, 'expert', None, 'dp')
- state_out: float32 [4, 2, 16, 3072, 768], P('group', None, 'expert', 'dp')
Outputs:
- block_out: bfloat16 [2, 16384, 768], P(None, ('group', 'dp', 'expert'))
- input_grad: float32 [2, 16384, 768], P(None, ('group', 'dp', 'expert'))
- new_gains: float32 [2, 768], P(None, ('dp', 'expert'))
- new_qkv: float32 [768, 2304], P(('dp', 'expert'))
- new_proj: float32 [768, 768], P(('dp', 'expert'))
- new_router: float32 [768, 17], P(('dp', 'expert'))
- new_in: float32 [16, 768, 3072], P('expert', 'group', 'dp')
- new_out: float32 [16, 3072, 768], P('expert', 'dp', 'group')
- new_mom_gains: float32 [2, 768], P(None, ('dp', 'expert'))
- new_mom_qkv: float32 [768, 2304], P(('dp', 'expert'))
- new_mom_proj: float32 [768, 768], P(('dp', 'expert'))
- new_mom_router: float32 [768, 17], P(('dp', 'expert'))
- new_mom_in: float32 [16, 768, 3072], P('expert', 'group', 'dp')
- new_mom_out: float32 [16, 3072, 768], P('expert', 'dp', 'group')
Inputs may be any that keep to these rules, and one draw needn't show every extreme that they name: `expert_ids`: A token's two experts differ. In every inner step the 128 consecutive rows of one device name each expert at most 22 times. Experts 0 to 0 are the frozen ones.
All inputs are finite; a program needn't handle non-finite values. No bound on the sum of `replay` on one device may be relied on, other than what follows from the above.
Results may differ from a plain program's by a relative error of at most 0.034.
Values may be sent and summed in bfloat16 or wider, within the bound.
A program may use at most 256 MiB of HBM per device.

v0:
```python
import jax
import jax.numpy as jnp
from jax import lax
from jax.sharding import PartitionSpec as P

HEADS = 12
LEN = 128
STEPS = 2
STEP = 10


EPS_NORM = 1e-06
BETA_ONE = 0.9
BETA_TWO = 0.95
ADAM_EPS = 1e-08
DECAY = 0.1
OUTER_RATE = 0.7
OUTER_MOMENTUM = 0.9
REPLAY_WEIGHT = 0.25
RATES = (0.6, 0.04, 0.3, 0.03, 0.04, 0.02)


def laid_out(blocks, dim):
    dims = list(blocks.shape[1:])
    dims[dim] *= blocks.shape[0]
    return jnp.moveaxis(blocks, 0, dim).reshape(dims)


def from_everyone(array, axis):
    count = lax.axis_size(axis)
    return lax.all_to_all(
        jnp.broadcast_to(array[None], (count, *array.shape)), axis, 0, 0, tiled=True
    )


def collect(array, axis, dim):
    return laid_out(from_everyone(array, axis), dim)


def in_blocks(array, dim, count):
    before, after = (array.shape[:dim], array.shape[dim + 1 :])
    return jnp.moveaxis(array.reshape(*before, count, -1, *after), dim, 0)


def summed_on_arrival(array, axis, dim):
    blocks = in_blocks(array, dim, lax.axis_size(axis))
    arrived = lax.all_to_all(blocks, axis, split_axis=0, concat_axis=0, tiled=True)
    return arrived.astype(jnp.float32).sum(axis=0)


def turned_gather(arrays, axis, dims):
    turned = [jnp.moveaxis(a, dim, 0) for a, dim in zip(arrays, dims)]
    widths = [t[0].size for t in turned]
    both = jnp.concatenate([t.reshape(-1, w) for t, w in zip(turned, widths)], axis=1)
    whole = lax.all_gather(both, axis, axis=0, tiled=True)
    blocks = jnp.split(whole, [sum(widths[:k]) for k in range(1, len(widths))], axis=1)
    return tuple(
        (
            jnp.moveaxis(b.reshape(-1, *t.shape[1:]), 0, dim)
            for b, t, dim in zip(blocks, turned, dims)
        )
    )


def one_scatter(arrays, axis, dims):
    count = lax.axis_size(axis)
    blocks = [in_blocks(a, dim, count) for a, dim in zip(arrays, dims)]
    lines = jnp.concatenate([b.reshape(count, -1) for b in blocks], axis=1)
    span = max(16, -(-lines.shape[1] // 1024) * 8)
    lines = jnp.pad(lines, ((0, 0), (0, span * 128 - lines.shape[1]))).reshape(-1, 128)
    line, at, finished = (lax.psum_scatter(lines, axis, tiled=True).reshape(-1), 0, [])
    for b in blocks:
        part = b[0]
        finished.append(line[at : at + part.size].reshape(part.shape))
        at += part.size
    return tuple(finished)


def as_sent(array):
    return jax.tree.map(lambda a: a.astype(jnp.bfloat16) if a.dtype == jnp.float32 else a, array)


def of_everyone(array, axis):
    everything = from_everyone(array, axis)
    return jnp.sum(everything.astype(jnp.float32), axis=0)


def normalize(values):
    return values * lax.rsqrt(jnp.mean(values * values, axis=-1, keepdims=True) + EPS_NORM)


def norm_back(values, grad_norm):
    scale = lax.rsqrt(jnp.mean(values * values, axis=-1, keepdims=True) + EPS_NORM)
    normed = values * scale
    return scale * (grad_norm - normed * jnp.mean(grad_norm * normed, axis=-1, keepdims=True))


def gelu_exact(values):
    return jax.nn.gelu(values, approximate=False)


def route_table(choices, count, capacity):
    flat = choices.reshape(-1)
    onehot = (flat[:, None] == jnp.arange(count, dtype=jnp.int32)[None, :]).astype(jnp.int32)
    before = jnp.cumsum(onehot, axis=0) - onehot
    slot = jnp.sum(before * onehot, axis=1)
    place = flat * capacity + slot
    marks = jnp.arange(flat.shape[0], dtype=jnp.int32) + 1
    table = jnp.zeros((count * capacity,), jnp.int32).at[place].set(marks)
    return (place, table)


def split_heads(qkv, heads):
    tokens_here, triple = qkv.shape
    size = triple // (3 * heads)
    parts = qkv.reshape(tokens_here // LEN, LEN, 3, heads, size)
    return (parts[:, :, 0], parts[:, :, 1], parts[:, :, 2], size ** (-0.5))


def attend(qkv, heads):
    query, key, value, scale = split_heads(qkv, heads)
    scores = jnp.einsum("sqhd,skhd->shqk", query, key, preferred_element_type=jnp.float32) * scale
    causal = jnp.arange(LEN)[:, None] >= jnp.arange(LEN)[None, :]
    scores = jnp.where(causal, scores, -1e30)
    top = jnp.max(scores, axis=-1, keepdims=True)
    expo = jnp.exp(scores - top)
    probs = expo / jnp.sum(expo, axis=-1, keepdims=True)
    probs_low = probs.astype(jnp.bfloat16)
    mixed = jnp.einsum("shqk,skhd->sqhd", probs_low, value, preferred_element_type=jnp.float32)
    return (probs, probs_low, mixed.reshape(qkv.shape[0], -1).astype(jnp.bfloat16))


def attend_back(qkv, probs, probs_low, grad_mixed, heads):
    query, key, value, scale = split_heads(qkv, heads)
    grad_heads = grad_mixed.reshape(query.shape)
    grad_value = jnp.einsum(
        "shqk,sqhd->skhd", probs_low, grad_heads, preferred_element_type=jnp.float32
    )
    grad_probs = jnp.einsum(
        "sqhd,skhd->shqk", grad_heads, value, preferred_element_type=jnp.float32
    )
    grad_scores = probs * (grad_probs - jnp.sum(probs * grad_probs, axis=-1, keepdims=True))
    grad_low = grad_scores.astype(jnp.bfloat16)
    grad_query = (
        jnp.einsum("shqk,skhd->sqhd", grad_low, key, preferred_element_type=jnp.float32) * scale
    )
    grad_key = (
        jnp.einsum("shqk,sqhd->skhd", grad_low, query, preferred_element_type=jnp.float32) * scale
    )
    stacked = jnp.stack([grad_query, grad_key, grad_value], axis=2)
    return stacked.reshape(qkv.shape).astype(jnp.bfloat16)


def expert_forward(rows, first, second):
    pre = jnp.einsum("secd,edf->secf", rows, first, preferred_element_type=jnp.float32)
    act = gelu_exact(pre).astype(jnp.bfloat16)
    result = jnp.einsum("secf,efd->secd", act, second, preferred_element_type=jnp.float32)
    return (pre, act, result)


def expert_backward(rows, first, second, pre, act, grad_result):
    grad_act = jnp.einsum("secd,efd->secf", grad_result, second, preferred_element_type=jnp.float32)
    unused, gelu_pull = jax.vjp(gelu_exact, pre)
    grad_pre = gelu_pull(grad_act)[0].astype(jnp.bfloat16)
    grad_second = jnp.einsum("secf,secd->efd", act, grad_result, preferred_element_type=jnp.float32)
    grad_first = jnp.einsum("secd,secf->edf", rows, grad_pre, preferred_element_type=jnp.float32)
    grad_rows = jnp.einsum("secf,edf->secd", grad_pre, first, preferred_element_type=jnp.float32)
    return (grad_first, grad_second, grad_rows)


def both_halves(values):
    return collect(values, "dp", 0)


def pair_total(values):
    return summed_on_arrival(values.astype(jnp.bfloat16), "dp", 0)


def adam_step(master, state, grad, rate, number):
    first = BETA_ONE * state[0] + (1.0 - BETA_ONE) * grad
    second = BETA_TWO * state[1] + (1.0 - BETA_TWO) * grad * grad
    fix_one = 1.0 - BETA_ONE**number
    fix_two = 1.0 - BETA_TWO**number
    update = first / fix_one / (jnp.sqrt(second / fix_two) + ADAM_EPS) + DECAY * master
    return (master - rate * update, jnp.stack([first, second]))


def body(
    tokens,
    out_grad,
    expert_ids,
    replay,
    frozen_in,
    frozen_out,
    gains,
    w_qkv,
    w_proj,
    router,
    exp_in,
    exp_out,
    mom_gains,
    mom_qkv,
    mom_proj,
    mom_router,
    mom_in,
    mom_out,
    state_gains,
    state_qkv,
    state_proj,
    state_router,
    state_in,
    state_out,
):
    groups = lax.axis_size("group")
    experts_axis = lax.axis_size("expert")
    frozen = frozen_in.shape[0]
    local = exp_in.shape[0]
    count = frozen + local * experts_axis
    width = tokens.shape[2]
    tok = tokens.shape[1]
    capacity = 3 * tok // count
    start_in, start_out = tuple(
        (
            part.astype(jnp.float32)
            for part in turned_gather(
                (exp_in.astype(jnp.bfloat16), exp_out.astype(jnp.bfloat16)), "group", (1, 2)
            )
        )
    )
    dense = [gains, w_qkv, w_proj, router]
    masters = dense + [start_in, start_out]
    moments = [
        state[0]
        for state in (state_gains, state_qkv, state_proj, state_router, state_in, state_out)
    ]
    block_list = []
    grad_list = []
    for step in range(STEPS):
        dense_low = tuple((value.astype(jnp.bfloat16) for value in masters[:4]))
        gain_b, qkv_b, proj_b, router_b = turned_gather(
            (dense_low[0], dense_low[1], dense_low[2], dense_low[3]), ("dp", "expert"), (1, 0, 0, 0)
        )
        first_b = masters[4].astype(jnp.bfloat16)
        second_b = masters[5].astype(jnp.bfloat16)
        inputs = tokens[step].astype(jnp.float32)
        choices = expert_ids[step]
        factor = jnp.where(replay[step] > 0, REPLAY_WEIGHT, 1.0).astype(jnp.float32)
        cotangent = out_grad[step].astype(jnp.float32) * factor[:, None]
        gain_f = gain_b.astype(jnp.float32)
        normed = normalize(inputs)
        acts = (normed * gain_f[0]).astype(jnp.bfloat16)
        qkv = jnp.dot(acts, qkv_b, preferred_element_type=jnp.float32).astype(jnp.bfloat16)
        probs, probs_low, mixed = attend(qkv, HEADS)
        middle = inputs + jnp.dot(mixed, proj_b, preferred_element_type=jnp.float32)
        normed_mid = normalize(middle)
        routed = (normed_mid * gain_f[1]).astype(jnp.bfloat16)
        logits = jnp.dot(routed, router_b, preferred_element_type=jnp.float32)
        select = (choices[:, :, None] == jnp.arange(count, dtype=jnp.int32)[None, None, :]).astype(
            jnp.float32
        )
        picked = jnp.sum(select * logits[:, None, :], axis=-1)
        picked_top = jnp.max(picked, axis=-1, keepdims=True)
        picked_exp = jnp.exp(picked - picked_top)
        weights = picked_exp / jnp.sum(picked_exp, axis=-1, keepdims=True)
        place, table = route_table(choices, count, capacity)
        doubled = jnp.repeat(routed, 2, axis=0)
        padded = jnp.concatenate([jnp.zeros((1, width), jnp.bfloat16), doubled])
        rows = padded[table].reshape(count, capacity, width)
        frozen_rows = rows[:frozen][None]
        sent = rows[frozen:].reshape(experts_axis, local, capacity, width)
        arrived = lax.all_to_all(sent, "expert", split_axis=0, concat_axis=0, tiled=True)
        frozen_pre, frozen_act, frozen_res = expert_forward(frozen_rows, frozen_in, frozen_out)
        pair_rows_all = both_halves(arrived)
        pre, act, partial_value = expert_forward(pair_rows_all, first_b, second_b)
        result = pair_total(partial_value).astype(jnp.bfloat16)
        returned = lax.all_to_all(result, "expert", split_axis=0, concat_axis=0, tiled=True)
        outputs = jnp.concatenate(
            [frozen_res.reshape(-1, width), returned.reshape(-1, width).astype(jnp.float32)]
        )
        gathered = outputs[place].reshape(tok, 2, width)
        block = middle + jnp.sum(weights[:, :, None] * gathered, axis=1)
        block_list.append(block.astype(jnp.bfloat16))
        grad_pick = jnp.sum(cotangent[:, None, :] * gathered, axis=-1)
        grad_logit_pick = weights * (
            grad_pick - jnp.sum(weights * grad_pick, axis=-1, keepdims=True)
        )
        grad_logits = jnp.sum(select * grad_logit_pick[:, :, None], axis=1)
        grad_router = jnp.dot(
            routed.astype(jnp.float32).T, grad_logits, precision=lax.Precision.HIGHEST
        )
        grad_routed = jnp.dot(
            grad_logits, router_b.astype(jnp.float32).T, precision=lax.Precision.HIGHEST
        )
        grad_choice = (weights[:, :, None] * cotangent[:, None, :]).reshape(2 * tok, width)
        grad_slots = jnp.concatenate([jnp.zeros((1, width), jnp.float32), grad_choice])[table]
        grad_slots = grad_slots.astype(jnp.bfloat16).reshape(count, capacity, width)
        sent_grad = grad_slots[frozen:].reshape(experts_axis, local, capacity, width)
        arrived_grad = lax.all_to_all(sent_grad, "expert", split_axis=0, concat_axis=0, tiled=True)
        unused_first, unused_second, frozen_rows_grad = expert_backward(
            frozen_rows, frozen_in, frozen_out, frozen_pre, frozen_act, grad_slots[:frozen][None]
        )
        pair_grad = both_halves(arrived_grad)
        grad_first, grad_second, partial_rows = expert_backward(
            pair_rows_all, first_b, second_b, pre, act, pair_grad
        )
        back = pair_total(partial_rows).astype(jnp.bfloat16)
        returned_grad = lax.all_to_all(back, "expert", split_axis=0, concat_axis=0, tiled=True)
        grad_outputs = jnp.concatenate(
            [
                frozen_rows_grad.reshape(-1, width),
                returned_grad.reshape(-1, width).astype(jnp.float32),
            ]
        )
        grad_routed = grad_routed + jnp.sum(grad_outputs[place].reshape(tok, 2, width), axis=1)
        grad_gain_two = jnp.sum(normed_mid * grad_routed, axis=0)
        grad_middle = cotangent + norm_back(middle, grad_routed * gain_f[1])
        grad_branch = grad_middle.astype(jnp.bfloat16)
        grad_proj = jnp.einsum("td,te->de", mixed, grad_branch, preferred_element_type=jnp.float32)
        grad_mixed = jnp.einsum(
            "te,de->td", grad_branch, proj_b, preferred_element_type=jnp.float32
        ).astype(jnp.bfloat16)
        grad_qkv = attend_back(qkv, probs, probs_low, grad_mixed, HEADS)
        grad_wqkv = jnp.einsum("td,te->de", acts, grad_qkv, preferred_element_type=jnp.float32)
        grad_acts = jnp.einsum("te,de->td", grad_qkv, qkv_b, preferred_element_type=jnp.float32)
        grad_gain_one = jnp.sum(normed * grad_acts, axis=0)
        grad_list.append(grad_middle + norm_back(inputs, grad_acts * gain_f[0]))
        grad_gains = jnp.stack([grad_gain_one, grad_gain_two])
        dense_grads = tuple(
            (
                part.astype(jnp.float32)
                for part in one_scatter(
                    (
                        grad_gains.astype(jnp.bfloat16),
                        grad_wqkv.astype(jnp.bfloat16),
                        grad_proj.astype(jnp.bfloat16),
                        grad_router.astype(jnp.bfloat16),
                    ),
                    ("dp", "expert"),
                    (1, 0, 0, 0),
                )
            )
        )
        grads = list(dense_grads) + [grad_first, grad_second]
        for index in range(6):
            masters[index], moments[index] = adam_step(
                masters[index], moments[index], grads[index], RATES[index], STEP + step
            )
    expert_deltas = (
        lax.psum_scatter(
            (start_in - masters[4]).astype(jnp.bfloat16), "group", scatter_dimension=1, tiled=True
        ).astype(jnp.float32),
        lax.psum_scatter(
            (start_out - masters[5]).astype(jnp.bfloat16), "group", scatter_dimension=2, tiled=True
        ).astype(jnp.float32),
    )
    dense_deltas = jax.tree.map(
        lambda part: part.astype(jnp.float32),
        jax.tree.map(
            lambda part: of_everyone(part, "group"),
            as_sent(tuple((begin - final for begin, final in zip(dense, masters[:4])))),
        ),
    )
    deltas = list(dense_deltas) + list(expert_deltas)
    outer = dense + [exp_in, exp_out]
    moms = [mom_gains, mom_qkv, mom_proj, mom_router, mom_in, mom_out]
    new_params = []
    new_moms = []
    for delta_sum, begin, moment in zip(deltas, outer, moms):
        delta = delta_sum / groups
        renewed = OUTER_MOMENTUM * moment + delta
        new_moms.append(renewed)
        new_params.append(begin - OUTER_RATE * (delta + OUTER_MOMENTUM * renewed))
    block_out = jnp.stack(block_list)
    input_grad = jnp.stack(grad_list)
    return (
        block_out,
        input_grad,
        new_params[0],
        new_params[1],
        new_params[2],
        new_params[3],
        new_params[4],
        new_params[5],
        new_moms[0],
        new_moms[1],
        new_moms[2],
        new_moms[3],
        new_moms[4],
        new_moms[5],
    )


def solution(mesh):
    return jax.shard_map(
        body,
        mesh=mesh,
        in_specs=(
            P(None, ("group", "dp", "expert"), None),
            P(None, ("group", "dp", "expert"), None),
            P(None, ("group", "dp", "expert"), None),
            P(None, ("group", "dp", "expert")),
            P(),
            P(),
            P(None, ("dp", "expert")),
            P(("dp", "expert"), None),
            P(("dp", "expert"), None),
            P(("dp", "expert"), None),
            P("expert", "group", "dp"),
            P("expert", "dp", "group"),
            P(None, ("dp", "expert")),
            P(("dp", "expert"), None),
            P(("dp", "expert"), None),
            P(("dp", "expert"), None),
            P("expert", "group", "dp"),
            P("expert", "dp", "group"),
            P("group", None, None, ("dp", "expert")),
            P("group", None, ("dp", "expert"), None),
            P("group", None, ("dp", "expert"), None),
            P("group", None, ("dp", "expert"), None),
            P("group", None, "expert", None, "dp"),
            P("group", None, "expert", "dp", None),
        ),
        out_specs=(
            P(None, ("group", "dp", "expert"), None),
            P(None, ("group", "dp", "expert"), None),
            P(None, ("dp", "expert")),
            P(("dp", "expert"), None),
            P(("dp", "expert"), None),
            P(("dp", "expert"), None),
            P("expert", "group", "dp"),
            P("expert", "dp", "group"),
            P(None, ("dp", "expert")),
            P(("dp", "expert"), None),
            P(("dp", "expert"), None),
            P(("dp", "expert"), None),
            P("expert", "group", "dp"),
            P("expert", "dp", "group"),
        ),
        check_vma=False,
    )
```

profile of v0, /device:TPU:1, one launch (start us, length us, event | category | flops | bytes accessed | tf_op | source)
XLA Modules:
  0.0 1277.8 jit_solution(6959501505895528289)
XLA Ops:
  21.7 133.3 %all-gather.4.cloned.1.call-done = bf16[768,3091]{1,0:T(8,128)(2,1)} async-done(((bf16[24,3091]{1,0:T(8,128)(2,1)}), bf16[768,3091]{1,0:T(8,128)(2,1)}) %all-gather.4.cloned.1.call-update) | async-done | bytes 4747792 | tf_op jit(solution)/shard_map/all_gather | solution.py:55
  168.7 6.0 all-to-all-start
  184.1 4.4 all-to-all-start.4
  189.4 8.4 all-to-all-done.4
  200.1 3.6 all-to-all-start.1
  204.8 16.9 %all-to-all-done.1 = bf16[2,16,1,22,768]{4,1,3,2,0:T(8,128)(2,1)S(1)} async-done(((bf16[2,16,1,22,768]{4,1,3,2,0:T(8,128)(2,1)}), bf16[2,16,1,22,768]{4,1,3,2,0:T(8,128)(2,1)S(1)}, u32[]{:S(2)}, u32[]{:S(2)}) %all-to-all-start.1) | async-done | bytes 1081376 | tf_op jit(solution)/shard_map/all_to_all | solution.py:31
  222.8 4.1 all-to-all-start.5
  228.0 4.0 fusion.110
  232.0 11.0 fusion.126
  244.1 3.6 all-to-all-start.2
  247.8 13.5 %fusion.96 = bf16[32,22,1536]{2,0,1:T(8,128)(2,1)S(1)} fusion(f32[1536,32,22]{0,1,2:T(8,128)} %copy-done.140, bf16[32,22,768]{2,0,1:T(8,128)(2,1)S(1)} %bitcast.998, bf16[768,3072]{1,0:T(8,128)(2,1)} %all-gather.6.cloned.1.call-done), kind=kOutput, calls=%fused_computation.138 | convolution fusion | flops 1738801152 | bytes 9928704 | tf_op jit(solution)/shard_map/secd,efd->secf/dot_general | solution.py:162
  261.4 4.3 fusion.120
  266.8 3.6 all-to-all-start.6
  271.0 3.8 fusion.45
  281.0 3.6 all-to-all-start.3
  284.6 7.2 fusion.43
  291.9 3.5 fusion.37
  298.6 6.7 all-to-all-start.7
  337.3 4.0 reshape_reshape.18
  341.4 5.5 fusion.160
  357.5 18.6 %dynamic-update-slice.5 = bf16[32,74184]{1,0:T(8,128)(2,1)} dynamic-update-slice(bf16[32,74184]{1,0:T(8,128)(2,1)} %dynamic-update-slice.4, bf16[32,55296]{1,0:T(8,128)(2,1)S(1)} %reshape_reshape.18, s32[]{} %constant.154, s32[]{} %constant.155) | dynamic-update-slice | bytes 7077892
  376.2 8.7 dynamic-update-slice.6
  386.3 4.9 pad.11
  391.2 6.1 reshape.1163
  398.2 169.1 %reduce-scatter.15.cloned.1.call-done = bf16[584,128]{1,0:T(8,128)(2,1)} async-done(((bf16[18688,128]{1,0:T(8,128)(2,1)}), bf16[584,128]{1,0:T(8,128)(2,1)}) %reduce-scatter.15.cloned.1.call-update) | async-done | bytes 149520
  576.0 7.9 fusion.477
  584.0 6.2 copy.459
  590.2 6.1 copy.460
  598.4 136.3 %all-gather.8.cloned.1.call-done = bf16[768,3091]{1,0:T(8,128)(2,1)} async-done(((bf16[24,3091]{1,0:T(8,128)(2,1)}), bf16[768,3091]{1,0:T(8,128)(2,1)}) %all-gather.8.cloned.1.call-update) | async-done | bytes 4747792 | tf_op jit(solution)/shard_map/all_gather | solution.py:55
  749.3 4.9 all-to-all-start.8
  759.0 4.6 all-to-all-done.8
  763.5 3.8 all-to-all-start.12
  767.3 19.7 %fusion.112 = (bf16[1,1536,768]{1,2,0:T(8,128)(2,1)}, f32[1536,768,1]{0,1,2:T(8,128)}) fusion(f32[1,1,1,1536,768]{3,4,2,1,0:T(8,128)} %copy.459, bf16[768,3072]{1,0:T(8,128)(2,1)} %all-gather.6.cloned.1.call-done, f32[1,1,1,1536,768]{3,4,2,1,0:T(8,128)} %copy.460, bf16[32,22,768]{2,0,1:T(8,128)(2,1)} %bitcast.999, f32[1536,32,22]{0,1,2:T(8,128)} %copy-done.140), kind=kOutput, calls=%fused_computation.154 | convolution fusion | flops 1751285760 | bytes 24281088 | tf_op jit(solution)/shard_map/secf,secd->efd/dot_general | solution.py:165
  788.2 3.6 all-to-all-start.9
  791.8 13.9 %fusion.115 = (bf16[768,1536]{1,0:T(8,128)(2,1)}, f32[768,1536,1]{1,0,2:T(8,128)}) fusion(bf16[768,3072]{1,0:T(8,128)(2,1)} %all-gather.6.cloned.1.call-done, f32[1,2,1,768,1536]{4,3,2,1,0:T(8,128)} %param.46, bf16[32,22,768]{2,0,1:T(8,128)(2,1)} %bitcast.997, bf16[32,22,1536]{2,0,1:T(8,128)(2,1)} %copy-done.139), kind=kOutput, calls=%fused_computation.157 | convolution fusion | flops 1680998400 | bytes 22118400 | tf_op jit(solution)/shard_map/secd,secf->edf/dot_general | solution.py:166
  810.0 3.6 all-to-all-start.13
  815.1 5.5 fusion.106
  820.6 6.2 all-to-all-done.13
  826.9 22.0 %fusion.4 = bf16[1,1536,768]{1,2,0:T(8,128)(2,1)} fusion(bf16[32,22,768]{2,0,1:T(8,128)(2,1)S(1)} %bitcast.1002, f32[1536,768,1]{0,1,2:T(8,128)} %get-tuple-element.78, f32[1,1,1,1536,768]{3,4,2,1,0:T(8,128)} %copy.459, bf16[768,3072]{1,0:T(8,128)(2,1)} %all-gather.6.cloned.1.call-done, f32[1,1,1,1536,768]{3,4,2,1,0:T(8,128)} %copy.460, ...), kind=kOutput, calls=%fused_computation.28 | convolution fusion | flops 1770160128 | bytes 24281088 | tf_op jit(solution)/shard_map/secf,secd->efd/dot_general | solution.py:165
  849.0 14.2 %fusion.97 = bf16[32,22,1536]{2,0,1:T(8,128)(2,1)} fusion(f32[1536,32,22]{0,1,2:T(8,128)} %fusion.106, bf16[32,22,768]{2,0,1:T(8,128)(2,1)S(1)} %bitcast.1003, bf16[1,1536,768]{1,2,0:T(8,128)(2,1)} %get-tuple-element.77), kind=kOutput, calls=%fused_computation.139 | convolution fusion | flops 1738801152 | bytes 9928704 | tf_op jit(solution)/shard_map/secd,efd->secf/dot_general | solution.py:162
  863.2 12.1 fusion.129
  876.3 3.6 all-to-all-start.10
  880.0 4.4 fusion.123
  888.4 3.6 all-to-all-start.14
  892.0 7.1 fusion.39
  900.3 15.1 %all-to-all-done.14 = bf16[2,16,1,22,768]{4,1,3,2,0:T(8,128)(2,1)S(1)} async-done(((bf16[2,16,1,22,768]{4,1,3,2,0:T(8,128)(2,1)}), bf16[2,16,1,22,768]{4,1,3,2,0:T(8,128)(2,1)S(1)}, u32[]{:S(2)}, u32[]{:S(2)}) %all-to-all-start.14) | async-done | bytes 1081376 | tf_op jit(solution)/shard_map/all_to_all | solution.py:47
  915.3 6.1 all-to-all-start.11
  921.5 15.5 %fusion.95 = bf16[1,768,1536]{2,1,0:T(8,128)(2,1)} fusion(bf16[32,22,768]{2,0,1:T(8,128)(2,1)} %bitcast.1001, bf16[32,22,1536]{2,0,1:T(8,128)(2,1)} %fusion.97, bf16[768,3072]{1,0:T(8,128)(2,1)} %all-gather.6.cloned.1.call-done, f32[768,1536,1]{1,0,2:T(8,128)} %get-tuple-element.76, f32[1,2,1,768,1536]{4,3,2,1,0:T(8,128)} %param.46), kind=kOutput, calls=%fused_computation.137 | convolution fusion | flops 1699872768 | bytes 22118400 | tf_op jit(solution)/shard_map/secd,secf->edf/dot_general | solution.py:166
  941.8 6.7 all-to-all-start.15
  974.7 3.7 reshape_reshape.21
  978.5 4.2 fusion.89
  989.2 18.7 %dynamic-update-slice.1 = bf16[32,74184]{1,0:T(8,128)(2,1)} dynamic-update-slice(bf16[32,74184]{1,0:T(8,128)(2,1)} %dynamic-update-slice, bf16[32,55296]{1,0:T(8,128)(2,1)S(1)} %reshape_reshape.21, s32[]{} %constant.154, s32[]{} %constant.155) | dynamic-update-slice | bytes 7077892
  1007.8 8.7 dynamic-update-slice.2
  1018.0 4.8 pad.12
  1022.8 6.1 reshape.1188
  1039.8 158.4 %reduce-scatter.17.cloned.1.call-done = bf16[584,128]{1,0:T(8,128)(2,1)} async-done(((bf16[18688,128]{1,0:T(8,128)(2,1)}), bf16[584,128]{1,0:T(8,128)(2,1)}) %reduce-scatter.17.cloned.1.call-update) | async-done | bytes 149520
  1203.0 29.7 %all-to-all-start.16 = ((bf16[4,2,24]{2,1,0:T(2,128)(2,1)}), bf16[4,2,24]{2,1,0:T(2,128)(2,1)S(1)}, u32[]{:S(2)}, u32[]{:S(2)}) async-start(bf16[4,2,24]{2,1,0:T(2,128)(2,1)} %broadcast_in_dim.70), calls=%async_computation.16 | async-start | bytes 4096 | tf_op jit(solution)/shard_map/all_to_all | solution.py:31
  1233.4 3.8 all-to-all-done.16
  1237.2 3.9 all-to-all-start.19
  1241.7 4.0 all-to-all-done.19
  1246.4 4.0 all-to-all-start.18
  1251.2 4.4 all-to-all-done.18
  1256.4 4.5 all-to-all-start.17
  1261.6 7.9 all-to-all-done.17
  (585 shorter events, 202.7 us)
Async XLA Ops:
  7.2 147.7 %all-gather.4.cloned.1.call-start = ((), (), s32[]{:S(2)}) async-start(), calls=%async_computation.24 | async-start | bytes 5068800 | tf_op jit(solution)/shard_map/all_gather | solution.py:55
  11.5 216.5 %all-gather.6.cloned.1.call-start = ((), (), s32[]{:S(2)}) async-start(), calls=%async_computation.25 | async-start | bytes 5898240 | tf_op jit(solution)/shard_map/all_gather | solution.py:55
  16.0 160.0 %copy-start.96 = (s32[128,2]{0,1:T(2,128)}, s32[128,2]{0,1:T(2,128)S(1)}, u32[]{:S(2)}) copy-start(s32[128,2]{0,1:T(2,128)S(1)} %get-tuple-element.56) | copy-start | bytes 3076
  18.2 141.5 %copy-start.116 = (f32[128]{0:T(128)}, f32[128]{0:T(128)S(1)}, u32[]{:S(2)}) copy-start(f32[128]{0:T(128)S(1)} %get-tuple-element.62) | copy-start | bytes 1540
  21.5 139.0 %copy-start.87 = (pred[128,128]{0,1:T(8,128)(4,1)}, pred[128,128]{0,1:T(8,128)(4,1)S(1)}, u32[]{:S(2)}) copy-start(pred[128,128]{0,1:T(8,128)(4,1)S(1)} %iota_compare_fusion) | copy-start | bytes 49156
  21.6 138.3 %copy-start.129 = (f32[128]{0:T(128)}, f32[128]{0:T(128)S(1)}, u32[]{:S(2)}) copy-start(f32[128]{0:T(128)S(1)} %add_rsqrt_fusion.3) | copy-start | bytes 1540
  168.7 15.3 %all-to-all-start = ((bf16[16,1,22,768]{3,2,1,0:T(8,128)(2,1)}), bf16[16,1,22,768]{3,2,1,0:T(8,128)(2,1)S(1)}, u32[]{:S(2)}, u32[]{:S(2)}) async-start(bf16[16,1,22,768]{3,2,1,0:T(8,128)(2,1)} %bitcast.975), calls=%async_computation | async-start | bytes 1179648 | tf_op jit(solution)/shard_map/all_to_all | solution.py:271
  184.1 13.7 %all-to-all-start.4 = ((bf16[16,1,22,768]{3,2,1,0:T(8,128)(2,1)}), bf16[16,1,22,768]{3,2,1,0:T(8,128)(2,1)S(1)}, u32[]{:S(2)}, u32[]{:S(2)}) async-start(bf16[16,1,22,768]{3,2,1,0:T(8,128)(2,1)} %bitcast.977), calls=%async_computation.4 | async-start | bytes 1179648 | tf_op jit(solution)/shard_map/all_to_all | solution.py:298
  200.1 21.7 %all-to-all-start.1 = ((bf16[2,16,1,22,768]{4,1,3,2,0:T(8,128)(2,1)}), bf16[2,16,1,22,768]{4,1,3,2,0:T(8,128)(2,1)S(1)}, u32[]{:S(2)}, u32[]{:S(2)}) async-start(bf16[2,16,1,22,768]{4,1,3,2,0:T(8,128)(2,1)} %broadcast_in_dim.59), calls=%async_computation.1 | async-start | bytes 2162688 | tf_op jit(solution)/shard_map/all_to_all | solution.py:31
  222.8 21.3 %all-to-all-start.5 = ((bf16[2,16,1,22,768]{4,1,3,2,0:T(8,128)(2,1)}), bf16[2,16,1,22,768]{4,1,3,2,0:T(8,128)(2,1)S(1)}, u32[]{:S(2)}, u32[]{:S(2)}) async-start(bf16[2,16,1,22,768]{4,1,3,2,0:T(8,128)(2,1)} %broadcast_in_dim.63), calls=%async_computation.5 | async-start | bytes 2162688 | tf_op jit(solution)/shard_map/all_to_all | solution.py:31
  244.1 22.7 %all-to-all-start.2 = ((bf16[2,16,1,22,768]{4,1,3,2,0:T(8,128)(2,1)}), bf16[2,16,1,22,768]{4,1,3,2,0:T(8,128)(2,1)S(1)}, u32[]{:S(2)}, u32[]{:S(2)}) async-start(bf16[2,16,1,22,768]{4,1,3,2,0:T(8,128)(2,1)} %copy.362), calls=%async_computation.2 | async-start | bytes 2162688 | tf_op jit(solution)/shard_map/all_to_all | solution.py:47
  266.8 14.3 %all-to-all-start.6 = ((bf16[2,16,1,22,768]{4,1,3,2,0:T(8,128)(2,1)}), bf16[2,16,1,22,768]{4,1,3,2,0:T(8,128)(2,1)S(1)}, u32[]{:S(2)}, u32[]{:S(2)}) async-start(bf16[2,16,1,22,768]{4,1,3,2,0:T(8,128)(2,1)} %copy.372), calls=%async_computation.6 | async-start | bytes 2162688 | tf_op jit(solution)/shard_map/all_to_all | solution.py:47
  281.0 17.6 %all-to-all-start.3 = ((bf16[16,1,22,768]{3,2,1,0:T(8,128)(2,1)}), bf16[16,1,22,768]{3,2,1,0:T(8,128)(2,1)S(1)}, u32[]{:S(2)}, u32[]{:S(2)}) async-start(bf16[16,1,22,768]{3,2,1,0:T(8,128)(2,1)} %copy.364), calls=%async_computation.3 | async-start | bytes 1179648 | tf_op jit(solution)/shard_map/all_to_all | solution.py:276
  298.6 16.6 %all-to-all-start.7 = ((bf16[16,1,22,768]{3,2,1,0:T(8,128)(2,1)}), bf16[16,1,22,768]{3,2,1,0:T(8,128)(2,1)}, u32[]{:S(2)}, u32[]{:S(2)}) async-start(bf16[16,1,22,768]{3,2,1,0:T(8,128)(2,1)} %copy.374), calls=%async_computation.7 | async-start | bytes 1179648 | tf_op jit(solution)/shard_map/all_to_all | solution.py:307
  305.3 262.0 %reduce-scatter.15.cloned.1.call-start = ((), (), s32[]{:S(2)}) async-start(), calls=%async_computation.29 | async-start | bytes 4933632
  397.3 173.6 %copy-start.98 = (f32[2,24]{1,0:T(2,128)S(1)}, f32[2,24]{1,0:T(2,128)}, u32[]{:S(2)}) copy-start(f32[2,24]{1,0:T(2,128)} %param.30) | copy-start | bytes 580
  397.3 173.6 %copy-start.109 = (f32[1,2,2,24]{3,2,1,0:T(2,128)S(1)}, f32[1,2,2,24]{3,2,1,0:T(2,128)}, u32[]{:S(2)}) copy-start(f32[1,2,2,24]{3,2,1,0:T(2,128)} %param.42) | copy-start | bytes 1156
  397.3 174.2 %copy-start.13 = (f32[24,2304]{1,0:T(8,128)S(1)}, f32[24,2304]{1,0:T(8,128)}, u32[]{:S(2)}) copy-start(f32[24,2304]{1,0:T(8,128)} %param.31) | copy-start | bytes 663556
  397.4 174.2 %copy-start.32 = (f32[1,2,24,2304]{3,2,1,0:T(8,128)S(1)}, f32[1,2,24,2304]{3,2,1,0:T(8,128)}, u32[]{:S(2)}) copy-start(f32[1,2,24,2304]{3,2,1,0:T(8,128)} %param.43) | copy-start | bytes 1327108
  397.4 174.4 %copy-start.42 = (f32[24,768]{1,0:T(8,128)S(1)}, f32[24,768]{1,0:T(8,128)}, u32[]{:S(2)}) copy-start(f32[24,768]{1,0:T(8,128)} %param.32) | copy-start | bytes 221188
  397.4 174.4 %copy-start.57 = (f32[1,2,24,768]{3,2,1,0:T(8,128)S(1)}, f32[1,2,24,768]{3,2,1,0:T(8,128)}, u32[]{:S(2)}) copy-start(f32[1,2,24,768]{3,2,1,0:T(8,128)} %param.44) | copy-start | bytes 442372
  397.4 174.5 %copy-start.63 = (f32[24,17]{1,0:T(8,128)S(1)}, f32[24,17]{1,0:T(8,128)}, u32[]{:S(2)}) copy-start(f32[24,17]{1,0:T(8,128)} %param.33) | copy-start | bytes 4900
  397.4 175.4 %copy-start.123 = (s32[1,128,2]{1,2,0:T(2,128)S(1)}, s32[1,128,2]{1,2,0:T(2,128)}, u32[]{:S(2)}) copy-start(s32[1,128,2]{1,2,0:T(2,128)} %get-tuple-element.59) | copy-start | bytes 3076
  397.4 176.7 %copy-start.122 = (s32[1,128,2]{1,2,0:T(2,128)S(1)}, s32[1,128,2]{1,2,0:T(2,128)}, u32[]{:S(2)}) copy-start(s32[1,128,2]{1,2,0:T(2,128)} %get-tuple-element.58) | copy-start | bytes 3076
  397.5 337.3 %all-gather.8.cloned.1.call-start = ((), (), s32[]{:S(2)}) async-start(), calls=%async_computation.26 | async-start | bytes 5068800 | tf_op jit(solution)/shard_map/all_gather | solution.py:55
  398.2 185.8 %copy-start.65 = (f32[1,1,24,17]{3,2,1,0:T(8,128)}, f32[1,1,24,17]{3,2,1,0:T(8,128)S(1)}, u32[]{:S(2)}) copy-start(f32[1,1,24,17]{3,2,1,0:T(8,128)S(1)} %copy.457) | copy-start | bytes 4900
  398.2 185.7 %copy-start.67 = (f32[1,1,24,17]{3,2,1,0:T(8,128)}, f32[1,1,24,17]{3,2,1,0:T(8,128)S(1)}, u32[]{:S(2)}) copy-start(f32[1,1,24,17]{3,2,1,0:T(8,128)S(1)} %copy.458) | copy-start | bytes 4900
  590.2 146.5 %copy-start.7 = (bf16[2,128,768]{2,1,0:T(8,128)(2,1)S(1)}, bf16[2,128,768]{2,1,0:T(8,128)(2,1)}, u32[]{:S(2)}) copy-start(bf16[2,128,768]{2,1,0:T(8,128)(2,1)} %param.24) | copy-start | bytes 1179652
  597.8 142.6 %copy-start.88 = (pred[128,128]{0,1:T(8,128)(4,1)S(1)}, pred[128,128]{0,1:T(8,128)(4,1)}, u32[]{:S(2)}) copy-start(pred[128,128]{0,1:T(8,128)(4,1)} %copy-done.87) | copy-start | bytes 49156
  598.4 137.7 %copy-start.111 = (f32[128]{0:T(128)}, f32[128]{0:T(128)S(1)}, u32[]{:S(2)}) copy-start(f32[128]{0:T(128)S(1)} %get-tuple-element.82) | copy-start | bytes 1540
  749.3 14.2 %all-to-all-start.8 = ((bf16[16,1,22,768]{3,2,1,0:T(8,128)(2,1)}), bf16[16,1,22,768]{3,2,1,0:T(8,128)(2,1)S(1)}, u32[]{:S(2)}, u32[]{:S(2)}) async-start(bf16[16,1,22,768]{3,2,1,0:T(8,128)(2,1)} %bitcast.145), calls=%async_computation.8 | async-start | bytes 1179648 | tf_op jit(solution)/shard_map/all_to_all | solution.py:271
  763.5 23.6 %all-to-all-start.12 = ((bf16[16,1,22,768]{3,2,1,0:T(8,128)(2,1)}), bf16[16,1,22,768]{3,2,1,0:T(8,128)(2,1)S(1)}, u32[]{:S(2)}, u32[]{:S(2)}) async-start(bf16[16,1,22,768]{3,2,1,0:T(8,128)(2,1)} %bitcast.176), calls=%async_computation.12 | async-start | bytes 1179648 | tf_op jit(solution)/shard_map/all_to_all | solution.py:298
  788.2 20.7 %all-to-all-start.9 = ((bf16[2,16,1,22,768]{4,1,3,2,0:T(8,128)(2,1)}), bf16[2,16,1,22,768]{4,1,3,2,0:T(8,128)(2,1)S(1)}, u32[]{:S(2)}, u32[]{:S(2)}) async-start(bf16[2,16,1,22,768]{4,1,3,2,0:T(8,128)(2,1)} %broadcast_in_dim.67), calls=%async_computation.9 | async-start | bytes 2162688 | tf_op jit(solution)/shard_map/all_to_all | solution.py:31
  810.0 16.8 %all-to-all-start.13 = ((bf16[2,16,1,22,768]{4,1,3,2,0:T(8,128)(2,1)}), bf16[2,16,1,22,768]{4,1,3,2,0:T(8,128)(2,1)S(1)}, u32[]{:S(2)}, u32[]{:S(2)}) async-start(bf16[2,16,1,22,768]{4,1,3,2,0:T(8,128)(2,1)} %broadcast_in_dim.69), calls=%async_computation.13 | async-start | bytes 2162688 | tf_op jit(solution)/shard_map/all_to_all | solution.py:31
  813.5 219.4 %reduce-scatter.13.cloned.1.call-start = ((), (), s32[]{:S(2)}) async-start(), calls=%async_computation.28 | async-start | bytes 2949120 | tf_op jit(solution)/shard_map/reduce_scatter | solution.py:352
  849.0 14.2 %copy-start.141 = (f32[1536,32,22]{0,1,2:T(8,128)S(1)}, f32[1536,32,22]{0,1,2:T(8,128)}, u32[]{:S(2)}) copy-start(f32[1536,32,22]{0,1,2:T(8,128)} %fusion.106) | copy-start | bytes 12976132
  876.3 12.0 all-to-all-start.10
  888.4 27.0 %all-to-all-start.14 = ((bf16[2,16,1,22,768]{4,1,3,2,0:T(8,128)(2,1)}), bf16[2,16,1,22,768]{4,1,3,2,0:T(8,128)(2,1)S(1)}, u32[]{:S(2)}, u32[]{:S(2)}) async-start(bf16[2,16,1,22,768]{4,1,3,2,0:T(8,128)(2,1)} %copy.411), calls=%async_computation.14 | async-start | bytes 2162688 | tf_op jit(solution)/shard_map/all_to_all | solution.py:47
  915.3 26.4 %all-to-all-start.11 = ((bf16[16,1,22,768]{3,2,1,0:T(8,128)(2,1)}), bf16[16,1,22,768]{3,2,1,0:T(8,128)(2,1)S(1)}, u32[]{:S(2)}, u32[]{:S(2)}) async-start(bf16[16,1,22,768]{3,2,1,0:T(8,128)(2,1)} %copy.403), calls=%async_computation.11 | async-start | bytes 1179648 | tf_op jit(solution)/shard_map/all_to_all | solution.py:276
  921.5 114.9 %reduce-scatter.11.cloned.1.call-start = ((), (), s32[]{:S(2)}) async-start(), calls=%async_computation.27 | async-start | bytes 2949120 | tf_op jit(solution)/shard_map/reduce_scatter | solution.py:349
  941.8 16.0 %all-to-all-start.15 = ((bf16[16,1,22,768]{3,2,1,0:T(8,128)(2,1)}), bf16[16,1,22,768]{3,2,1,0:T(8,128)(2,1)S(1)}, u32[]{:S(2)}, u32[]{:S(2)}) async-start(bf16[16,1,22,768]{3,2,1,0:T(8,128)(2,1)} %copy.413), calls=%async_computation.15 | async-start | bytes 1179648 | tf_op jit(solution)/shard_map/all_to_all | solution.py:307
  948.5 249.8 %reduce-scatter.17.cloned.1.call-start = ((), (), s32[]{:S(2)}) async-start(), calls=%async_computation.30 | async-start | bytes 4933632
  1032.9 168.6 %copy-start.64 = (f32[24,17]{1,0:T(8,128)S(1)}, f32[24,17]{1,0:T(8,128)}, u32[]{:S(2)}) copy-start(f32[24,17]{1,0:T(8,128)} %param.33) | copy-start | bytes 4900
  1032.9 168.6 %copy-start.66 = (f32[1,1,24,17]{3,2,1,0:T(8,128)S(1)}, f32[1,1,24,17]{3,2,1,0:T(8,128)}, u32[]{:S(2)}) copy-start(f32[1,1,24,17]{3,2,1,0:T(8,128)} %copy-done.65) | copy-start | bytes 4900
  1032.9 168.6 %copy-start.68 = (f32[1,1,24,17]{3,2,1,0:T(8,128)S(1)}, f32[1,1,24,17]{3,2,1,0:T(8,128)}, u32[]{:S(2)}) copy-start(f32[1,1,24,17]{3,2,1,0:T(8,128)} %copy-done.67) | copy-start | bytes 4900
  1033.0 168.6 %copy-start.70 = (f32[24,17]{1,0:T(8,128)S(1)}, f32[24,17]{1,0:T(8,128)}, u32[]{:S(2)}) copy-start(f32[24,17]{1,0:T(8,128)} %copy-done.69) | copy-start | bytes 4900
  1036.2 165.5 %copy-start.43 = (f32[24,768]{1,0:T(8,128)S(1)}, f32[24,768]{1,0:T(8,128)}, u32[]{:S(2)}) copy-start(f32[24,768]{1,0:T(8,128)} %param.32) | copy-start | bytes 221188
  1036.2 165.5 %copy-start.56 = (f32[24,768]{1,0:T(8,128)S(1)}, f32[24,768]{1,0:T(8,128)}, u32[]{:S(2)}) copy-start(f32[24,768]{1,0:T(8,128)} %copy-done.55) | copy-start | bytes 221188
  1036.2 165.5 %copy-start.58 = (f32[1,2,24,768]{3,2,1,0:T(8,128)S(1)}, f32[1,2,24,768]{3,2,1,0:T(8,128)}, u32[]{:S(2)}) copy-start(f32[1,2,24,768]{3,2,1,0:T(8,128)} %param.44) | copy-start | bytes 442372
  1036.2 165.7 %copy-start.14 = (f32[24,2304]{1,0:T(8,128)S(1)}, f32[24,2304]{1,0:T(8,128)}, u32[]{:S(2)}) copy-start(f32[24,2304]{1,0:T(8,128)} %param.31) | copy-start | bytes 663556
  1036.2 165.7 %copy-start.31 = (f32[24,2304]{1,0:T(8,128)S(1)}, f32[24,2304]{1,0:T(8,128)}, u32[]{:S(2)}) copy-start(f32[24,2304]{1,0:T(8,128)} %copy-done.30) | copy-start | bytes 663556
  1036.3 165.7 %copy-start.33 = (f32[1,2,24,2304]{3,2,1,0:T(8,128)S(1)}, f32[1,2,24,2304]{3,2,1,0:T(8,128)}, u32[]{:S(2)}) copy-start(f32[1,2,24,2304]{3,2,1,0:T(8,128)} %param.43) | copy-start | bytes 1327108
  1036.3 166.1 %copy-start.99 = (f32[2,24]{1,0:T(2,128)S(1)}, f32[2,24]{1,0:T(2,128)}, u32[]{:S(2)}) copy-start(f32[2,24]{1,0:T(2,128)} %param.30) | copy-start | bytes 580
  1036.3 166.1 %copy-start.110 = (f32[1,2,2,24]{3,2,1,0:T(2,128)S(1)}, f32[1,2,2,24]{3,2,1,0:T(2,128)}, u32[]{:S(2)}) copy-start(f32[1,2,2,24]{3,2,1,0:T(2,128)} %param.42) | copy-start | bytes 1156
  1036.3 166.1 %copy-start.125 = (f32[2,24]{1,0:T(2,128)S(1)}, f32[2,24]{1,0:T(2,128)}, u32[]{:S(2)}) copy-start(f32[2,24]{1,0:T(2,128)} %copy-done.124) | copy-start | bytes 580
  1036.3 166.1 %copy-start.126 = (f32[2,24]{1,0:T(2,128)S(1)}, f32[2,24]{1,0:T(2,128)}, u32[]{:S(2)}) copy-start(f32[2,24]{1,0:T(2,128)} %get-tuple-element.44) | copy-start | bytes 580
  1036.3 204.8 %copy-start.132 = (f32[2,24]{1,0:T(2,128)S(1)}, f32[2,24]{1,0:T(2,128)}, u32[]{:S(2)}) copy-start(f32[2,24]{1,0:T(2,128)} %param.36) | copy-start | bytes 580
  1036.3 214.2 %copy-start.93 = (f32[24,17]{1,0:T(8,128)S(1)}, f32[24,17]{1,0:T(8,128)}, u32[]{:S(2)}) copy-start(f32[24,17]{1,0:T(8,128)} %param.39) | copy-start | bytes 4900
  1036.3 224.6 %copy-start.71 = (f32[24,768]{1,0:T(8,128)S(1)}, f32[24,768]{1,0:T(8,128)}, u32[]{:S(2)}) copy-start(f32[24,768]{1,0:T(8,128)} %param.38) | copy-start | bytes 221188
  1039.8 229.8 %copy-start.62 = (f32[24,2304]{1,0:T(8,128)S(1)}, f32[24,2304]{1,0:T(8,128)}, u32[]{:S(2)}) copy-start(f32[24,2304]{1,0:T(8,128)} %param.37) | copy-start | bytes 663556
  1203.0 34.2 %all-to-all-start.16 = ((bf16[4,2,24]{2,1,0:T(2,128)(2,1)}), bf16[4,2,24]{2,1,0:T(2,128)(2,1)S(1)}, u32[]{:S(2)}, u32[]{:S(2)}) async-start(bf16[4,2,24]{2,1,0:T(2,128)(2,1)} %broadcast_in_dim.70), calls=%async_computation.16 | async-start | bytes 4096 | tf_op jit(solution)/shard_map/all_to_all | solution.py:31
  1237.2 8.5 all-to-all-start.19
  1246.4 9.2 all-to-all-start.18
  1256.4 13.1 %all-to-all-start.17 = ((bf16[4,24,2304]{2,1,0:T(8,128)(2,1)}), bf16[4,24,2304]{2,1,0:T(8,128)(2,1)S(1)}, u32[]{:S(2)}, u32[]{:S(2)}) async-start(bf16[4,24,2304]{2,1,0:T(8,128)(2,1)} %broadcast_in_dim.71), calls=%async_computation.17 | async-start | bytes 884736 | tf_op jit(solution)/shard_map/all_to_all | solution.py:31
  (106 other events, 542.1 us)
Sparse Core Ops, SparseCore 0:
  11.6 143.2 all-gather.3
  157.2 67.5 all-gather.5
  397.6 169.7 reduce-scatter.14
  572.9 161.7 all-gather.7
  849.1 69.1 reduce-scatter.12
  937.1 57.7 reduce-scatter.10
  1029.1 169.0 reduce-scatter.16
where the time goes:
time: 1290 us; the launch traced here: 1280 us
  waiting for transfers between devices  682 us (53%)
  matrix products  215 us (17%)
  local copies, waits for them, and re-layouts  196 us (15%)
  starting transfers between devices  115 us (9%)
  other arithmetic  53.3 us (4%)
  between operations  17.3 us (1%)
    unnamed x9, waiting for transfers between devices  328 us
    all_gather x3, waiting for transfers between devices, turned_gather(): whole = lax.all_gather(both, axis, axis=0, tiled=True)  270 us
    unnamed x303, local copies, waits for them, and re-layouts  77.6 us
    all_to_all x8, starting transfers between devices, from_everyone(): lax.all_to_all(jnp.broadcast_to(array[None], (count, *array.shape)), axis...  56.9 us
    all_to_all x8, waiting for transfers between devices, from_everyone(): lax.all_to_all(jnp.broadcast_to(array[None], (count, *array.shape)), axis...  43.2 us
    dot_general x2, matrix products, expert_backward(): jnp.einsum('secf,secd->efd', act, grad_result, preferred_element_type=jnp...  41.8 us
    dot_general x4, matrix products, expert_forward(): jnp.einsum('secf,efd->secd', act, second, preferred_element_type=jnp.floa...  30.1 us
    dot_general x2, matrix products, expert_backward(): jnp.einsum('secd,secf->edf', rows, grad_pre, preferred_element_type=jnp.f...  29.4 us
  transfers between devices with their start and end apart: 27, of which 18 were waited for; matrix products, arithmetic and copies ran while one was open for 25% of the time, Pallas kernels for 0%

commit v1 on v0

v1 whole, which is shorter than its diff:
```python
import functools

import jax
import jax.numpy as jnp
from jax import lax
from jax.experimental import pallas as pl
from jax.experimental.pallas import tpu as pltpu
from jax.sharding import PartitionSpec as P

MESH = pl.DeviceIdType.MESH
VMEM = pltpu.VMEM
F32 = jnp.float32
BF16 = jnp.bfloat16


class Links:
    def __init__(self, sends, recvs):
        self.sends, self.recvs, self.used, self.begun = sends, recvs, 0, []

    def make(self, src, dst, to):
        at = self.used
        self.used += 1
        copy = pltpu.make_async_remote_copy(
            src_ref=src, dst_ref=dst, send_sem=self.sends.at[at], recv_sem=self.recvs.at[at],
            device_id=to, device_id_type=MESH,
        )
        self.begun.append(copy)
        return copy

    def send(self, src, dst, to):
        copy = self.make(src, dst, to)
        copy.start()
        return copy

    def finish(self):
        for copy in self.begun:
            copy.wait_send()


class Place:
    def __init__(self):
        self.g, self.d = lax.axis_index("group"), lax.axis_index("dp")
        e = lax.axis_index("expert")
        self.x, self.y = lax.div(e, 4), lax.rem(e, 4)

    def along_x(self, step):
        return {"expert": lax.rem(self.x + step, 4) * 4 + self.y}

    def along_y(self, step):
        return {"expert": self.x * 4 + lax.rem(self.y + step, 4)}

    def other_dp(self):
        return {"dp": 1 - self.d}

    def in_group(self, step):
        return {"group": lax.rem(self.g + step, 4)}

    def other_core(self):
        return {"group": self.g + 1 - 2 * lax.rem(self.g, 2)}


def greet(partners):
    barrier = pltpu.get_barrier_semaphore()
    for partner in partners:
        pl.semaphore_signal(barrier, inc=1, device_id=partner, device_id_type=MESH)
    pl.semaphore_wait(barrier, len(partners))


class Gather:
    def __init__(self, links, place, whole, h, p1, p2, near1, near2, at):
        self.links, self.whole, self.h, self.at = links, whole, h, at
        self.d, self.place = place.d, place
        self.p1, self.p2, self.near1, self.near2 = p1, p2, near1, near2

    def slot(self, k1, k2, dp=None):
        c, x = self.at(lax.rem(k1, 4), lax.rem(k2, 4))
        return self.whole.at[c, slice(None) if dp is None else dp, x, self.h]

    def push(self, k1, k2, dp, to):
        ref = self.slot(k1, k2, dp)
        return self.links.send(ref, ref, to)

    def start(self):
        p1, p2, d = self.p1, self.p2, self.d
        self.over_dp = self.push(p1, p2, d, self.place.other_dp())
        self.own = [self.push(p1, p2, d, self.near1(1)), self.push(p1, p2, d, self.near1(3))]

    def ring_one(self):
        p1, p2, d = self.p1, self.p2, self.d
        self.over_dp.wait_recv()
        self.own += [self.push(p1, p2, 1 - d, self.near1(1)), self.push(p1, p2, 1 - d, self.near1(3))]
        self.pushed = [(p1, self.push(p1, p2, None, self.near2(1)), self.push(p1, p2, None, self.near2(3)))]
        for copy in self.own:
            copy.wait_recv()
        self.passed = [self.push(p1 + 3, p2, 0, self.near1(1)), self.push(p1 + 1, p2, 1, self.near1(3))]
        for k1 in (p1 + 3, p1 + 1):
            self.pushed.append((k1, self.push(k1, p2, None, self.near2(1)), self.push(k1, p2, None, self.near2(3))))

    def ring_two(self):
        p1, p2 = self.p1, self.p2
        for copy in self.passed:
            copy.wait_recv()
        k1 = p1 + 2
        self.pushed.append((k1, self.push(k1, p2, None, self.near2(1)), self.push(k1, p2, None, self.near2(3))))
        self.last = []
        for k1, right, left in self.pushed:
            right.wait_recv()
            self.last.append(self.push(k1, p2 + 3, 0, self.near2(1)))
            left.wait_recv()
            self.last.append(self.push(k1, p2 + 1, 1, self.near2(3)))

    def end(self):
        for copy in self.last:
            copy.wait_recv()


def gather_parts(links, place, whole):
    by_x = lambda kx, ky: (ky, kx)
    by_y = lambda ky, kx: (ky, kx)
    first = Gather(links, place, whole, 0, place.x, place.y, place.along_x, place.along_y, by_x)
    second = Gather(links, place, whole, 1, place.y, place.x, place.along_y, place.along_x, by_y)
    return first, second


def gather_all(links, place, whole):
    parts = gather_parts(links, place, whole)
    for stage in ("start", "ring_one", "ring_two", "end"):
        for part in parts:
            getattr(part, stage)()


class RingSum:
    def __init__(self, links, near, p, term, far, near_buf, add):
        self.links, self.near, self.p, self.term = links, near, p, term
        self.far, self.near_buf, self.add = far, near_buf, add

    def start(self):
        p, links = self.p, self.links
        right, left = self.near(1), self.near(3)
        self.far_copies = [
            links.send(self.term(p + 2, 1), self.far.at[0], right),
            links.send(self.term(p + 2, 0), self.far.at[1], left),
        ]
        self.direct = [
            links.send(self.term(p + 1, 0), self.near_buf.at[0, 0], right),
            links.send(self.term(p + 3, 1), self.near_buf.at[1, 1], left),
        ]

    def middle(self):
        p, links = self.p, self.links
        for side, to, dp, k in ((0, self.near(1), 1, p + 1), (1, self.near(3), 0, p + 3)):
            self.far_copies[side].wait_recv()
            self.far[side] = (self.far[side].astype(F32) + self.term(k, dp)[...].astype(F32)).astype(BF16)
            self.direct.append(links.send(self.far.at[side], self.near_buf.at[side, dp], to))

    def finish(self):
        for copy in self.direct:
            copy.wait_recv()
        return [
            self.term(self.p, dp)[...].astype(F32)
            + self.near_buf[0, dp].astype(F32)
            + self.near_buf[1, dp].astype(F32)
            for dp in range(2)
        ]


def add_over(links, own, box, position, size, reach):
    box[position] = own
    copies = [links.send(box.at[position], box.at[position], reach(step)) for step in range(1, size)]

    def finish():
        for copy in copies:
            copy.wait_recv()
        total = box[0]
        for k in range(1, size):
            total = total + box[k]
        return total

    return finish


def ring_scratch(blocks):
    return [VMEM((2, *blocks, 48, 768), BF16), VMEM((2, 2, *blocks, 48, 768), BF16)]


def reduce_all(links, place, grads, extra, scratch, result):
    (far_a, near_a, far_b, near_b, mid_a, mid_b, far_c, near_c, far_d, near_d, last, zbox, box_x, box_y, box_z) = scratch
    r4 = lambda k: lax.rem(k, 4)
    first = RingSum(links, place.along_y, place.y, lambda k, dp: grads.at[r4(k), dp, :, 0], far_a, near_a, None)
    second = RingSum(links, place.along_x, place.x, lambda k, dp: grads.at[:, dp, r4(k), 1], far_b, near_b, None)
    first.start()
    second.start()
    extra_x = add_over(links, extra[...], box_x, place.x, 4, place.along_x)
    first.middle()
    second.middle()
    extra_y = add_over(links, extra_x(), box_y, place.y, 4, place.along_y)
    for part, mid in ((first, mid_a), (second, mid_b)):
        for dp, value in enumerate(part.finish()):
            mid[dp] = value.astype(BF16)
    third = RingSum(links, place.along_x, place.x, lambda k, dp: mid_a.at[dp, r4(k)], far_c, near_c, None)
    fourth = RingSum(links, place.along_y, place.y, lambda k, dp: mid_b.at[dp, r4(k)], far_d, near_d, None)
    third.start()
    fourth.start()
    total_xy = extra_y()
    extra_z = add_over(links, total_xy, box_z, place.d, 2, lambda step: place.other_dp())
    third.middle()
    fourth.middle()
    over = []
    for h, part in enumerate((third, fourth)):
        for dp, value in enumerate(part.finish()):
            last[dp, h] = value.astype(BF16)
        over.append(links.send(last.at[1 - place.d, h], zbox.at[h], place.other_dp()))
    for h in range(2):
        over[h].wait_recv()
        result[h] = last[place.d, h].astype(F32) + zbox[h].astype(F32)
    return extra_z()


REDUCE_SCRATCH = (
    ring_scratch((4,)) + ring_scratch((4,))
    + [VMEM((2, 4, 48, 768), BF16)] * 2
    + ring_scratch(()) + ring_scratch(())
    + [VMEM((2, 2, 48, 768), BF16), VMEM((2, 48, 768), BF16)]
    + [VMEM((4, 24, 768), F32), VMEM((4, 24, 768), F32), VMEM((2, 24, 768), F32)]
)
REDUCE_COPIES = 4 * 6 + 2 + 7
GATHER_COPIES = 2 * 23


def ring_partners(place):
    return (
        [place.along_x(k) for k in (1, 2, 3)]
        + [place.along_y(k) for k in (1, 2, 3)]
        + [place.other_dp()]
    )


EPS_NORM = 1e-06
BETA_ONE = 0.9
BETA_TWO = 0.95
ADAM_EPS = 1e-08
DECAY = 0.1
OUTER_RATE = 0.7
OUTER_MOMENTUM = 0.9
REPLAY_WEIGHT = 0.25
RATES = (0.6, 0.04, 0.3, 0.03, 0.04, 0.02)
HEADS = 12
LEN = 128
STEPS = 2
STEP = 10


def entry_kernel(p_in, mv_in, e_in, whole, p_out, mv_out, e_out, sends, recvs):
    place = Place()
    greet(ring_partners(place) + [place.other_core()])
    links = Links(sends, recvs)
    x, y, d = place.x, place.y, place.d
    h = lax.rem(place.g, 2)
    masters = [links.send(p_in.at[lax.rem(y + k, 4)], p_out.at[y], place.along_y(k)) for k in (1, 2, 3)]
    e_out[d, x, y] = e_in[...]
    mine = e_out.at[d, x, y]
    extra_z = links.send(mine, mine, place.other_dp())
    p_out[y] = p_in[y]
    mv_out[:, y] = mv_in[:, y]
    for copy in masters:
        copy.wait_recv()
    low = p_out[...].astype(BF16).reshape(2, 48, 768)

    @pl.when(h == 0)
    def _():
        whole[y, d, x, 0] = low[0]

    @pl.when(h == 1)
    def _():
        whole[y, d, x, 1] = low[1]

    def mix(a, b):
        return a * (1 - h) + b * h

    def near1(step):
        return {"expert": mix(place.along_x(step)["expert"], place.along_y(step)["expert"])}

    def near2(step):
        return {"expert": mix(place.along_y(step)["expert"], place.along_x(step)["expert"])}

    def at(k1, k2):
        return mix(k2, k1), mix(k1, k2)

    part = Gather(links, place, whole, h, mix(x, y), mix(y, x), near1, near2, at)
    p1, p2 = part.p1, part.p2
    part.start()
    extra_z.wait_recv()
    mine = e_out.at[:, x, y]
    extra_x = [links.send(mine, mine, place.along_x(k)) for k in (1, 2, 3)]
    part.ring_one()
    share = place.other_core()
    shared = [part.push(k1, p2, None, share) for k1 in (p1, p1 + 3, p1 + 1)]
    for copy in extra_x:
        copy.wait_recv()
    mine = e_out.at[:, :, y]
    extra_y = [links.send(mine, mine, place.along_y(k)) for k in (1, 2, 3)]
    part.ring_two()
    moments = [links.send(mv_in.at[:, lax.rem(y + k, 4)], mv_out.at[:, y], place.along_y(k)) for k in (1, 2, 3)]
    shared.append(part.push(p1 + 2, p2, None, share))
    for k1 in (p1, p1 + 3, p1 + 1, p1 + 2):
        shared += [part.push(k1, p2 + 3, None, share), part.push(k1, p2 + 1, None, share)]
    part.end()
    shared += [part.push(k1, p2 + 2, None, share) for k1 in (p1, p1 + 3, p1 + 1, p1 + 2)]
    for copy in shared:
        copy.wait_recv()
    for copy in extra_y + moments:
        copy.wait_recv()
    links.finish()


def adam_values(master, first, second, grad, rate, number):
    first = BETA_ONE * first + (1.0 - BETA_ONE) * grad
    second = BETA_TWO * second + (1.0 - BETA_TWO) * grad * grad
    fix_one = 1.0 - BETA_ONE**number
    fix_two = 1.0 - BETA_TWO**number
    update = first / fix_one / (jnp.sqrt(second / fix_two) + ADAM_EPS) + DECAY * master
    return master - rate * update, first, second


def block_rate(place):
    return jnp.where(place.y == 3, RATES[2], RATES[1]).astype(F32)


def extra_rates():
    row = lax.broadcasted_iota(jnp.int32, (24, 768), 0)
    return jnp.where(row < 17, RATES[3], RATES[0]).astype(F32)


def renew_kernel(number, grads, extra, p_in, mv_in, pe_in, mve_in,
                 whole, p_out, mv_out, pe_out, mve_out, result, *scratch):
    *scratch, sends, recvs = scratch
    place = Place()
    greet(ring_partners(place))
    links = Links(sends, recvs)
    total = reduce_all(links, place, grads, extra, scratch, result)
    fresh, first, second = adam_values(p_in[...], mv_in[0], mv_in[1], result[...], block_rate(place), number)
    whole[place.y, place.d, place.x] = fresh.astype(BF16)
    gather = gather_parts(links, place, whole)
    for part in gather:
        part.start()
    p_out[...] = fresh
    mv_out[0] = first
    mv_out[1] = second
    pe_out[...], mve_out[0], mve_out[1] = adam_values(pe_in[...], mve_in[0], mve_in[1], total, extra_rates(), number)
    for stage in ("ring_one", "ring_two", "end"):
        for part in gather:
            getattr(part, stage)()
    links.finish()


def final_kernel(number, grads, extra, p_in, mv_in, pe_in, mve_in, p_start, pe_start, w_old, mom_old,
                 w_new, mom_new, delta_e, result, delta, quarters, whole, turned, boxes, *scratch):
    *scratch, sends, recvs = scratch
    place = Place()
    greet(ring_partners(place) + [place.in_group(k) for k in (1, 2, 3)])
    links = Links(sends, recvs)
    g, y = place.g, place.y
    total = reduce_all(links, place, grads, extra, scratch, result)
    fresh, _, _ = adam_values(p_in[...], mv_in[0], mv_in[1], result[...], block_rate(place), number)
    delta[...] = (p_start[...] - fresh).reshape(4, 24, 768)
    summed = [
        links.send(delta.at[lax.rem(g + k, 4)], quarters.at[g], place.in_group(k)) for k in (1, 2, 3)
    ]
    fresh_e, _, _ = adam_values(pe_in[...], mve_in[0], mve_in[1], total, extra_rates(), number)
    sum_e = add_over(links, pe_start[...] - fresh_e, boxes, g, 4, place.in_group)
    quarters[g] = delta[g]
    for copy in summed:
        copy.wait_recv()
    whole[g] = (quarters[0] + quarters[1] + quarters[2] + quarters[3]) * 0.25
    spread = [links.send(whole.at[g], whole.at[g], place.in_group(k)) for k in (1, 2, 3)]
    delta_e[...] = sum_e() * 0.25
    for copy in spread:
        copy.wait_recv()
    turned[y] = whole[y]
    across = [links.send(whole.at[lax.rem(y + k, 4)], turned.at[y], place.along_y(k)) for k in (1, 2, 3)]
    for copy in across:
        copy.wait_recv()
    mean = turned[...]
    renewed = OUTER_MOMENTUM * mom_old[...] + mean
    mom_new[...] = renewed
    w_new[...] = w_old[...] - OUTER_RATE * (mean + OUTER_MOMENTUM * renewed)
    links.finish()


def semaphores(count):
    return [pltpu.SemaphoreType.DMA((count,)), pltpu.SemaphoreType.DMA((count,))]


def vmem_call(kernel, outs, scratch, collective_id, *args, limit=56 << 20):
    return pl.pallas_call(
        kernel,
        out_shape=tuple(jax.ShapeDtypeStruct(shape, kind) for shape, kind in outs),
        in_specs=[pl.BlockSpec(memory_space=VMEM)] * len(args),
        out_specs=tuple(pl.BlockSpec(memory_space=VMEM) for _ in outs),
        scratch_shapes=scratch,
        compiler_params=pltpu.CompilerParams(
            collective_id=collective_id, has_side_effects=True, vmem_limit_bytes=limit
        ),
    )(*args)


WHOLE = (4, 2, 4, 2, 48, 768)


def entry_call(p_in, mv_in, e_in):
    return vmem_call(
        entry_kernel,
        [(WHOLE, BF16), ((4, 24, 768), F32), ((2, 4, 24, 768), F32), ((2, 4, 4, 24, 128), F32)],
        semaphores(3 + 7 + 23 + 3 + 16), 1, p_in, mv_in, e_in,
    )


def renew_call(number, *args):
    return vmem_call(
        functools.partial(renew_kernel, number),
        [(WHOLE, BF16), ((2, 48, 768), F32), ((2, 2, 48, 768), F32), ((24, 768), F32), ((2, 24, 768), F32)],
        [VMEM((2, 48, 768), F32)] + REDUCE_SCRATCH + semaphores(REDUCE_COPIES + GATHER_COPIES), 2, *args,
    )


def final_call(number, *args):
    box = VMEM((4, 24, 768), F32)
    return vmem_call(
        functools.partial(final_kernel, number),
        [((4, 24, 768), F32), ((4, 24, 768), F32), ((24, 768), F32)],
        [VMEM((2, 48, 768), F32), box, box, box, box, box] + REDUCE_SCRATCH + semaphores(REDUCE_COPIES + 12),
        3, *args,
    )


def turned_gather(arrays, axis, dims):
    turned = [jnp.moveaxis(a, dim, 0) for a, dim in zip(arrays, dims)]
    widths = [t[0].size for t in turned]
    both = jnp.concatenate([t.reshape(-1, w) for t, w in zip(turned, widths)], axis=1)
    whole = lax.all_gather(both, axis, axis=0, tiled=True)
    blocks = jnp.split(whole, [sum(widths[:k]) for k in range(1, len(widths))], axis=1)
    return tuple(
        (
            jnp.moveaxis(b.reshape(-1, *t.shape[1:]), 0, dim)
            for b, t, dim in zip(blocks, turned, dims)
        )
    )


def normalize(values):
    return values * lax.rsqrt(jnp.mean(values * values, axis=-1, keepdims=True) + EPS_NORM)


def norm_back(values, grad_norm):
    scale = lax.rsqrt(jnp.mean(values * values, axis=-1, keepdims=True) + EPS_NORM)
    normed = values * scale
    return scale * (grad_norm - normed * jnp.mean(grad_norm * normed, axis=-1, keepdims=True))


def gelu_exact(values):
    return jax.nn.gelu(values, approximate=False)


def route_table(choices, count, capacity):
    flat = choices.reshape(-1)
    onehot = (flat[:, None] == jnp.arange(count, dtype=jnp.int32)[None, :]).astype(jnp.int32)
    before = jnp.cumsum(onehot, axis=0) - onehot
    slot = jnp.sum(before * onehot, axis=1)
    place = flat * capacity + slot
    marks = jnp.arange(flat.shape[0], dtype=jnp.int32) + 1
    table = jnp.zeros((count * capacity,), jnp.int32).at[place].set(marks)
    return (place, table)


def split_heads(qkv, heads):
    tokens_here, triple = qkv.shape
    size = triple // (3 * heads)
    parts = qkv.reshape(tokens_here // LEN, LEN, 3, heads, size)
    return (parts[:, :, 0], parts[:, :, 1], parts[:, :, 2], size ** (-0.5))


def attend(qkv, heads):
    query, key, value, scale = split_heads(qkv, heads)
    scores = jnp.einsum("sqhd,skhd->shqk", query, key, preferred_element_type=jnp.float32) * scale
    causal = jnp.arange(LEN)[:, None] >= jnp.arange(LEN)[None, :]
    scores = jnp.where(causal, scores, -1e30)
    top = jnp.max(scores, axis=-1, keepdims=True)
    expo = jnp.exp(scores - top)
    probs = expo / jnp.sum(expo, axis=-1, keepdims=True)
    probs_low = probs.astype(jnp.bfloat16)
    mixed = jnp.einsum("shqk,skhd->sqhd", probs_low, value, preferred_element_type=jnp.float32)
    return (probs, probs_low, mixed.reshape(qkv.shape[0], -1).astype(jnp.bfloat16))


def attend_back(qkv, probs, probs_low, grad_mixed, heads):
    query, key, value, scale = split_heads(qkv, heads)
    grad_heads = grad_mixed.reshape(query.shape)
    grad_value = jnp.einsum(
        "shqk,sqhd->skhd", probs_low, grad_heads, preferred_element_type=jnp.float32
    )
    grad_probs = jnp.einsum(
        "sqhd,skhd->shqk", grad_heads, value, preferred_element_type=jnp.float32
    )
    grad_scores = probs * (grad_probs - jnp.sum(probs * grad_probs, axis=-1, keepdims=True))
    grad_low = grad_scores.astype(jnp.bfloat16)
    grad_query = (
        jnp.einsum("shqk,skhd->sqhd", grad_low, key, preferred_element_type=jnp.float32) * scale
    )
    grad_key = (
        jnp.einsum("shqk,sqhd->skhd", grad_low, query, preferred_element_type=jnp.float32) * scale
    )
    stacked = jnp.stack([grad_query, grad_key, grad_value], axis=2)
    return stacked.reshape(qkv.shape).astype(jnp.bfloat16)


def expert_forward(rows, first, second):
    pre = jnp.dot(rows, first, preferred_element_type=jnp.float32)
    act = gelu_exact(pre).astype(jnp.bfloat16)
    result = jnp.dot(act, second, preferred_element_type=jnp.float32)
    return (pre, act, result)


def expert_rows_back(first, second, pre, grad_result):
    grad_act = lax.dot_general(grad_result, second, (((1,), (1,)), ((), ())), preferred_element_type=F32)
    unused, gelu_pull = jax.vjp(gelu_exact, pre)
    grad_pre = gelu_pull(grad_act)[0].astype(jnp.bfloat16)
    grad_rows = lax.dot_general(grad_pre, first, (((1,), (1,)), ((), ())), preferred_element_type=F32)
    return grad_pre, grad_rows


def expert_weight_grads(rows, grad_pre, act, grad_result):
    over_rows = (((0,), (0,)), ((), ()))
    grad_second = lax.dot_general(act, grad_result, over_rows, preferred_element_type=F32)
    grad_first = lax.dot_general(rows, grad_pre, over_rows, preferred_element_type=F32)
    return grad_first, grad_second


def adam_step(master, state, grad, rate, number):
    fresh, first, second = adam_values(master, state[0], state[1], grad, rate, number)
    return fresh, (first, second)


def cols_and_square(wide, square):
    return jnp.stack([wide[:, :768], wide[:, 768:1536], wide[:, 1536:], square])


def extra_rows(all_extra, start):
    return jnp.pad(all_extra[:, start : start + 19].T, ((0, 5), (0, 0)))


def body(
    tokens,
    out_grad,
    expert_ids,
    replay,
    frozen_in,
    frozen_out,
    gains,
    w_qkv,
    w_proj,
    router,
    exp_in,
    exp_out,
    mom_gains,
    mom_qkv,
    mom_proj,
    mom_router,
    mom_in,
    mom_out,
    state_gains,
    state_qkv,
    state_proj,
    state_router,
    state_in,
    state_out,
):
    groups = lax.axis_size("group")
    frozen = frozen_in.shape[0]
    count = 17
    width = tokens.shape[2]
    tok = tokens.shape[1]
    capacity = 3 * tok // count
    start_in, start_out = tuple(
        (
            part[0].astype(jnp.float32)
            for part in turned_gather(
                (exp_in.astype(jnp.bfloat16), exp_out.astype(jnp.bfloat16)), "group", (1, 2)
            )
        )
    )
    w_start = cols_and_square(w_qkv, w_proj)
    moments = jnp.stack([cols_and_square(state_qkv[0, k], state_proj[0, k]) for k in range(2)])
    packed = jnp.concatenate(
        [router, gains.T, state_router[0, 0], state_gains[0, 0].T, state_router[0, 1], state_gains[0, 1].T], axis=1
    )
    packed = jnp.pad(packed, ((0, 0), (0, 128 - packed.shape[1])))
    whole, p_start, mv, all_extra = entry_call(w_start, moments, packed)
    p_start, mv = p_start.reshape(2, 48, 768), mv.reshape(2, 2, 48, 768)
    all_extra = all_extra.reshape(768, 128)
    pe_start = extra_rows(all_extra, 0)
    mve = jnp.stack([extra_rows(all_extra, 19), extra_rows(all_extra, 38)])
    p_now, pe_now = p_start, pe_start
    masters = [start_in, start_out]
    expert_moments = [state_in[0, :, 0], state_out[0, :, 0]]
    block_list = []
    grad_list = []
    for step in range(STEPS):
        blocks = whole.reshape(4, 768, 768)
        qkv_b = jnp.concatenate([blocks[0], blocks[1], blocks[2]], axis=1)
        proj_b = blocks[3]
        low_extra = pe_now.astype(BF16)
        router_b = low_extra[:17].T
        gain_f = low_extra[17:19].astype(F32)
        first_b = masters[0].astype(jnp.bfloat16)
        second_b = masters[1].astype(jnp.bfloat16)
        inputs = tokens[step].astype(jnp.float32)
        choices = expert_ids[step]
        factor = jnp.where(replay[step] > 0, REPLAY_WEIGHT, 1.0).astype(jnp.float32)
        cotangent = out_grad[step].astype(jnp.float32) * factor[:, None]
        normed = normalize(inputs)
        acts = (normed * gain_f[0]).astype(jnp.bfloat16)
        qkv = jnp.dot(acts, qkv_b, preferred_element_type=jnp.float32).astype(jnp.bfloat16)
        probs, probs_low, mixed = attend(qkv, HEADS)
        middle = inputs + jnp.dot(mixed, proj_b, preferred_element_type=jnp.float32)
        normed_mid = normalize(middle)
        routed = (normed_mid * gain_f[1]).astype(jnp.bfloat16)
        logits = jnp.dot(routed, router_b, preferred_element_type=jnp.float32)
        select = (choices[:, :, None] == jnp.arange(count, dtype=jnp.int32)[None, None, :]).astype(
            jnp.float32
        )
        picked = jnp.sum(select * logits[:, None, :], axis=-1)
        picked_top = jnp.max(picked, axis=-1, keepdims=True)
        picked_exp = jnp.exp(picked - picked_top)
        weights = picked_exp / jnp.sum(picked_exp, axis=-1, keepdims=True)
        place, table = route_table(choices, count, capacity)
        doubled = jnp.repeat(routed, 2, axis=0)
        grad_choice = (weights[:, :, None] * cotangent[:, None, :]).reshape(2 * tok, width).astype(BF16)
        both = jnp.concatenate([doubled, grad_choice], axis=1)
        padded = jnp.concatenate([jnp.zeros((1, 2 * width), jnp.bfloat16), both])
        rows = padded[table].reshape(count, capacity, 2 * width)
        sent = jnp.concatenate([rows[frozen:], rows[frozen:]])
        arrived = lax.all_to_all(sent, ("dp", "expert"), split_axis=0, concat_axis=0, tiled=True)
        frozen_rows, frozen_grad = rows[0, :, :width], rows[0, :, width:]
        frozen_pre, frozen_act, frozen_res = expert_forward(frozen_rows, frozen_in[0], frozen_out[0])
        unused_pre, frozen_back = expert_rows_back(frozen_in[0], frozen_out[0], frozen_pre, frozen_grad)
        expert_rows = arrived[:, :, :width].reshape(-1, width)
        expert_grad = arrived[:, :, width:].reshape(-1, width)
        pre, act, partial_value = expert_forward(expert_rows, first_b, second_b)
        grad_pre, partial_rows = expert_rows_back(first_b, second_b, pre, expert_grad)
        answer = jnp.concatenate([partial_value.astype(BF16), partial_rows.astype(BF16)], axis=1)
        answer = answer.reshape(32, capacity, 2 * width)
        returned = lax.all_to_all(answer, ("dp", "expert"), split_axis=0, concat_axis=0, tiled=True)
        returned = returned.astype(F32)
        returned = (returned[:16] + returned[16:]).astype(BF16).astype(F32).reshape(-1, 2 * width)
        grads = expert_weight_grads(expert_rows, grad_pre, act, expert_grad)
        outputs = jnp.concatenate([jnp.concatenate([frozen_res, frozen_back], axis=1), returned])
        gathered_both = outputs[place].reshape(tok, 2, 2 * width)
        gathered = gathered_both[:, :, :width]
        block = middle + jnp.sum(weights[:, :, None] * gathered, axis=1)
        block_list.append(block.astype(jnp.bfloat16))
        grad_pick = jnp.sum(cotangent[:, None, :] * gathered, axis=-1)
        grad_logit_pick = weights * (
            grad_pick - jnp.sum(weights * grad_pick, axis=-1, keepdims=True)
        )
        grad_logits = jnp.sum(select * grad_logit_pick[:, :, None], axis=1)
        grad_router = jnp.dot(
            grad_logits.T, routed.astype(jnp.float32), precision=lax.Precision.HIGHEST
        )
        grad_routed = jnp.dot(
            grad_logits, router_b.astype(jnp.float32).T, precision=lax.Precision.HIGHEST
        )
        grad_routed = grad_routed + jnp.sum(gathered_both[:, :, width:], axis=1)
        grad_gain_two = jnp.sum(normed_mid * grad_routed, axis=0)
        grad_middle = cotangent + norm_back(middle, grad_routed * gain_f[1])
        grad_branch = grad_middle.astype(jnp.bfloat16)
        over_rows = (((0,), (0,)), ((), ()))
        grad_proj = lax.dot_general(mixed, grad_branch, over_rows, preferred_element_type=F32)
        grad_mixed = jnp.einsum(
            "te,de->td", grad_branch, proj_b, preferred_element_type=jnp.float32
        ).astype(jnp.bfloat16)
        grad_qkv = attend_back(qkv, probs, probs_low, grad_mixed, HEADS)
        grad_acts = jnp.einsum("te,de->td", grad_qkv, qkv_b, preferred_element_type=jnp.float32)
        grad_gain_one = jnp.sum(normed * grad_acts, axis=0)
        grad_list.append(grad_middle + norm_back(inputs, grad_acts * gain_f[0]))
        dense_grads = jnp.stack(
            [
                lax.dot_general(acts, grad_qkv[:, k * 768 : (k + 1) * 768], over_rows, preferred_element_type=F32)
                for k in range(3)
            ]
            + [grad_proj]
        ).astype(BF16).reshape(WHOLE)
        extra = jnp.concatenate(
            [grad_router, grad_gain_one[None], grad_gain_two[None], jnp.zeros((5, 768), F32)]
        )
        if step == 0:
            whole, p_now, mv, pe_now, mve = renew_call(STEP, dense_grads, extra, p_now, mv, pe_now, mve)
        else:
            w_new, mom_new, delta_e = final_call(
                STEP + 1, dense_grads, extra, p_now, mv, pe_now, mve, p_start, pe_start,
                w_start, cols_and_square(mom_qkv, mom_proj),
            )
        for index in range(2):
            masters[index], expert_moments[index] = adam_step(
                masters[index], expert_moments[index], grads[index], RATES[4 + index], STEP + step
            )
    expert_deltas = (
        lax.psum_scatter(
            (start_in - masters[0]).astype(jnp.bfloat16), "group", scatter_dimension=0, tiled=True
        ).astype(jnp.float32),
        lax.psum_scatter(
            (start_out - masters[1]).astype(jnp.bfloat16), "group", scatter_dimension=1, tiled=True
        ).astype(jnp.float32),
    )
    at = 24 * (16 * lax.axis_index("dp") + lax.axis_index("expert"))
    mine = lax.dynamic_slice(delta_e, (0, at), (24, 24))
    new_params = []
    new_moms = []
    for delta, begin, moment in (
        (mine[17:19], gains, mom_gains),
        (mine[:17].T, router, mom_router),
        (expert_deltas[0][None] / groups, exp_in, mom_in),
        (expert_deltas[1][None] / groups, exp_out, mom_out),
    ):
        renewed = OUTER_MOMENTUM * moment + delta
        new_moms.append(renewed)
        new_params.append(begin - OUTER_RATE * (delta + OUTER_MOMENTUM * renewed))
    wide = lambda stack: jnp.concatenate([stack[0], stack[1], stack[2]], axis=1)
    return (
        jnp.stack(block_list),
        jnp.stack(grad_list),
        new_params[0],
        wide(w_new),
        w_new[3],
        new_params[1],
        new_params[2],
        new_params[3],
        new_moms[0],
        wide(mom_new),
        mom_new[3],
        new_moms[1],
        new_moms[2],
        new_moms[3],
    )


def solution(mesh):
    return jax.shard_map(
        body,
        mesh=mesh,
        in_specs=(
            P(None, ("group", "dp", "expert"), None),
            P(None, ("group", "dp", "expert"), None),
            P(None, ("group", "dp", "expert"), None),
            P(None, ("group", "dp", "expert")),
            P(),
            P(),
            P(None, ("dp", "expert")),
            P(("dp", "expert"), None),
            P(("dp", "expert"), None),
            P(("dp", "expert"), None),
            P("expert", "group", "dp"),
            P("expert", "dp", "group"),
            P(None, ("dp", "expert")),
            P(("dp", "expert"), None),
            P(("dp", "expert"), None),
            P(("dp", "expert"), None),
            P("expert", "group", "dp"),
            P("expert", "dp", "group"),
            P("group", None, None, ("dp", "expert")),
            P("group", None, ("dp", "expert"), None),
            P("group", None, ("dp", "expert"), None),
            P("group", None, ("dp", "expert"), None),
            P("group", None, "expert", None, "dp"),
            P("group", None, "expert", "dp", None),
        ),
        out_specs=(
            P(None, ("group", "dp", "expert"), None),
            P(None, ("group", "dp", "expert"), None),
            P(None, ("dp", "expert")),
            P(("dp", "expert"), None),
            P(("dp", "expert"), None),
            P(("dp", "expert"), None),
            P("expert", "group", "dp"),
            P("expert", "dp", "group"),
            P(None, ("dp", "expert")),
            P(("dp", "expert"), None),
            P(("dp", "expert"), None),
            P(("dp", "expert"), None),
            P("expert", "group", "dp"),
            P("expert", "dp", "group"),
        ),
        check_vma=False,
    )
```

time: 1290 us -> 592 us (0.46)
  waiting for transfers between devices: 682 us -> 24.4 us
  Pallas kernels: 0 us -> 189 us
  local copies, waits for them, and re-layouts: 196 us -> 101 us
  starting transfers between devices: 115 us -> 29.1 us
  matrix products: 215 us -> 156 us
    unnamed x9 -> x3, waiting for transfers between devices: 328 us -> 0.05 us
    all_gather x3 -> x1, waiting for transfers between devices: 270 us -> 0.01 us  [turned_gather(): whole = lax.all_gather(both, axis, axis=0, tiled=True)]
    pallas_call x0 -> x3, Pallas kernels: none -> 189 us  [vmem_call(): pl.pallas_call(kernel, out_shape=tuple((jax.ShapeDtypeStruct(shape, kind)...]
    all_to_all x20 -> x4, starting transfers between devices: 113 us -> 28.6 us  [the longest x2 14.8 us: body(): lax.all_to_all(answer, ('dp', 'expert'), split_axis=0, concat_axis=0, til...]
    all_to_all x20 -> x4, waiting for transfers between devices: 84.3 us -> 24.3 us  [the longest x2 18 us: body(): lax.all_to_all(sent, ('dp', 'expert'), split_axis=0, concat_axis=0, tiled...]
    unnamed x303 -> x240, local copies, waits for them, and re-layouts: 77.6 us -> 24.1 us
    dot_general x24 -> x28, matrix products: 177 us -> 131 us  [the longest x4 32.5 us: expert_forward(): pre = jnp.dot(rows, first, preferred_element_type=jnp.float32)]
    another operation x15 -> x13, local copies, waits for them, and re-layouts: 17.3 us -> 0.32 us  [the longest x6 14.3 us: one_scatter(): lines = jnp.concatenate([b.reshape(count, -1) for b in blocks], axis=1)]
  transfers between devices with their start and end apart: 27 -> 7, of which waited for: 18 -> 2; matrix products, arithmetic and copies ran while one was open for 25% -> 32% of each run, Pallas kernels for 0% -> 20%
where the time goes in v1:
time: 592 us; the launch traced here: 582 us
  Pallas kernels  189 us (32%)
  matrix products  156 us (26%)
  local copies, waits for them, and re-layouts  101 us (17%)
  other arithmetic  66 us (11%)
  starting transfers between devices  29.1 us (5%)
  waiting for transfers between devices  24.4 us (4%)
  between operations  16.2 us (3%)
    pallas_call x3, Pallas kernels, vmem_call(): pl.pallas_call(kernel, out_shape=tuple((jax.ShapeDtypeStruct(shape, kind)...  189 us
    dot_general x4, matrix products, expert_forward(): pre = jnp.dot(rows, first, preferred_element_type=jnp.float32)  32.5 us
    dot_general x2, matrix products, expert_weight_grads(): lax.dot_general(rows, grad_pre, over_rows, preferred_element_type=F32)  28 us
    unnamed x240, local copies, waits for them, and re-layouts  24.1 us
    dot_general x2, matrix products, expert_weight_grads(): lax.dot_general(act, grad_result, over_rows, preferred_element_type=F32)  18.1 us
    all_to_all x2, waiting for transfers between devices, body(): lax.all_to_all(sent, ('dp', 'expert'), split_axis=0, concat_axis=0, tiled...  18 us
    dot_general x4, matrix products, expert_rows_back(): lax.dot_general(grad_pre, first, (((1,), (1,)), ((), ())), preferred_elem...  18 us
    all_to_all x2, starting transfers between devices, body(): lax.all_to_all(answer, ('dp', 'expert'), split_axis=0, concat_axis=0, til...  14.8 us
  transfers between devices with their start and end apart: 7, of which 2 were waited for; matrix products, arithmetic and copies ran while one was open for 32% of the time, Pallas kernels for 20%

profile of v1, /device:TPU:1, one launch (start us, length us, event | category | flops | bytes accessed | tf_op | source)
XLA Modules:
  0.0 581.9 jit_solution(3464947037825559208)
XLA Ops:
  19.1 44.6 %shard_map.335 = (bf16[4,2,4,2,48,768]{5,4,3,2,1,0:T(8,128)(2,1)}, f32[4,24,768]{2,1,0:T(8,128)}, f32[2,4,24,768]{3,2,1,0:T(8,128)}, f32[2,4,4,24,128]{4,3,2,1,0:T(8,128)}) custom-call(f32[4,24,768]{2,1,0:T(8,128)} %get-tuple-element.209.p_in.w_old, f32[2,4,24,768]{3,2,1,0:T(8,128)} %pad_maximum_fusion.16.mv_in, f32[24,128]{1,0:T(8,128)} %pad.16.e_in), custom_call_target="tpu_custom_call" | custom-call | tf_op jit(solution)/shard_map/pallas_call | solution.py:395
  63.8 2.5 fusion.227
  66.5 2.6 fusion.224
  82.9 2.2 gather_fusion
  87.8 1.7 pad_maximum_fusion.4
  89.5 5.0 all-to-all-start
  97.8 8.0 %fusion.222 = (f32[1,1,1,1536,768]{4,3,2,1,0:T(8,128)}, f32[1,1,1,1536,768]{4,3,2,1,0:T(8,128)}) fusion(f32[1,2,1,1536,768]{4,3,2,1,0:T(8,128)} %param.47), kind=kLoop, calls=%fused_computation.465 | loop fusion | bytes 18874368 | tf_op jit(solution)/shard_map/slice | solution.py:539
  105.8 18.0 %all-to-all-done = bf16[32,22,1536]{2,1,0:T(8,128)(2,1)} async-done(((bf16[32,22,1536]{2,1,0:T(8,128)(2,1)}), bf16[32,22,1536]{2,1,0:T(8,128)(2,1)}, u32[]{:S(2)}, u32[]{:S(2)}) %all-to-all-start) | async-done | bytes 2162720 | tf_op jit(solution)/shard_map/all_to_all | solution.py:642
  123.8 2.8 fusion.226
  126.6 2.2 reshape.760
  130.0 12.4 %multiply_convert_fusion.1 = (bf16[704,1536]{1,0:T(8,128)(2,1)S(1)}, f32[704,1536]{1,0:T(8,128)S(1)}, f32[704,1536]{1,0:T(8,128)S(1)}) fusion(bf16[704,768]{1,0:T(8,128)(2,1)} %reshape.757, bf16[768,3072]{1,0:T(8,128)(2,1)} %all-gather.2.cloned.1.call-done), kind=kOutput, calls=%fused_computation.77 | convolution fusion | flops 1731231744 | bytes 14254080 | tf_op jit(solution)/shard_map/dot_general | solution.py:517
  142.5 3.2 add_convert_fusion.1
  145.7 1.9 fusion.64
  147.6 1.9 fusion.67
  151.0 4.1 reshape.761
  155.1 6.8 %all-to-all-start.1 = ((bf16[32,22,1536]{2,1,0:T(8,128)(2,1)}), bf16[32,22,1536]{2,1,0:T(8,128)(2,1)}, u32[]{:S(2)}, u32[]{:S(2)}) async-start(bf16[32,22,1536]{2,1,0:T(8,128)(2,1)} %reshape.761), calls=%async_computation.1 | async-start | bytes 4718592 | tf_op jit(solution)/shard_map/all_to_all | solution.py:652
  166.8 6.2 %copy.277 = f32[1,1,1,1536,768]{3,4,2,1,0:T(8,128)} copy(f32[1,1,1,1536,768]{4,3,2,1,0:T(8,128)} %get-tuple-element.127) | data formatting | bytes 9437184
  173.0 6.1 %copy.276 = f32[1,1,1,1536,768]{3,4,2,1,0:T(8,128)} copy(f32[1,1,1,1536,768]{4,3,2,1,0:T(8,128)} %get-tuple-element.128) | data formatting | bytes 9437184
  180.9 3.1 fusion.36
  184.0 4.2 fusion.28
  188.2 7.1 %fusion.34 = f32[22,768]{1,0:T(8,128)} fusion(bf16[1,768,3072]{2,1,0:T(8,128)(2,1)} %param.28, bf16[1,3072,768]{2,1,0:T(8,128)(2,1)} %param.29, f32[22,3072]{1,0:T(8,128)S(1)} %fusion.36, bf16[17,22,1536]{2,1,0:T(8,128)(2,1)} %reshape.756), kind=kOutput, calls=%fused_computation.56 | convolution fusion | flops 212484096 | bytes 9811968 | tf_op jit(solution)/shard_map/dot_general | solution.py:527
  195.3 2.3 convert_element_type.277
  199.5 1.8 pad_maximum_fusion.6
  201.3 2.6 gather_fusion.1
  204.0 2.5 reshape.764
  206.5 4.0 multiply_reduce_fusion.5
  215.1 1.9 fusion.150
  223.0 1.9 fusion.112
  228.6 2.5 fusion.72
  231.6 2.4 fusion.75
  235.2 2.6 mul.780
  239.3 3.8 pad_maximum_fusion.grads
  243.1 70.3 %shard_map.336 = (bf16[4,2,4,2,48,768]{5,4,3,2,1,0:T(8,128)(2,1)}, f32[2,48,768]{2,1,0:T(8,128)}, f32[2,2,48,768]{3,2,1,0:T(8,128)}, f32[24,768]{1,0:T(8,128)}, f32[2,24,768]{2,1,0:T(8,128)}) custom-call(bf16[4,2,4,2,48,768]{5,4,3,2,1,0:T(8,128)(2,1)} %pad_maximum_fusion.grads, f32[24,768]{1,0:T(8,128)} %maximum_maximum_fusion.extra, ...), custom_call_target="tpu_custom_call" | custom-call | tf_op jit(solution)/shard_map/pallas_call | solution.py:395
  313.5 2.7 fusion.223
  327.3 2.2 gather_fusion.2
  332.2 1.6 pad_maximum_fusion.5
  333.8 8.8 %all-to-all-start.2 = ((bf16[32,22,1536]{2,1,0:T(8,128)(2,1)}), bf16[32,22,1536]{2,1,0:T(8,128)(2,1)}, u32[]{:S(2)}, u32[]{:S(2)}) async-start(bf16[32,22,1536]{2,1,0:T(8,128)(2,1)} %pad_maximum_fusion.5), calls=%async_computation.2 | async-start | bytes 4718592 | tf_op jit(solution)/shard_map/all_to_all | solution.py:642
  343.1 14.1 %fusion.52 = (bf16[768,1536]{1,0:T(8,128)(2,1)}, f32[768,1536]{1,0:T(8,128)}) fusion(bf16[768,3072]{1,0:T(8,128)(2,1)} %all-gather.2.cloned.1.call-done, f32[1,2,1,768,1536]{4,3,2,1,0:T(8,128)} %param.46, bf16[704,768]{1,0:T(8,128)(2,1)} %reshape.757, bf16[704,1536]{1,0:T(8,128)(2,1)} %copy-done.109), kind=kOutput, calls=%fused_computation.107 | convolution fusion | flops 1680998400 | bytes 22118400 | tf_op jit(solution)/shard_map/dot_general | solution.py:534
  357.1 4.2 fusion.235
  362.8 3.1 fusion.32
  365.8 4.2 fusion.24
  370.0 7.1 %fusion.30 = f32[22,768]{1,0:T(8,128)} fusion(bf16[1,768,3072]{2,1,0:T(8,128)(2,1)} %param.28, bf16[1,3072,768]{2,1,0:T(8,128)(2,1)} %param.29, f32[22,3072]{1,0:T(8,128)S(1)} %fusion.32, bf16[17,22,1536]{2,1,0:T(8,128)(2,1)} %reshape.776), kind=kOutput, calls=%fused_computation.52 | convolution fusion | flops 212484096 | bytes 9811968 | tf_op jit(solution)/shard_map/dot_general | solution.py:527
  377.2 1.8 fusion.225
  380.6 13.9 %multiply_convert_fusion = (bf16[704,1536]{1,0:T(8,128)(2,1)S(1)}, f32[704,1536]{1,0:T(8,128)}, f32[704,1536]{1,0:T(8,128)}) fusion(bf16[704,768]{1,0:T(8,128)(2,1)} %reshape.777, bf16[768,1536]{1,0:T(8,128)(2,1)} %get-tuple-element.201), kind=kOutput, calls=%fused_computation.63 | convolution fusion | flops 1731231744 | bytes 14254080 | tf_op jit(solution)/shard_map/dot_general | solution.py:517
  394.5 13.9 %fusion.8 = (bf16[1536,768]{0,1:T(8,128)(2,1)}, bf16[1536,768]{0,1:T(8,128)(2,1)}) fusion(bf16[768,3072]{1,0:T(8,128)(2,1)} %all-gather.2.cloned.1.call-done, f32[1536,768]{0,1:T(8,128)} %fusion.235, f32[1,1,1,1536,768]{3,4,2,1,0:T(8,128)} %copy.276, f32[1,1,1,1536,768]{3,4,2,1,0:T(8,128)} %copy.277, bf16[704,1536]{1,0:T(8,128)(2,1)S(1)} %get-tuple-element.121, ...), kind=kOutput, calls=%fused_computation.26 | convolution fusion | flops 1701052416 | bytes 24477696 | tf_op jit(solution)/shard_map/dot_general | solution.py:533
  408.4 4.3 convolution_convert_fusion.11
  412.8 6.5 %add_convert_fusion = bf16[704,1536]{1,0:T(8,128)(2,1)S(1)} fusion(f32[704,1536]{1,0:T(8,128)} %get-tuple-element.122, f32[704,1536]{1,0:T(8,128)} %get-tuple-element.203, bf16[704,768]{1,0:T(8,128)(2,1)S(1)} %reshape.778, bf16[1536,768]{0,1:T(8,128)(2,1)S(1)} %copy-done.108), kind=kOutput, calls=%fused_computation.62 | convolution fusion | flops 1676083200 | bytes 14254080 | tf_op jit(solution)/shard_map/dot_general | solution.py:524
  419.3 1.9 convolution_convert_fusion.10
  421.4 2.2 reshape.779
  423.6 8.0 %all-to-all-start.3 = ((bf16[32,22,1536]{2,1,0:T(8,128)(2,1)}), bf16[32,22,1536]{2,1,0:T(8,128)(2,1)}, u32[]{:S(2)}, u32[]{:S(2)}) async-start(bf16[32,22,1536]{2,1,0:T(8,128)(2,1)} %reshape.779), calls=%async_computation.3 | async-start | bytes 4718592 | tf_op jit(solution)/shard_map/all_to_all | solution.py:652
  431.6 14.0 %fusion.4 = bf16[768,1536]{1,0:T(8,128)(2,1)} fusion(bf16[768,3072]{1,0:T(8,128)(2,1)} %all-gather.2.cloned.1.call-done, f32[768,1536]{1,0:T(8,128)} %get-tuple-element.202, f32[1,2,1,768,1536]{4,3,2,1,0:T(8,128)} %param.46, bf16[704,768]{1,0:T(8,128)(2,1)S(1)} %copy-done.44, bf16[704,1536]{1,0:T(8,128)(2,1)} %copy-done.110), kind=kOutput, calls=%fused_computation.22 | convolution fusion | flops 1699872768 | bytes 22118400 | tf_op jit(solution)/shard_map/dot_general | solution.py:534
  445.6 6.3 %all-to-all-done.3 = bf16[32,22,1536]{2,1,0:T(8,128)(2,1)} async-done(((bf16[32,22,1536]{2,1,0:T(8,128)(2,1)}), bf16[32,22,1536]{2,1,0:T(8,128)(2,1)}, u32[]{:S(2)}, u32[]{:S(2)}) %all-to-all-start.3) | async-done | bytes 2162720 | tf_op jit(solution)/shard_map/all_to_all | solution.py:652
  452.0 2.3 convert_element_type.311
  456.2 1.8 pad_maximum_fusion.7
  458.0 2.5 gather_fusion.3
  460.5 2.3 reshape.782
  462.8 3.9 multiply_reduce_fusion.1
  469.7 1.9 multiply_reduce_fusion.6
  477.7 2.0 fusion.68
  483.0 2.5 pad_maximum_fusion.1.grads
  485.6 73.9 %shard_map.337 = (f32[4,24,768]{2,1,0:T(8,128)}, f32[4,24,768]{2,1,0:T(8,128)}, f32[24,768]{1,0:T(8,128)}) custom-call(bf16[4,2,4,2,48,768]{5,4,3,2,1,0:T(8,128)(2,1)} %pad_maximum_fusion.1.grads, f32[24,768]{1,0:T(8,128)} %maximum_maximum_fusion.1.extra, f32[2,48,768]{2,1,0:T(8,128)} %get-tuple-element.32.p_in, f32[2,2,48,768]{3,2,1,0:T(8,128)} %get-tuple-element.33.mv_in, ...), custom_call_target="tpu_custom_call" | custom-call | tf_op jit(solution)/shard_map/pallas_call | solution.py:395
  565.2 1.6 slice_bitcast_fusion.49
  568.9 3.2 fusion.87
  572.1 2.8 fusion.89
  (432 shorter events, 98.9 us)
Async XLA Ops:
  7.2 5.2 copy-start.6
  7.2 5.3 copy-start.99
  7.2 5.9 %copy-start.97 = (f32[1,2,2,24]{3,2,1,0:T(2,128)S(1)}, f32[1,2,2,24]{3,2,1,0:T(2,128)}, u32[]{:S(2)}) copy-start(f32[1,2,2,24]{3,2,1,0:T(2,128)} %param.42) | copy-start | bytes 1156
  7.2 6.0 %copy-start.91 = (f32[2,24]{1,0:T(2,128)S(1)}, f32[2,24]{1,0:T(2,128)}, u32[]{:S(2)}) copy-start(f32[2,24]{1,0:T(2,128)} %param.30) | copy-start | bytes 580
  7.2 6.1 %copy-start.71 = (f32[1,2,24,17]{2,1,3,0:T(2,128)S(1)}, f32[1,2,24,17]{2,1,3,0:T(2,128)}, u32[]{:S(2)}) copy-start(f32[1,2,24,17]{2,1,3,0:T(2,128)} %param.45) | copy-start | bytes 9796
  7.2 7.5 %copy-start.59 = (f32[1,2,24,768]{3,2,1,0:T(8,128)S(1)}, f32[1,2,24,768]{3,2,1,0:T(8,128)}, u32[]{:S(2)}) copy-start(f32[1,2,24,768]{3,2,1,0:T(8,128)} %param.44) | copy-start | bytes 442372
  7.3 7.5 %copy-start.57 = (f32[24,2304]{1,0:T(8,128)S(1)}, f32[24,2304]{1,0:T(8,128)}, u32[]{:S(2)}) copy-start(f32[24,2304]{1,0:T(8,128)} %param.31) | copy-start | bytes 663556
  7.3 7.6 %copy-start.58 = (f32[24,2304]{1,0:T(8,128)S(1)}, f32[24,2304]{1,0:T(8,128)}, u32[]{:S(2)}) copy-start(f32[24,2304]{1,0:T(8,128)} %param.37) | copy-start | bytes 663556
  7.3 7.6 %copy-start.53 = (f32[1,2,24,2304]{3,2,1,0:T(8,128)S(1)}, f32[1,2,24,2304]{3,2,1,0:T(8,128)}, u32[]{:S(2)}) copy-start(f32[1,2,24,2304]{3,2,1,0:T(8,128)} %param.43) | copy-start | bytes 1327108
  7.3 122.7 %all-gather.2.cloned.1.call-start = ((), (), s32[]{:S(2)}) async-start(), calls=%async_computation.6 | async-start | bytes 5898240 | tf_op jit(solution)/shard_map/all_gather | solution.py:440
  8.8 6.2 %copy-start.28 = (bf16[2,128,768]{2,1,0:T(8,128)(2,1)S(1)}, bf16[2,128,768]{2,1,0:T(8,128)(2,1)}, u32[]{:S(2)}) copy-start(bf16[2,128,768]{2,1,0:T(8,128)(2,1)} %param.25) | copy-start | bytes 1179652
  11.4 5.3 copy-start.64
  12.0 66.1 %copy-start.81 = (s32[128,2]{0,1:T(2,128)}, s32[128,2]{0,1:T(2,128)S(1)}, u32[]{:S(2)}) copy-start(s32[128,2]{0,1:T(2,128)S(1)} %get-tuple-element.179) | copy-start | bytes 3076
  13.1 5.2 copy-start.89
  66.4 11.6 %copy-start.18 = (f32[768,19]{0,1:T(8,128)}, f32[768,19]{0,1:T(8,128)S(1)}, u32[]{:S(2)}) copy-start(f32[768,19]{0,1:T(8,128)S(1)} %copy.270) | copy-start | bytes 175108
  66.4 10.7 %copy-start.62 = (f32[768]{0:T(1024)}, f32[768]{0:T(1024)S(1)}, u32[]{:S(2)}) copy-start(f32[768]{0:T(1024)S(1)} %get-tuple-element.111) | copy-start | bytes 9220
  73.8 6.3 %copy-start.21 = (bf16[128,2304]{0,1:T(8,128)(2,1)}, bf16[128,2304]{0,1:T(8,128)(2,1)S(1)}, u32[]{:S(2)}) copy-start(bf16[128,2304]{0,1:T(8,128)(2,1)S(1)} %copy.200) | copy-start | bytes 1769476
  73.9 6.2 %copy-start.75 = (pred[128,128]{0,1:T(8,128)(4,1)}, pred[128,128]{0,1:T(8,128)(4,1)S(1)}, u32[]{:S(2)}) copy-start(pred[128,128]{0,1:T(8,128)(4,1)S(1)} %iota_compare_fusion.1) | copy-start | bytes 49156
  75.2 7.7 %copy-start.82 = (f32[12,128]{1,0:T(8,128)}, f32[12,128]{1,0:T(8,128)S(1)}, u32[]{:S(2)}) copy-start(f32[12,128]{1,0:T(8,128)S(1)} %get-tuple-element.188) | copy-start | bytes 18436
  78.2 7.0 %copy-start.77 = (f32[128]{0:T(128)}, f32[128]{0:T(128)S(1)}, u32[]{:S(2)}) copy-start(f32[128]{0:T(128)S(1)} %reduce_max.37) | copy-start | bytes 1540
  89.5 34.3 %all-to-all-start = ((bf16[32,22,1536]{2,1,0:T(8,128)(2,1)}), bf16[32,22,1536]{2,1,0:T(8,128)(2,1)}, u32[]{:S(2)}, u32[]{:S(2)}) async-start(bf16[32,22,1536]{2,1,0:T(8,128)(2,1)} %pad_maximum_fusion.4), calls=%async_computation | async-start | bytes 4718592 | tf_op jit(solution)/shard_map/all_to_all | solution.py:642
  130.0 12.5 %copy-start.42 = (bf16[704,768]{1,0:T(8,128)(2,1)S(1)}, bf16[704,768]{1,0:T(8,128)(2,1)}, u32[]{:S(2)}) copy-start(bf16[704,768]{1,0:T(8,128)(2,1)} %reshape.760) | copy-start | bytes 3244036
  130.0 12.5 %copy-start.103 = (bf16[768,3072]{1,0:T(8,128)(2,1)S(1)}, bf16[768,3072]{1,0:T(8,128)(2,1)}, u32[]{:S(2)}) copy-start(bf16[768,3072]{1,0:T(8,128)(2,1)} %all-gather.2.cloned.1.call-done) | copy-start | bytes 14155780
  142.5 5.1 copy-start.105
  151.0 12.2 %copy-start.19 = (f32[768,19]{0,1:T(8,128)S(1)}, f32[768,19]{0,1:T(8,128)}, u32[]{:S(2)}) copy-start(f32[768,19]{0,1:T(8,128)} %copy-done.18) | copy-start | bytes 175108
  155.1 10.7 %copy-start.78 = (f32[24,17]{1,0:T(8,128)S(1)}, f32[24,17]{1,0:T(8,128)}, u32[]{:S(2)}) copy-start(f32[24,17]{1,0:T(8,128)} %param.39) | copy-start | bytes 4900
  155.1 11.4 %copy-start.26 = (f32[768,19]{1,0:T(8,128)S(1)}, f32[768,19]{1,0:T(8,128)}, u32[]{:S(2)}) copy-start(f32[768,19]{1,0:T(8,128)} %get-tuple-element.151) | copy-start | bytes 175108
  155.1 11.6 %copy-start.25 = (f32[768,19]{1,0:T(8,128)S(1)}, f32[768,19]{1,0:T(8,128)}, u32[]{:S(2)}) copy-start(f32[768,19]{1,0:T(8,128)} %get-tuple-element.153) | copy-start | bytes 175108
  155.1 40.2 %all-to-all-start.1 = ((bf16[32,22,1536]{2,1,0:T(8,128)(2,1)}), bf16[32,22,1536]{2,1,0:T(8,128)(2,1)}, u32[]{:S(2)}, u32[]{:S(2)}) async-start(bf16[32,22,1536]{2,1,0:T(8,128)(2,1)} %reshape.761), calls=%async_computation.1 | async-start | bytes 4718592 | tf_op jit(solution)/shard_map/all_to_all | solution.py:652
  201.3 5.1 copy-start.51
  204.0 6.6 %copy-start.70 = (f32[128,2]{0,1:T(2,128)S(1)}, f32[128,2]{0,1:T(2,128)}, u32[]{:S(2)}) copy-start(f32[128,2]{0,1:T(2,128)} %copy-done.69) | copy-start | bytes 3076
  204.0 8.7 %copy-start.14 = (bf16[128,768]{1,0:T(8,128)(2,1)S(1)}, bf16[128,768]{1,0:T(8,128)(2,1)}, u32[]{:S(2)}) copy-start(bf16[128,768]{1,0:T(8,128)(2,1)} %copy-done.13) | copy-start | bytes 589828
  204.0 9.5 %copy-start.1 = (f32[128,768]{1,0:T(8,128)S(1)}, f32[128,768]{1,0:T(8,128)}, u32[]{:S(2)}) copy-start(f32[128,768]{1,0:T(8,128)} %copy-done) | copy-start | bytes 1179652
  204.0 9.5 %copy-start.20 = (f32[768,19]{0,1:T(8,128)S(1)}, f32[768,19]{0,1:T(8,128)}, u32[]{:S(2)}) copy-start(f32[768,19]{0,1:T(8,128)} %copy-done.18) | copy-start | bytes 175108
  204.0 9.5 %copy-start.63 = (f32[768]{0:T(1024)S(1)}, f32[768]{0:T(1024)}, u32[]{:S(2)}) copy-start(f32[768]{0:T(1024)} %copy-done.62) | copy-start | bytes 9220
  210.5 7.2 %copy-start.83 = (f32[12,128]{1,0:T(8,128)S(1)}, f32[12,128]{1,0:T(8,128)}, u32[]{:S(2)}) copy-start(f32[12,128]{1,0:T(8,128)} %copy-done.82) | copy-start | bytes 18436
  213.5 5.7 copy-start.22
  217.0 17.0 %copy-start.10 = (f32[128,768]{1,0:T(8,128)}, f32[128,768]{1,0:T(8,128)S(1)}, u32[]{:S(2)}) copy-start(f32[128,768]{1,0:T(8,128)S(1)} %get-tuple-element.150) | copy-start | bytes 1179652
  225.9 5.2 copy-start.104
  226.6 11.1 %copy-start.93 = (f32[24]{0:T(128)S(1)}, f32[24]{0:T(128)}, u32[]{:S(2)}) copy-start(f32[24]{0:T(128)} %pad.62.clone) | copy-start | bytes 292
  316.2 8.7 %copy-start.54 = (bf16[24,768]{1,0:T(8,128)(2,1)}, bf16[24,768]{1,0:T(8,128)(2,1)S(1)}, u32[]{:S(2)}) copy-start(bf16[24,768]{1,0:T(8,128)(2,1)S(1)} %convert_element_type.286) | copy-start | bytes 110596
  319.5 5.6 copy-start.80
  320.9 6.1 %copy-start.12 = (f32[256,768]{1,0:T(8,128)S(1)}, f32[256,768]{1,0:T(8,128)}, u32[]{:S(2)}) copy-start(f32[256,768]{1,0:T(8,128)} %mul.780) | copy-start | bytes 2359300
  322.2 5.1 copy-start.79
  333.8 43.4 %all-to-all-start.2 = ((bf16[32,22,1536]{2,1,0:T(8,128)(2,1)}), bf16[32,22,1536]{2,1,0:T(8,128)(2,1)}, u32[]{:S(2)}, u32[]{:S(2)}) async-start(bf16[32,22,1536]{2,1,0:T(8,128)(2,1)} %pad_maximum_fusion.5), calls=%async_computation.2 | async-start | bytes 4718592 | tf_op jit(solution)/shard_map/all_to_all | solution.py:642
  342.6 14.5 %copy-start.43 = (bf16[704,768]{1,0:T(8,128)(2,1)S(1)}, bf16[704,768]{1,0:T(8,128)(2,1)}, u32[]{:S(2)}) copy-start(bf16[704,768]{1,0:T(8,128)(2,1)} %reshape.760) | copy-start | bytes 3244036
  342.6 226.3 %reduce-scatter.5.cloned.1.call-start = ((), (), s32[]{:S(2)}) async-start(), calls=%async_computation.8 | async-start | bytes 2949120 | tf_op jit(solution)/shard_map/reduce_scatter | solution.py:710
  343.1 14.1 %copy-start.106 = (bf16[704,1536]{1,0:T(8,128)(2,1)S(1)}, bf16[704,1536]{1,0:T(8,128)(2,1)}, u32[]{:S(2)}) copy-start(bf16[704,1536]{1,0:T(8,128)(2,1)} %copy-done.105) | copy-start | bytes 6488068
  394.5 13.9 %copy-start.111 = (bf16[704,1536]{1,0:T(8,128)(2,1)}, bf16[704,1536]{1,0:T(8,128)(2,1)S(1)}, u32[]{:S(2)}) copy-start(bf16[704,1536]{1,0:T(8,128)(2,1)S(1)} %get-tuple-element.121) | copy-start | bytes 6488068
  412.8 6.6 %copy-start.107 = (bf16[768,1536]{1,0:T(8,128)(2,1)S(1)}, bf16[768,1536]{1,0:T(8,128)(2,1)}, u32[]{:S(2)}) copy-start(bf16[768,1536]{1,0:T(8,128)(2,1)} %get-tuple-element.201) | copy-start | bytes 7077892
  423.6 8.0 %copy-start.44 = (bf16[704,768]{1,0:T(8,128)(2,1)S(1)}, bf16[704,768]{1,0:T(8,128)(2,1)}, u32[]{:S(2)}) copy-start(bf16[704,768]{1,0:T(8,128)(2,1)} %reshape.777) | copy-start | bytes 3244036
  423.6 28.4 %all-to-all-start.3 = ((bf16[32,22,1536]{2,1,0:T(8,128)(2,1)}), bf16[32,22,1536]{2,1,0:T(8,128)(2,1)}, u32[]{:S(2)}, u32[]{:S(2)}) async-start(bf16[32,22,1536]{2,1,0:T(8,128)(2,1)} %reshape.779), calls=%async_computation.3 | async-start | bytes 4718592 | tf_op jit(solution)/shard_map/all_to_all | solution.py:652
  431.6 140.6 %reduce-scatter.3.cloned.1.call-start = ((), (), s32[]{:S(2)}) async-start(), calls=%async_computation.7 | async-start | bytes 2949120 | tf_op jit(solution)/shard_map/reduce_scatter | solution.py:707
  460.5 9.1 %copy-start.3 = (f32[128,768]{1,0:T(8,128)S(1)}, f32[128,768]{1,0:T(8,128)}, u32[]{:S(2)}) copy-start(f32[128,768]{1,0:T(8,128)} %copy-done.2) | copy-start | bytes 1179652
  466.7 8.4 %copy-start.24 = (bf16[128,2304]{0,1:T(8,128)(2,1)S(1)}, bf16[128,2304]{0,1:T(8,128)(2,1)}, u32[]{:S(2)}) copy-start(bf16[128,2304]{0,1:T(8,128)(2,1)} %copy-done.23) | copy-start | bytes 1769476
  485.5 74.0 %copy-start.65 = (f32[24,17]{0,1:T(8,128)S(1)}, f32[24,17]{0,1:T(8,128)}, u32[]{:S(2)}) copy-start(f32[24,17]{0,1:T(8,128)} %copy.244) | copy-start | bytes 4900
  485.5 74.0 %copy-start.66 = (f32[24,17]{0,1:T(8,128)S(1)}, f32[24,17]{0,1:T(8,128)}, u32[]{:S(2)}) copy-start(f32[24,17]{0,1:T(8,128)} %copy.243) | copy-start | bytes 4900
  485.5 76.3 %copy-start.48 = (bf16[1,128,768]{2,1,0:T(8,128)(2,1)S(1)}, bf16[1,128,768]{2,1,0:T(8,128)(2,1)}, u32[]{:S(2)}) copy-start(bf16[1,128,768]{2,1,0:T(8,128)(2,1)} %get-tuple-element.148) | copy-start | bytes 589828
  485.5 77.2 %copy-start.27 = (f32[1,128,768]{2,1,0:T(8,128)S(1)}, f32[1,128,768]{2,1,0:T(8,128)}, u32[]{:S(2)}) copy-start(f32[1,128,768]{2,1,0:T(8,128)} %get-tuple-element.144) | copy-start | bytes 1179652
  485.5 78.2 %copy-start.92 = (f32[2,24]{1,0:T(2,128)S(1)}, f32[2,24]{1,0:T(2,128)}, u32[]{:S(2)}) copy-start(f32[2,24]{1,0:T(2,128)} %param.30) | copy-start | bytes 580
  485.6 78.2 %copy-start.100 = (f32[2,24]{1,0:T(2,128)S(1)}, f32[2,24]{1,0:T(2,128)}, u32[]{:S(2)}) copy-start(f32[2,24]{1,0:T(2,128)} %param.36) | copy-start | bytes 580
  559.5 9.4 %copy-start.4 = (f32[1,1536,192]{1,2,0:T(8,128)S(1)}, f32[1,1536,192]{1,2,0:T(8,128)}, u32[]{:S(2)}) copy-start(f32[1,1536,192]{1,2,0:T(8,128)} %param.35) | copy-start | bytes 3538948
  562.8 9.3 %copy-start.5 = (f32[1,192,1536]{2,1,0:T(8,128)S(1)}, f32[1,192,1536]{2,1,0:T(8,128)}, u32[]{:S(2)}) copy-start(f32[1,192,1536]{2,1,0:T(8,128)} %param.34) | copy-start | bytes 3538948
  563.7 8.4 %copy-start.41 = (f32[1,192,1536]{2,1,0:T(8,128)S(1)}, f32[1,192,1536]{2,1,0:T(8,128)}, u32[]{:S(2)}) copy-start(f32[1,192,1536]{2,1,0:T(8,128)} %param.40) | copy-start | bytes 3538948
  (55 other events, 133.8 us)
Sparse Core Ops, SparseCore 0:
  11.5 46.9 all-gather.1
  408.5 67.7 reduce-scatter.4
  479.1 38.1 reduce-scatter.2

commit v2 on v1

--- a/solution.py
+++ b/solution.py
@@ -432,6 +432,348 @@
         3, *args,
     )
 
+CAP = 24
+TOK = 128
+DIMS = {"nn": (((1,), (0,)), ((), ())), "nt": (((1,), (1,)), ((), ())), "tn": (((0,), (0,)), ((), ()))}
+
+
+def mm(a, b, form="nn"):
+    return lax.dot_general(a, b, DIMS[form], preferred_element_type=F32)
+
+
+def split_low(values):
+    high = values.astype(BF16)
+    return high, (values - high.astype(F32)).astype(BF16)
+
+
+def row_scale(values):
+    return lax.rsqrt(jnp.mean(values * values, axis=-1, keepdims=True) + EPS_NORM)
+
+
+def iota(shape, dim):
+    return lax.broadcasted_iota(jnp.int32, shape, dim)
+
+
+def routing(ids):
+    names = [(iota((24, TOK), 0) == ids[k : k + 1]).astype(F32) for k in range(2)]
+    either = names[0] + names[1]
+    earlier = (iota((TOK, TOK), 0) < iota((TOK, TOK), 1)).astype(BF16)
+    slot = mm(either.astype(BF16), earlier).astype(jnp.int32)
+    taken = jnp.where(iota((17, CAP, TOK), 1) == slot[:17][:, None, :], 1.0, 0.0)
+    return names, taken * either[:17][:, None, :]
+
+
+def pair_stack(part):
+    lane = iota(part.shape, 1)
+    zero = jnp.zeros_like(part)
+    return jnp.concatenate([jnp.where(lane < 64, part, zero), jnp.where(lane < 64, zero, part)], axis=0)
+
+
+def side_by_side(stacked):
+    return jnp.concatenate([stacked[:TOK], stacked[TOK:]], axis=1)
+
+
+def front_kernel(x_ref, og_ref, factor_ref, ids_ref, whole, pe_ref,
+                 send, frozen, qkv_out, probs_out, mixed_out, middle_out, a1_out, a2_out, weights_out):
+    gain = pe_ref[16:24].astype(BF16).astype(F32)
+    x = x_ref[...].astype(F32)
+    a1 = (x * row_scale(x) * gain[1:2]).astype(BF16)
+    a1_out[...] = a1
+    for c in range(3):
+        qkv_out[c] = mm(a1, whole[c]).astype(BF16)
+    row, col = iota((2 * TOK, TOK), 0), iota((2 * TOK, TOK), 1)
+    causal = lax.rem(row, TOK) >= col
+    for pair in range(6):
+        lanes = slice(128 * pair, 128 * pair + 128)
+        scores = mm(pair_stack(qkv_out[0, :, lanes]), qkv_out[1, :, lanes], "nt") * 0.125
+        scores = jnp.where(causal, scores, -1e30)
+        expo = jnp.exp(scores - jnp.max(scores, axis=-1, keepdims=True))
+        probs = expo / jnp.sum(expo, axis=-1, keepdims=True)
+        probs_out[pair] = probs
+        mixed_out[:, lanes] = mm(side_by_side(probs.astype(BF16)), pair_stack(qkv_out[2, :, lanes])).astype(BF16)
+    middle = x + mm(mixed_out[...], whole[3])
+    middle_out[...] = middle
+    a2 = (middle * row_scale(middle) * gain[2:3]).astype(BF16)
+    a2_out[...] = a2
+    logits = mm(pe_ref[...].astype(BF16), a2, "nt")
+    names, taken = routing(ids_ref[...])
+    picked = [jnp.sum(name * logits, axis=0, keepdims=True) for name in names]
+    top = jnp.maximum(picked[0], picked[1])
+    expo = [jnp.exp(z - top) for z in picked]
+    whole_sum = expo[0] + expo[1]
+    weights = [e / whole_sum for e in expo]
+    weights_out[...] = jnp.zeros((8, TOK), F32)
+    for k in range(2):
+        weights_out[k : k + 1] = weights[k]
+    by_expert = names[0] * weights[0] + names[1] * weights[1]
+    row_weight = jnp.sum(taken * by_expert[:17][:, None, :], axis=-1, keepdims=True)
+    cot = (og_ref[...].astype(F32) * factor_ref[...]).astype(BF16)
+    low = taken.astype(BF16).reshape(17 * CAP, TOK)
+    rows = mm(low, a2).reshape(17, CAP, 768)
+    grads = mm(low, cot).reshape(17, CAP, 768) * row_weight
+    both = jnp.concatenate([rows, grads], axis=1).astype(BF16)
+    frozen[...] = both[0]
+    send[...] = both[1:]
+
+
+def back_kernel(x_ref, og_ref, factor_ref, ids_ref, whole, pe_ref, qkv, probs_ref, mixed, middle_ref, a1, a2,
+                weights_ref, ret, frozen, block_out, grad_out, grads, extra):
+    gain = pe_ref[16:24].astype(BF16).astype(F32)
+    low_rows = pe_ref[...].astype(BF16)
+    cot = og_ref[...].astype(F32) * factor_ref[...]
+    names, taken = routing(ids_ref[...])
+    weights = [weights_ref[k : k + 1] for k in range(2)]
+    by_expert = names[0] * weights[0] + names[1] * weights[1]
+    row_weight = jnp.sum(taken * by_expert[:17][:, None, :], axis=-1, keepdims=True)
+    low = taken.astype(BF16).reshape(17 * CAP, TOK)
+    both = (ret[:16].astype(F32) + ret[16:].astype(F32)).astype(BF16).astype(F32)
+    both = jnp.concatenate([frozen[...][None], both], axis=0)
+    results, back = both[:, :CAP], both[:, CAP:].reshape(17 * CAP, 768)
+    high, rest = split_low((results * row_weight).reshape(17 * CAP, 768))
+    middle = middle_ref[...]
+    block_out[...] = (middle + mm(low, high, "tn") + mm(low, rest, "tn")).astype(BF16)
+    cot_rows = mm(low, cot.astype(BF16)).reshape(17, CAP, 768)
+    grad_row = jnp.sum(cot_rows * results, axis=-1, keepdims=True)
+    by_name = jnp.concatenate([jnp.sum(taken * grad_row, axis=1), jnp.zeros((7, TOK), F32)], axis=0)
+    grad_w = [jnp.sum(name * by_name, axis=0, keepdims=True) for name in names]
+    mean = weights[0] * grad_w[0] + weights[1] * grad_w[1]
+    grad_logits = sum(names[k] * (weights[k] * (grad_w[k] - mean)) for k in range(2))
+    high, rest = split_low(grad_logits)
+    extra[0:16] = (mm(high, a2[...]) + mm(rest, a2[...]))[0:16]
+    last_router = (mm(high, a2[...]) + mm(rest, a2[...]))[16:17]
+    da2 = mm(high, low_rows, "tn") + mm(rest, low_rows, "tn")
+    high, rest = split_low(back)
+    da2 = da2 + mm(low, high, "tn") + mm(low, rest, "tn")
+    scale = row_scale(middle)
+    normed = middle * scale
+    dg2 = jnp.sum(normed * da2, axis=0, keepdims=True)
+    into = da2 * gain[2:3]
+    dmiddle = cot + scale * (into - normed * jnp.mean(into * normed, axis=-1, keepdims=True))
+    branch = dmiddle.astype(BF16)
+    grads[3] = mm(mixed[...], branch, "tn").astype(BF16)
+    dmixed = mm(branch, whole[3], "nt").astype(BF16)
+    da1 = jnp.zeros((TOK, 768), F32)
+    parts = [[], [], []]
+    for pair in range(6):
+        lanes = slice(128 * pair, 128 * pair + 128)
+        probs = probs_ref[pair]
+        dms = pair_stack(dmixed[:, lanes])
+        parts[2].append(mm(probs.astype(BF16), dms, "tn").astype(BF16))
+        dpb = mm(dms, qkv[2, :, lanes], "nt")
+        ds = (probs * (dpb - jnp.sum(probs * dpb, axis=-1, keepdims=True))).astype(BF16)
+        parts[0].append((mm(side_by_side(ds), pair_stack(qkv[1, :, lanes])) * 0.125).astype(BF16))
+        parts[1].append((mm(ds, pair_stack(qkv[0, :, lanes]), "tn") * 0.125).astype(BF16))
+    for c in range(3):
+        dqkv = jnp.concatenate(parts[c], axis=1)
+        grads[c] = mm(a1[...], dqkv, "tn").astype(BF16)
+        da1 = da1 + mm(dqkv, whole[c], "nt")
+    x = x_ref[...].astype(F32)
+    scale = row_scale(x)
+    normed = x * scale
+    dg1 = jnp.sum(normed * da1, axis=0, keepdims=True)
+    into = da1 * gain[1:2]
+    grad_out[...] = dmiddle + scale * (into - normed * jnp.mean(into * normed, axis=-1, keepdims=True))
+    extra[16:24] = jnp.concatenate([last_router, dg1, dg2, jnp.zeros((5, 768), F32)], axis=0)
+
+
+SQRT_HALF = 0.7071067811865476
+DENSITY = 0.3989422804014327
+
+
+def expert_rows(rows, grad, first, second):
+    u = mm(rows, first)
+    chance = 0.5 + 0.5 * lax.erf(u * SQRT_HALF)
+    h = (u * chance).astype(BF16)
+    value = mm(h, second)
+    slope = chance + u * (jnp.exp(u * u * -0.5) * DENSITY)
+    du = (slope * mm(grad, second, "nt")).astype(BF16)
+    return value, mm(du, first, "nt"), h, du
+
+
+def trade_kernel(send, frozen_in, w1_hbm, w2_hbm, fin_hbm, fout_hbm,
+                 ret, frozen_out, rows_out, grad_out, h_out, du_out,
+                 recv, ans, w1, w2, fin, fout, loads, sends, recvs, sends2, recvs2):
+    copies = [
+        pltpu.make_async_copy(src, dst, loads.at[k])
+        for k, (src, dst) in enumerate(((fin_hbm, fin), (fout_hbm, fout), (w1_hbm, w1), (w2_hbm, w2)))
+    ]
+    for copy in copies:
+        copy.start()
+    d, e = lax.axis_index("dp"), lax.axis_index("expert")
+    me = d * 16 + e
+
+    def device(k, sign):
+        dd, ee = lax.rem(k, 2), lax.div(k, 2)
+        return lax.rem(d + dd, 2), lax.rem(e + sign * ee + 16, 16)
+
+    barrier = pltpu.get_barrier_semaphore()
+
+    @pl.loop(1, 32)
+    def _(k):
+        dp, ex = device(k, 1)
+        pl.semaphore_signal(barrier, inc=1, device_id={"dp": dp, "expert": ex}, device_id_type=MESH)
+
+    pl.semaphore_wait(barrier, 31)
+
+    def out_copy(k):
+        dp, ex = device(k, 1)
+        return pltpu.make_async_remote_copy(
+            src_ref=send.at[ex], dst_ref=recv.at[me], send_sem=sends.at[k], recv_sem=recvs.at[k],
+            device_id={"dp": dp, "expert": ex}, device_id_type=MESH,
+        )
+
+    def back_copy(k):
+        dp, ex = device(k, -1)
+        return pltpu.make_async_remote_copy(
+            src_ref=ans.at[dp * 16 + ex], dst_ref=ret.at[me], send_sem=sends2.at[k], recv_sem=recvs2.at[k],
+            device_id={"dp": dp, "expert": ex}, device_id_type=MESH,
+        )
+
+    @pl.loop(1, 32)
+    def _(k):
+        out_copy(k).start()
+
+    recv[me] = send[e]
+    copies[0].wait()
+    copies[1].wait()
+    both = frozen_in[...].astype(F32)
+    value, back, _, _ = expert_rows(both[:CAP].astype(BF16), both[CAP:].astype(BF16), fin[...], fout[...])
+    frozen_out[...] = jnp.concatenate([value, back], axis=0)
+    copies[2].wait()
+    copies[3].wait()
+
+    @pl.loop(0, 4)
+    def _(j):
+        @pl.loop(0, 8)
+        def _(i):
+            k = j * 8 + i
+
+            @pl.when(k > 0)
+            def _():
+                out_copy(k).wait_recv()
+
+        blocks = []
+        for i in range(8):
+            dp, ex = device(j * 8 + i, -1)
+            blocks.append(recv[dp * 16 + ex].astype(F32))
+        rows = jnp.concatenate([b[:CAP] for b in blocks], axis=0).astype(BF16)
+        grad = jnp.concatenate([b[CAP:] for b in blocks], axis=0).astype(BF16)
+        value, back, h, du = expert_rows(rows, grad, w1[...], w2[...])
+        at = pl.ds(pl.multiple_of(j * 192, 192), 192)
+        rows_out[at] = rows
+        grad_out[at] = grad
+        h_out[at] = h
+        du_out[at] = du
+        for i in range(8):
+            dp, ex = device(j * 8 + i, -1)
+            part = slice(i * CAP, (i + 1) * CAP)
+            ans[dp * 16 + ex] = jnp.concatenate([value[part], back[part]], axis=0).astype(BF16)
+
+        @pl.loop(0, 8)
+        def _(i):
+            k = j * 8 + i
+
+            @pl.when(k > 0)
+            def _():
+                back_copy(k).start()
+
+    ret[me] = ans[me]
+
+    @pl.loop(1, 32)
+    def _(k):
+        back_copy(k).wait_recv()
+        back_copy(k).wait_send()
+        out_copy(k).wait_send()
+
+
+def plain_call(kernel, outs, *args, scratch=(), limit=48 << 20, spaces=None):
+    spaces = spaces or [VMEM] * len(args)
+    return pl.pallas_call(
+        kernel,
+        out_shape=tuple(jax.ShapeDtypeStruct(shape, kind) for shape, kind in outs),
+        in_specs=[pl.BlockSpec(memory_space=space) for space in spaces],
+        out_specs=tuple(pl.BlockSpec(memory_space=VMEM) for _ in outs),
+        scratch_shapes=list(scratch),
+        compiler_params=pltpu.CompilerParams(vmem_limit_bytes=limit),
+    )(*args)
+
+
+def front_call(*args):
+    row = (TOK, 768)
+    return plain_call(
+        front_kernel,
+        [((16, 48, 768), BF16), ((48, 768), BF16), ((3, *row), BF16), ((6, 256, 128), F32), (row, BF16), (row, F32),
+         (row, BF16), (row, BF16), ((8, TOK), F32)],
+        *args,
+    )
+
+
+def back_call(*args):
+    row = (TOK, 768)
+    return plain_call(
+        back_kernel, [(row, BF16), (row, F32), ((4, 768, 768), BF16), ((24, 768), F32)], *args
+    )
+
+
+def trade_call(collective_id, *args):
+    wide, tall = (768, 1536), (1536, 768)
+    return pl.pallas_call(
+        trade_kernel,
+        out_shape=tuple(
+            jax.ShapeDtypeStruct(shape, kind)
+            for shape, kind in (
+                ((32, 48, 768), BF16), ((48, 768), F32), ((768, 768), BF16), ((768, 768), BF16), (wide, BF16), (wide, BF16)
+            )
+        ),
+        in_specs=[pl.BlockSpec(memory_space=VMEM)] * 2 + [pl.BlockSpec(memory_space=pl.ANY)] * 4,
+        out_specs=tuple(pl.BlockSpec(memory_space=VMEM) for _ in range(6)),
+        scratch_shapes=[
+            VMEM((32, 48, 768), BF16), VMEM((32, 48, 768), BF16), VMEM(wide, BF16), VMEM(tall, BF16),
+            VMEM((768, 3072), BF16), VMEM((3072, 768), BF16), pltpu.SemaphoreType.DMA((4,)),
+        ] + semaphores(32) + semaphores(32),
+        compiler_params=pltpu.CompilerParams(
+            collective_id=collective_id, has_side_effects=True, vmem_limit_bytes=56 << 20
+        ),
+    )(*args)
+
+
+def grow_kernel(number, rate, first_step, lhs, rhs, w_ref, mv_ref, *refs):
+    grad = mm(lhs[...], rhs[...], "tn")
+    if first_step:
+        w_out, mv_out, delta_out = refs
+        begin = w_ref[...].astype(F32)
+        fresh, first, second = adam_values(begin, mv_ref[0], mv_ref[1], grad, rate, number)
+        w_out[...] = fresh.astype(BF16)
+        mv_out[0] = first.astype(BF16)
+        mv_out[1] = second.astype(BF16)
+        delta_out[...] = (begin - fresh).astype(BF16)
+    else:
+        delta_in, delta_out = refs
+        begin = w_ref[...].astype(F32)
+        fresh, _, _ = adam_values(begin, mv_ref[0].astype(F32), mv_ref[1].astype(F32), grad, rate, number)
+        delta_out[...] = (delta_in[...].astype(F32) + (begin - fresh)).astype(BF16)
+
+
+def grow_call(number, rate, first_step, lhs, rhs, w, mv, *more):
+    deep, wide = w.shape
+    tile = 256
+    mat = pl.BlockSpec((tile, wide), lambda i: (i, 0))
+    pair = pl.BlockSpec((2, tile, wide), lambda i: (0, i, 0))
+    low = jax.ShapeDtypeStruct((deep, wide), BF16)
+    if first_step:
+        outs, specs = (low, jax.ShapeDtypeStruct((2, deep, wide), BF16), low), (mat, pair, mat)
+    else:
+        outs, specs = low, mat
+    return pl.pallas_call(
+        functools.partial(grow_kernel, number, rate, first_step),
+        out_shape=outs,
+        grid=(deep // tile,),
+        in_specs=[pl.BlockSpec((768, tile), lambda i: (0, i)), pl.BlockSpec((768, wide), lambda i: (0, 0)), mat, pair]
+        + [mat] * len(more),
+        out_specs=specs,
+        compiler_params=pltpu.CompilerParams(vmem_limit_bytes=48 << 20),
+    )(lhs, rhs, w, mv, *more)
+
 
 def turned_gather(arrays, axis, dims):
     turned = [jnp.moveaxis(a, dim, 0) for a, dim in zip(arrays, dims)]
@@ -445,99 +787,6 @@
             for b, t, dim in zip(blocks, turned, dims)
         )
     )
-
-
-def normalize(values):
-    return values * lax.rsqrt(jnp.mean(values * values, axis=-1, keepdims=True) + EPS_NORM)
-
-
-def norm_back(values, grad_norm):
-    scale = lax.rsqrt(jnp.mean(values * values, axis=-1, keepdims=True) + EPS_NORM)
-    normed = values * scale
-    return scale * (grad_norm - normed * jnp.mean(grad_norm * normed, axis=-1, keepdims=True))
-
-
-def gelu_exact(values):
-    return jax.nn.gelu(values, approximate=False)
-
-
-def route_table(choices, count, capacity):
-    flat = choices.reshape(-1)
-    onehot = (flat[:, None] == jnp.arange(count, dtype=jnp.int32)[None, :]).astype(jnp.int32)
-    before = jnp.cumsum(onehot, axis=0) - onehot
-    slot = jnp.sum(before * onehot, axis=1)
-    place = flat * capacity + slot
-    marks = jnp.arange(flat.shape[0], dtype=jnp.int32) + 1
-    table = jnp.zeros((count * capacity,), jnp.int32).at[place].set(marks)
-    return (place, table)
-
-
-def split_heads(qkv, heads):
-    tokens_here, triple = qkv.shape
-    size = triple // (3 * heads)
-    parts = qkv.reshape(tokens_here // LEN, LEN, 3, heads, size)
-    return (parts[:, :, 0], parts[:, :, 1], parts[:, :, 2], size ** (-0.5))
-
-
-def attend(qkv, heads):
-    query, key, value, scale = split_heads(qkv, heads)
-    scores = jnp.einsum("sqhd,skhd->shqk", query, key, preferred_element_type=jnp.float32) * scale
-    causal = jnp.arange(LEN)[:, None] >= jnp.arange(LEN)[None, :]
-    scores = jnp.where(causal, scores, -1e30)
-    top = jnp.max(scores, axis=-1, keepdims=True)
-    expo = jnp.exp(scores - top)
-    probs = expo / jnp.sum(expo, axis=-1, keepdims=True)
-    probs_low = probs.astype(jnp.bfloat16)
-    mixed = jnp.einsum("shqk,skhd->sqhd", probs_low, value, preferred_element_type=jnp.float32)
-    return (probs, probs_low, mixed.reshape(qkv.shape[0], -1).astype(jnp.bfloat16))
-
-
-def attend_back(qkv, probs, probs_low, grad_mixed, heads):
-    query, key, value, scale = split_heads(qkv, heads)
-    grad_heads = grad_mixed.reshape(query.shape)
-    grad_value = jnp.einsum(
-        "shqk,sqhd->skhd", probs_low, grad_heads, preferred_element_type=jnp.float32
-    )
-    grad_probs = jnp.einsum(
-        "sqhd,skhd->shqk", grad_heads, value, preferred_element_type=jnp.float32
-    )
-    grad_scores = probs * (grad_probs - jnp.sum(probs * grad_probs, axis=-1, keepdims=True))
-    grad_low = grad_scores.astype(jnp.bfloat16)
-    grad_query = (
-        jnp.einsum("shqk,skhd->sqhd", grad_low, key, preferred_element_type=jnp.float32) * scale
-    )
-    grad_key = (
-        jnp.einsum("shqk,sqhd->skhd", grad_low, query, preferred_element_type=jnp.float32) * scale
-    )
-    stacked = jnp.stack([grad_query, grad_key, grad_value], axis=2)
-    return stacked.reshape(qkv.shape).astype(jnp.bfloat16)
-
-
-def expert_forward(rows, first, second):
-    pre = jnp.dot(rows, first, preferred_element_type=jnp.float32)
-    act = gelu_exact(pre).astype(jnp.bfloat16)
-    result = jnp.dot(act, second, preferred_element_type=jnp.float32)
-    return (pre, act, result)
-
-
-def expert_rows_back(first, second, pre, grad_result):
-    grad_act = lax.dot_general(grad_result, second, (((1,), (1,)), ((), ())), preferred_element_type=F32)
-    unused, gelu_pull = jax.vjp(gelu_exact, pre)
-    grad_pre = gelu_pull(grad_act)[0].astype(jnp.bfloat16)
-    grad_rows = lax.dot_general(grad_pre, first, (((1,), (1,)), ((), ())), preferred_element_type=F32)
-    return grad_pre, grad_rows
-
-
-def expert_weight_grads(rows, grad_pre, act, grad_result):
-    over_rows = (((0,), (0,)), ((), ()))
-    grad_second = lax.dot_general(act, grad_result, over_rows, preferred_element_type=F32)
-    grad_first = lax.dot_general(rows, grad_pre, over_rows, preferred_element_type=F32)
-    return grad_first, grad_second
-
-
-def adam_step(master, state, grad, rate, number):
-    fresh, first, second = adam_values(master, state[0], state[1], grad, rate, number)
-    return fresh, (first, second)
 
 
 def cols_and_square(wide, square):
@@ -574,19 +823,9 @@
     state_in,
     state_out,
 ):
-    groups = lax.axis_size("group")
-    frozen = frozen_in.shape[0]
-    count = 17
-    width = tokens.shape[2]
-    tok = tokens.shape[1]
-    capacity = 3 * tok // count
-    start_in, start_out = tuple(
-        (
-            part[0].astype(jnp.float32)
-            for part in turned_gather(
-                (exp_in.astype(jnp.bfloat16), exp_out.astype(jnp.bfloat16)), "group", (1, 2)
-            )
-        )
+    low_in, low_out = tuple(
+        part[0]
+        for part in turned_gather((exp_in.astype(BF16), exp_out.astype(BF16)), "group", (1, 2))
     )
     w_start = cols_and_square(w_qkv, w_proj)
     moments = jnp.stack([cols_and_square(state_qkv[0, k], state_proj[0, k]) for k in range(2)])
@@ -594,104 +833,44 @@
         [router, gains.T, state_router[0, 0], state_gains[0, 0].T, state_router[0, 1], state_gains[0, 1].T], axis=1
     )
     packed = jnp.pad(packed, ((0, 0), (0, 128 - packed.shape[1])))
+    ids = jnp.pad(jnp.swapaxes(expert_ids, 1, 2), ((0, 0), (0, 6), (0, 0)))
+    factor = jnp.where(replay > 0, REPLAY_WEIGHT, 1.0).astype(F32)[:, :, None]
     whole, p_start, mv, all_extra = entry_call(w_start, moments, packed)
     p_start, mv = p_start.reshape(2, 48, 768), mv.reshape(2, 2, 48, 768)
     all_extra = all_extra.reshape(768, 128)
     pe_start = extra_rows(all_extra, 0)
     mve = jnp.stack([extra_rows(all_extra, 19), extra_rows(all_extra, 38)])
     p_now, pe_now = p_start, pe_start
-    masters = [start_in, start_out]
-    expert_moments = [state_in[0, :, 0], state_out[0, :, 0]]
+    states = [state_in[0, :, 0], state_out[0, :, 0]]
+    weights = [low_in, low_out]
+    deltas = [(), ()]
     block_list = []
     grad_list = []
     for step in range(STEPS):
         blocks = whole.reshape(4, 768, 768)
-        qkv_b = jnp.concatenate([blocks[0], blocks[1], blocks[2]], axis=1)
-        proj_b = blocks[3]
-        low_extra = pe_now.astype(BF16)
-        router_b = low_extra[:17].T
-        gain_f = low_extra[17:19].astype(F32)
-        first_b = masters[0].astype(jnp.bfloat16)
-        second_b = masters[1].astype(jnp.bfloat16)
-        inputs = tokens[step].astype(jnp.float32)
-        choices = expert_ids[step]
-        factor = jnp.where(replay[step] > 0, REPLAY_WEIGHT, 1.0).astype(jnp.float32)
-        cotangent = out_grad[step].astype(jnp.float32) * factor[:, None]
-        normed = normalize(inputs)
-        acts = (normed * gain_f[0]).astype(jnp.bfloat16)
-        qkv = jnp.dot(acts, qkv_b, preferred_element_type=jnp.float32).astype(jnp.bfloat16)
-        probs, probs_low, mixed = attend(qkv, HEADS)
-        middle = inputs + jnp.dot(mixed, proj_b, preferred_element_type=jnp.float32)
-        normed_mid = normalize(middle)
-        routed = (normed_mid * gain_f[1]).astype(jnp.bfloat16)
-        logits = jnp.dot(routed, router_b, preferred_element_type=jnp.float32)
-        select = (choices[:, :, None] == jnp.arange(count, dtype=jnp.int32)[None, None, :]).astype(
-            jnp.float32
+        given = (tokens[step], out_grad[step], factor[step], ids[step], blocks, pe_now)
+        send, frozen, *kept = front_call(*given)
+        ret, frozen_res, rows, grad_rows, hidden, grad_hidden = trade_call(
+            4 + step, send, frozen, weights[0], weights[1], frozen_in[0], frozen_out[0]
         )
-        picked = jnp.sum(select * logits[:, None, :], axis=-1)
-        picked_top = jnp.max(picked, axis=-1, keepdims=True)
-        picked_exp = jnp.exp(picked - picked_top)
-        weights = picked_exp / jnp.sum(picked_exp, axis=-1, keepdims=True)
-        place, table = route_table(choices, count, capacity)
-        doubled = jnp.repeat(routed, 2, axis=0)
-        grad_choice = (weights[:, :, None] * cotangent[:, None, :]).reshape(2 * tok, width).astype(BF16)
-        both = jnp.concatenate([doubled, grad_choice], axis=1)
-        padded = jnp.concatenate([jnp.zeros((1, 2 * width), jnp.bfloat16), both])
-        rows = padded[table].reshape(count, capacity, 2 * width)
-        sent = jnp.concatenate([rows[frozen:], rows[frozen:]])
-        arrived = lax.all_to_all(sent, ("dp", "expert"), split_axis=0, concat_axis=0, tiled=True)
-        frozen_rows, frozen_grad = rows[0, :, :width], rows[0, :, width:]
-        frozen_pre, frozen_act, frozen_res = expert_forward(frozen_rows, frozen_in[0], frozen_out[0])
-        unused_pre, frozen_back = expert_rows_back(frozen_in[0], frozen_out[0], frozen_pre, frozen_grad)
-        expert_rows = arrived[:, :, :width].reshape(-1, width)
-        expert_grad = arrived[:, :, width:].reshape(-1, width)
-        pre, act, partial_value = expert_forward(expert_rows, first_b, second_b)
-        grad_pre, partial_rows = expert_rows_back(first_b, second_b, pre, expert_grad)
-        answer = jnp.concatenate([partial_value.astype(BF16), partial_rows.astype(BF16)], axis=1)
-        answer = answer.reshape(32, capacity, 2 * width)
-        returned = lax.all_to_all(answer, ("dp", "expert"), split_axis=0, concat_axis=0, tiled=True)
-        returned = returned.astype(F32)
-        returned = (returned[:16] + returned[16:]).astype(BF16).astype(F32).reshape(-1, 2 * width)
-        grads = expert_weight_grads(expert_rows, grad_pre, act, expert_grad)
-        outputs = jnp.concatenate([jnp.concatenate([frozen_res, frozen_back], axis=1), returned])
-        gathered_both = outputs[place].reshape(tok, 2, 2 * width)
-        gathered = gathered_both[:, :, :width]
-        block = middle + jnp.sum(weights[:, :, None] * gathered, axis=1)
-        block_list.append(block.astype(jnp.bfloat16))
-        grad_pick = jnp.sum(cotangent[:, None, :] * gathered, axis=-1)
-        grad_logit_pick = weights * (
-            grad_pick - jnp.sum(weights * grad_pick, axis=-1, keepdims=True)
-        )
-        grad_logits = jnp.sum(select * grad_logit_pick[:, :, None], axis=1)
-        grad_router = jnp.dot(
-            grad_logits.T, routed.astype(jnp.float32), precision=lax.Precision.HIGHEST
-        )
-        grad_routed = jnp.dot(
-            grad_logits, router_b.astype(jnp.float32).T, precision=lax.Precision.HIGHEST
-        )
-        grad_routed = grad_routed + jnp.sum(gathered_both[:, :, width:], axis=1)
-        grad_gain_two = jnp.sum(normed_mid * grad_routed, axis=0)
-        grad_middle = cotangent + norm_back(middle, grad_routed * gain_f[1])
-        grad_branch = grad_middle.astype(jnp.bfloat16)
-        over_rows = (((0,), (0,)), ((), ()))
-        grad_proj = lax.dot_general(mixed, grad_branch, over_rows, preferred_element_type=F32)
-        grad_mixed = jnp.einsum(
-            "te,de->td", grad_branch, proj_b, preferred_element_type=jnp.float32
-        ).astype(jnp.bfloat16)
-        grad_qkv = attend_back(qkv, probs, probs_low, grad_mixed, HEADS)
-        grad_acts = jnp.einsum("te,de->td", grad_qkv, qkv_b, preferred_element_type=jnp.float32)
-        grad_gain_one = jnp.sum(normed * grad_acts, axis=0)
-        grad_list.append(grad_middle + norm_back(inputs, grad_acts * gain_f[0]))
-        dense_grads = jnp.stack(
-            [
-                lax.dot_general(acts, grad_qkv[:, k * 768 : (k + 1) * 768], over_rows, preferred_element_type=F32)
-                for k in range(3)
+        for index, (lhs, rhs) in enumerate(((rows, grad_hidden), (hidden, grad_rows))):
+            grown = grow_call(
+                STEP + step, RATES[4 + index], step == 0, lhs, rhs, weights[index], states[index], *deltas[index]
+            )
+            if step == 0:
+                weights[index], states[index], delta = grown
+                deltas[index] = (delta,)
+            else:
+                deltas[index] = grown
+        if step == 1:
+            summed = [
+                lax.psum_scatter(deltas[0], "group", scatter_dimension=0, tiled=True),
+                lax.psum_scatter(deltas[1], "group", scatter_dimension=1, tiled=True),
             ]
-            + [grad_proj]
-        ).astype(BF16).reshape(WHOLE)
-        extra = jnp.concatenate(
-            [grad_router, grad_gain_one[None], grad_gain_two[None], jnp.zeros((5, 768), F32)]
-        )
+        block, grad, dense_grads, extra = back_call(*given, *kept, ret, frozen_res)
+        block_list.append(block)
+        grad_list.append(grad)
+        dense_grads = dense_grads.reshape(WHOLE)
         if step == 0:
             whole, p_now, mv, pe_now, mve = renew_call(STEP, dense_grads, extra, p_now, mv, pe_now, mve)
         else:
@@ -699,18 +878,6 @@
                 STEP + 1, dense_grads, extra, p_now, mv, pe_now, mve, p_start, pe_start,
                 w_start, cols_and_square(mom_qkv, mom_proj),
             )
-        for index in range(2):
-            masters[index], expert_moments[index] = adam_step(
-                masters[index], expert_moments[index], grads[index], RATES[4 + index], STEP + step
-            )
-    expert_deltas = (
-        lax.psum_scatter(
-            (start_in - masters[0]).astype(jnp.bfloat16), "group", scatter_dimension=0, tiled=True
-        ).astype(jnp.float32),
-        lax.psum_scatter(
-            (start_out - masters[1]).astype(jnp.bfloat16), "group", scatter_dimension=1, tiled=True
-        ).astype(jnp.float32),
-    )
     at = 24 * (16 * lax.axis_index("dp") + lax.axis_index("expert"))
     mine = lax.dynamic_slice(delta_e, (0, at), (24, 24))
     new_params = []
@@ -718,8 +885,8 @@
     for delta, begin, moment in (
         (mine[17:19], gains, mom_gains),
         (mine[:17].T, router, mom_router),
-        (expert_deltas[0][None] / groups, exp_in, mom_in),
-        (expert_deltas[1][None] / groups, exp_out, mom_out),
+        (summed[0].astype(F32)[None] * 0.25, exp_in, mom_in),
+        (summed[1].astype(F32)[None] * 0.25, exp_out, mom_out),
     ):
         renewed = OUTER_MOMENTUM * moment + delta
         new_moms.append(renewed)

time: 592 us -> 540 us (0.912); the launches traced: 582 us -> 536 us
  Pallas kernels: 189 us -> 440 us
  matrix products: 156 us -> 0 us
  other arithmetic: 66 us -> 17.2 us
  local copies, waits for them, and re-layouts: 101 us -> 64.9 us
  starting transfers between devices: 29.1 us -> 0.12 us
  waiting for transfers between devices: 24.4 us -> 0.05 us
    pallas_call x0 -> x10, Pallas kernels: none -> 229 us  [the longest x2 157 us: trade_call(): pl.pallas_call(trade_kernel, out_shape=tuple((jax.ShapeDtypeStruct(shape,...]
    dot_general x50 -> x0, matrix products: 153 us -> none  [the longest x4 32.5 us: expert_forward(): pre = jnp.dot(rows, first, preferred_element_type=jnp.float32)]
    unnamed x240 -> x165, local copies, waits for them, and re-layouts: 24.1 us -> 55.8 us
    all_to_all x4 -> x0, starting transfers between devices: 28.6 us -> none  [the longest x2 14.8 us: body(): lax.all_to_all(answer, ('dp', 'expert'), split_axis=0, concat_axis=0, til...]
    all_to_all x4 -> x0, waiting for transfers between devices: 24.3 us -> none  [the longest x2 18 us: body(): lax.all_to_all(sent, ('dp', 'expert'), split_axis=0, concat_axis=0, tiled...]
    slice x14 -> x0, local copies, waits for them, and re-layouts: 23.6 us -> none  [the longest x1 8 us: adam_step(): state[1]]
    reshape x14 -> x0, local copies, waits for them, and re-layouts: 22.9 us -> none  [the longest x2 6.29 us: body(): answer = answer.reshape(32, capacity, 2 * width)]
    pallas_call x3, Pallas kernels: 189 us -> 211 us  [vmem_call(): pl.pallas_call(kernel, out_shape=tuple((jax.ShapeDtypeStruct(shape, kind)...]
  transfers between devices with their start and end apart: 7 -> 3, of which waited for: 2 -> 0; matrix products, arithmetic and copies ran while one was open for 32% -> 5% of each run, Pallas kernels for 20% -> 28%
where the time goes in v2:
time: 540 us; the launch traced here: 536 us
  Pallas kernels  440 us (81%)
  local copies, waits for them, and re-layouts  64.9 us (12%)
  other arithmetic  17.2 us (3%)
  between operations  14.6 us (3%)
    pallas_call x3, Pallas kernels, vmem_call(): pl.pallas_call(kernel, out_shape=tuple((jax.ShapeDtypeStruct(shape, kind)...  211 us
    pallas_call x2, Pallas kernels, trade_call(): pl.pallas_call(trade_kernel, out_shape=tuple((jax.ShapeDtypeStruct(shape,...  157 us
    unnamed x165, local copies, waits for them, and re-layouts  55.8 us
    pallas_call x4, Pallas kernels, grow_call(): pl.pallas_call(functools.partial(grow_kernel, number, rate, first_step),...  40.1 us
    pallas_call x4, Pallas kernels, plain_call(): pl.pallas_call(kernel, out_shape=tuple((jax.ShapeDtypeStruct(shape, kind)...  31.6 us
  transfers between devices with their start and end apart: 3, of which 0 were waited for; matrix products, arithmetic and copies ran while one was open for 5% of the time, Pallas kernels for 28%

profile of v2, /device:TPU:1, one launch (start us, length us, event | category | flops | bytes accessed | tf_op | source)
XLA Modules:
  0.0 536.4 jit_solution(18026392263841915018)
XLA Ops:
  7.2 1.4 convert_bitcast_fusion
  8.9 1.1 pad_maximum_fusion
  11.5 0.9 pad_maximum_fusion.2.mv_in
  12.7 0.8 pad_maximum_fusion.4
  13.5 43.6 %shard_map.335 = (bf16[4,2,4,2,48,768]{5,4,3,2,1,0:T(8,128)(2,1)}, f32[4,24,768]{2,1,0:T(8,128)}, f32[2,4,24,768]{3,2,1,0:T(8,128)}, f32[2,4,4,24,128]{4,3,2,1,0:T(8,128)}) custom-call(f32[4,24,768]{2,1,0:T(8,128)} %get-tuple-element.221.p_in.w_old, f32[2,4,24,768]{3,2,1,0:T(8,128)} %pad_maximum_fusion.2.mv_in, f32[24,128]{1,0:T(8,128)} %pad.19.e_in), custom_call_target="tpu_custom_call" | custom-call | tf_op jit(solution)/shard_map/pallas_call | solution.py:395
  57.2 1.6 fusion.7
  59.6 4.8 shard_map.336
  64.5 1.0 copy-done.9
  65.5 0.7 copy-done.21
  66.2 0.7 copy-done.37
  66.9 0.7 copy-done.39
  70.2 4.9 fusion.6
  75.1 4.9 copy.110
  80.0 79.1 %shard_map.337 = (bf16[32,48,768]{2,1,0:T(8,128)(2,1)}, f32[48,768]{1,0:T(8,128)}, bf16[768,768]{1,0:T(8,128)(2,1)}, bf16[768,768]{1,0:T(8,128)(2,1)}, bf16[768,...) custom-call(bf16[16,48,768]{2,1,0:T(8,128)(2,1)} %copy-done.9, bf16[48,768]{1,0:T(8,128)(2,1)} %copy-done.45, ...), custom_call_target="tpu_custom_call" | custom-call | tf_op jit(solution)/shard_map/pallas_call | solution.py:720
  159.1 1.3 copy-done.13
  160.4 11.2 %shard_map.342 = (bf16[1536,768]{1,0:T(8,128)(2,1)S(1)}, bf16[2,1536,768]{2,1,0:T(8,128)(2,1)}, bf16[1536,768]{1,0:T(8,128)(2,1)S(1)}) custom-call(bf16[768,1536]{1,0:T(8,128)(2,1)} %get-tuple-element.102.lhs, bf16[768,768]{1,0:T(8,128)(2,1)S(1)} %copy-done.13, bf16[1536,768]{1,0:T(8,128)(2,1)} %bitcast.144, f32[2,1536,768]{2,1,0:T(8,128)} %bitcast.154), custom_call_target="tpu_custom_call" | custom-call | tf_op jit(solution)/shard_map/pallas_call | solution.py:767
  171.5 1.5 copy-done.1
  173.0 1.5 copy-done.5
  174.5 11.0 %shard_map.341 = (bf16[768,1536]{1,0:T(8,128)(2,1)S(1)}, bf16[2,768,1536]{2,1,0:T(8,128)(2,1)}, bf16[768,1536]{1,0:T(8,128)(2,1)S(1)}) custom-call(bf16[768,768]{1,0:T(8,128)(2,1)S(1)} %copy-done.12, bf16[768,1536]{1,0:T(8,128)(2,1)} %get-tuple-element.100.rhs, bf16[768,1536]{1,0:T(8,128)(2,1)} %get-tuple-element.175.w1_hbm.w_ref, f32[2,768,1536]{2,1,0:T(8,128)} %bitcast.155), custom_call_target="tpu_custom_call" | custom-call | tf_op jit(solution)/shard_map/pallas_call | solution.py:767
  185.5 1.4 copy-done
  186.9 1.4 copy-done.4
  188.4 10.7 %shard_map.338 = (bf16[128,768]{1,0:T(8,128)(2,1)S(1)}, f32[128,768]{1,0:T(8,128)S(1)}, bf16[4,768,768]{2,1,0:T(8,128)(2,1)}, f32[24,768]{1,0:T(8,128)S(1)}) custom-call(bf16[128,768]{1,0:T(8,128)(2,1)S(1)} %get-tuple-element.220.x_ref, bf16[128,768]{1,0:T(8,128)(2,1)S(1)} %get-tuple-element.183.og_ref, f32[128,1]{1,0:T(8,128)S(1)} %copy.92.factor_ref, ...), custom_call_target="tpu_custom_call" | custom-call | tf_op jit(solution)/shard_map/pallas_call | solution.py:691
  199.1 0.7 copy-done.23
  199.8 0.7 copy-done.27
  201.2 86.3 %shard_map.339 = (bf16[4,2,4,2,48,768]{5,4,3,2,1,0:T(8,128)(2,1)}, f32[2,48,768]{2,1,0:T(8,128)}, f32[2,2,48,768]{3,2,1,0:T(8,128)}, f32[24,768]{1,0:T(8,128)}, f32[2,24,768]{2,1,0:T(8,128)}) custom-call(bf16[4,2,4,2,48,768]{5,4,3,2,1,0:T(8,128)(2,1)} %bitcast.157, f32[24,768]{1,0:T(8,128)} %copy-done.47, f32[2,48,768]{2,1,0:T(8,128)} %bitcast.159, ...), custom_call_target="tpu_custom_call" | custom-call | tf_op jit(solution)/shard_map/pallas_call | solution.py:395
  287.4 0.9 copy-done.17
  288.3 4.8 shard_map.340
  293.2 1.0 copy-done.10
  294.2 0.9 copy-done.15
  295.1 0.7 copy-done.19
  297.2 0.7 copy-done.35
  298.5 78.1 %shard_map.343 = (bf16[32,48,768]{2,1,0:T(8,128)(2,1)}, f32[48,768]{1,0:T(8,128)}, bf16[768,768]{1,0:T(8,128)(2,1)}, bf16[768,768]{1,0:T(8,128)(2,1)}, bf16[768,...) custom-call(bf16[16,48,768]{2,1,0:T(8,128)(2,1)} %copy-done.10, bf16[48,768]{1,0:T(8,128)(2,1)} %copy-done.46, ...), custom_call_target="tpu_custom_call" | custom-call | tf_op jit(solution)/shard_map/pallas_call | solution.py:720
  376.6 1.7 copy-done.7
  378.3 1.3 copy-done.14
  379.6 8.7 %shard_map.347 = bf16[1536,768]{1,0:T(8,128)(2,1)S(1)} custom-call(bf16[768,1536]{1,0:T(8,128)(2,1)S(1)} %copy-done.7, bf16[768,768]{1,0:T(8,128)(2,1)S(1)} %copy-done.14, bf16[1536,768]{1,0:T(8,128)(2,1)} %copy-done.1, bf16[2,1536,768]{2,1,0:T(8,128)(2,1)} %get-tuple-element.123.mv_ref, bf16[1536,768]{1,0:T(8,128)(2,1)} %copy-done.5), custom_call_target="tpu_custom_call" | custom-call | tf_op jit(solution)/shard_map/pallas_call | solution.py:767
  388.2 2.5 copy.105
  390.8 1.6 copy-done.6
  392.3 1.3 copy-done.11
  393.6 9.3 %shard_map.346 = bf16[768,1536]{1,0:T(8,128)(2,1)} custom-call(bf16[768,768]{1,0:T(8,128)(2,1)S(1)} %copy-done.11, bf16[768,1536]{1,0:T(8,128)(2,1)S(1)} %copy-done.6, bf16[768,1536]{1,0:T(8,128)(2,1)} %copy-done, bf16[2,768,1536]{2,1,0:T(8,128)(2,1)} %get-tuple-element.119.mv_ref, bf16[768,1536]{1,0:T(8,128)(2,1)} %copy-done.4), custom_call_target="tpu_custom_call" | custom-call | tf_op jit(solution)/shard_map/pallas_call | solution.py:767
  402.9 1.2 copy-done.53
  404.2 1.6 copy.100
  405.9 3.0 copy.99
  409.0 1.1 copy-done.16
  410.1 1.0 copy-done.20
  411.1 0.9 copy-done.32
  412.1 1.0 copy-done.34
  413.0 0.9 copy-done.36
  414.0 0.9 copy-done.43
  414.9 11.3 %shard_map.344 = (bf16[128,768]{1,0:T(8,128)(2,1)S(1)}, f32[128,768]{1,0:T(8,128)S(1)}, bf16[4,768,768]{2,1,0:T(8,128)(2,1)}, f32[24,768]{1,0:T(8,128)S(1)}) custom-call(bf16[128,768]{1,0:T(8,128)(2,1)S(1)} %get-tuple-element.219.x_ref, bf16[128,768]{1,0:T(8,128)(2,1)S(1)} %get-tuple-element.184.og_ref, f32[128,1]{1,0:T(8,128)S(1)} %copy.96.factor_ref, ...), custom_call_target="tpu_custom_call" | custom-call | tf_op jit(solution)/shard_map/pallas_call | solution.py:691
  426.1 0.7 copy-done.25
  428.2 80.8 %shard_map.345 = (f32[4,24,768]{2,1,0:T(8,128)}, f32[4,24,768]{2,1,0:T(8,128)}, f32[24,768]{1,0:T(8,128)}) custom-call(bf16[4,2,4,2,48,768]{5,4,3,2,1,0:T(8,128)(2,1)} %bitcast.156, f32[24,768]{1,0:T(8,128)} %copy-done.48, f32[2,48,768]{2,1,0:T(8,128)} %get-tuple-element.112.p_in, f32[2,2,48,768]{3,2,1,0:T(8,128)} %get-tuple-element.113.mv_in, ...), custom_call_target="tpu_custom_call" | custom-call | tf_op jit(solution)/shard_map/pallas_call | solution.py:395
  509.0 0.9 multiply_subtract_fusion
  509.9 0.7 copy.101
  510.6 0.7 copy.103
  511.3 0.8 pad_maximum_fusion.3
  512.0 0.9 pad_maximum_fusion.1
  513.0 1.3 multiply_subtract_fusion.1
  515.6 0.7 pad_maximum_fusion.7
  516.3 0.7 pad_maximum_fusion.6
  517.0 1.3 copy.106
  518.4 3.5 bitcast_add_fusion.1
  521.9 3.0 copy.102
  524.9 1.5 copy.104
  526.4 3.3 fusion.3
  (163 shorter events, 10.8 us)
Async XLA Ops:
  7.2 1.6 copy-start.54
  7.2 63.0 %all-gather.2.cloned.1.call-start = ((), (), s32[]{:S(2)}) async-start(), calls=%async_computation.2 | async-start | bytes 5898240 | tf_op jit(solution)/shard_map/all_gather | solution.py:782
  8.9 1.3 copy-start.67
  8.9 1.5 copy-start.71
  8.9 1.6 copy-start.69
  8.9 1.7 copy-start.66
  8.9 2.4 copy-start.63
  8.9 2.4 copy-start.56
  10.1 506.9 %reduce-scatter.7.cloned.1.call-start = ((), (), s32[]{:S(2)}) async-start(), calls=%async_computation.4 | async-start | bytes 2949120
  11.4 1.0 copy-start.61
  11.4 1.0 copy-start.62
  11.5 1.1 copy-start.64
  11.5 1.2 copy-start.65
  57.1 1.8 copy-start.72
  57.1 2.4 copy-start.70
  57.2 2.4 copy-start.57
  57.2 2.4 copy-start.58
  58.9 129.4 %copy-start.8 = (f32[24,768]{1,0:T(8,128)}, f32[24,768]{1,0:T(8,128)S(1)}, u32[]{:S(2)}) copy-start(f32[24,768]{1,0:T(8,128)S(1)} %pad.20.pe_ref.pe_in.pe_start) | copy-start | bytes 221188
  64.5 1.0 copy-start.9
  65.5 0.7 copy-start.21
  159.1 1.3 copy-start.13
  160.3 14.1 %copy-start.12 = (bf16[768,768]{1,0:T(8,128)(2,1)S(1)}, bf16[768,768]{1,0:T(8,128)(2,1)}, u32[]{:S(2)}) copy-start(bf16[768,768]{1,0:T(8,128)(2,1)} %get-tuple-element.99.lhs) | copy-start | bytes 3538948
  171.5 1.5 copy-start.1
  173.0 1.5 copy-start.5
  174.5 13.9 %copy-start.3 = (bf16[32,48,768]{2,1,0:T(8,128)(2,1)S(1)}, bf16[32,48,768]{2,1,0:T(8,128)(2,1)}, u32[]{:S(2)}) copy-start(bf16[32,48,768]{2,1,0:T(8,128)(2,1)} %get-tuple-element.81.ret) | copy-start | bytes 7077892
  174.5 13.9 %copy-start.22 = (f32[128,768]{1,0:T(8,128)S(1)}, f32[128,768]{1,0:T(8,128)}, u32[]{:S(2)}) copy-start(f32[128,768]{1,0:T(8,128)} %copy-done.21) | copy-start | bytes 1179652
  174.5 13.9 %copy-start.38 = (bf16[128,768]{1,0:T(8,128)(2,1)S(1)}, bf16[128,768]{1,0:T(8,128)(2,1)}, u32[]{:S(2)}) copy-start(bf16[128,768]{1,0:T(8,128)(2,1)} %copy-done.37) | copy-start | bytes 589828
  174.5 13.9 %copy-start.40 = (bf16[128,768]{1,0:T(8,128)(2,1)S(1)}, bf16[128,768]{1,0:T(8,128)(2,1)}, u32[]{:S(2)}) copy-start(bf16[128,768]{1,0:T(8,128)(2,1)} %copy-done.39) | copy-start | bytes 589828
  174.5 13.9 %copy-start.42 = (bf16[128,768]{1,0:T(8,128)(2,1)S(1)}, bf16[128,768]{1,0:T(8,128)(2,1)}, u32[]{:S(2)}) copy-start(bf16[128,768]{1,0:T(8,128)(2,1)} %copy-done.41) | copy-start | bytes 589828
  174.5 13.9 %copy-start.44 = (f32[48,768]{1,0:T(8,128)S(1)}, f32[48,768]{1,0:T(8,128)}, u32[]{:S(2)}) copy-start(f32[48,768]{1,0:T(8,128)} %get-tuple-element.82.frozen) | copy-start | bytes 442372
  174.5 13.9 %copy-start.50 = (f32[8,128]{1,0:T(8,128)S(1)}, f32[8,128]{1,0:T(8,128)}, u32[]{:S(2)}) copy-start(f32[8,128]{1,0:T(8,128)} %copy-done.49) | copy-start | bytes 12292
  185.5 1.4 copy-start
  186.9 1.4 copy-start.4
  199.1 0.7 copy-start.23
  287.4 0.9 copy-start.17
  293.2 1.0 copy-start.10
  294.2 0.9 copy-start.15
  295.1 0.7 copy-start.19
  376.6 1.7 copy-start.7
  378.3 1.3 copy-start.14
  390.7 1.7 copy-start.6
  390.7 135.7 %reduce-scatter.5.cloned.1.call-start = ((), (), s32[]{:S(2)}) async-start(), calls=%async_computation.3 | async-start | bytes 2949120 | tf_op jit(solution)/shard_map/reduce_scatter | solution.py:867
  392.3 1.3 copy-start.11
  402.9 1.3 copy-start.53
  405.8 3.1 copy-start.68
  405.8 3.2 copy-start.2
  405.8 3.2 copy-start.18
  409.0 1.1 copy-start.16
  410.1 1.0 copy-start.20
  411.1 0.9 copy-start.32
  412.1 1.0 copy-start.34
  413.0 0.9 copy-start.36
  414.0 0.9 copy-start.43
  426.1 0.7 copy-start.25
  428.2 83.1 %copy-start.28 = (bf16[128,768]{1,0:T(8,128)(2,1)S(1)}, bf16[128,768]{1,0:T(8,128)(2,1)}, u32[]{:S(2)}) copy-start(bf16[128,768]{1,0:T(8,128)(2,1)} %copy-done.27) | copy-start | bytes 589828
  428.2 83.1 %copy-start.30 = (bf16[128,768]{1,0:T(8,128)(2,1)S(1)}, bf16[128,768]{1,0:T(8,128)(2,1)}, u32[]{:S(2)}) copy-start(bf16[128,768]{1,0:T(8,128)(2,1)} %copy-done.29) | copy-start | bytes 589828
  428.2 83.8 %copy-start.24 = (f32[128,768]{1,0:T(8,128)S(1)}, f32[128,768]{1,0:T(8,128)}, u32[]{:S(2)}) copy-start(f32[128,768]{1,0:T(8,128)} %copy-done.23) | copy-start | bytes 1179652
  428.2 83.8 %copy-start.26 = (f32[128,768]{1,0:T(8,128)S(1)}, f32[128,768]{1,0:T(8,128)}, u32[]{:S(2)}) copy-start(f32[128,768]{1,0:T(8,128)} %copy-done.25) | copy-start | bytes 1179652
  509.0 4.0 copy-start.73
  509.0 5.3 copy-start.60
  509.0 6.0 %copy-start.59 = (f32[4,24,768]{2,1,0:T(8,128)S(1)}, f32[4,24,768]{2,1,0:T(8,128)}, u32[]{:S(2)}) copy-start(f32[4,24,768]{2,1,0:T(8,128)} %get-tuple-element.116) | copy-start | bytes 884740
  515.0 3.4 copy-start.51
  521.9 3.0 copy-start.52
  524.9 1.5 copy-start.55
  (13 other events, 8.6 us)
Sparse Core Ops, SparseCore 0:
  10.3 46.8 all-gather.1
  390.8 53.9 reduce-scatter.6
  447.7 43.6 reduce-scatter.4

commit v3 on v2

v3 whole, which is shorter than its diff:
```python
import functools

import jax
import jax.numpy as jnp
from jax import lax
from jax.experimental import pallas as pl
from jax.experimental.pallas import tpu as pltpu
from jax.sharding import PartitionSpec as P

MESH = pl.DeviceIdType.MESH
VMEM = pltpu.VMEM
F32 = jnp.float32
BF16 = jnp.bfloat16


class Links:
    def __init__(self, sends, recvs):
        self.sends, self.recvs, self.used, self.begun = sends, recvs, 0, []

    def send(self, src, dst, to):
        at = self.used
        self.used += 1
        copy = pltpu.make_async_remote_copy(
            src_ref=src, dst_ref=dst, send_sem=self.sends.at[at], recv_sem=self.recvs.at[at],
            device_id=to, device_id_type=MESH,
        )
        self.begun.append(copy)
        copy.start()
        return copy

    def finish(self):
        for copy in self.begun:
            copy.wait_send()


class Place:
    def __init__(self):
        self.g, self.d = lax.axis_index("group"), lax.axis_index("dp")
        e = lax.axis_index("expert")
        self.x, self.y = lax.div(e, 4), lax.rem(e, 4)

    def along_x(self, step, over=0):
        return {"dp": lax.rem(self.d + over, 2), "expert": lax.rem(self.x + step, 4) * 4 + self.y}

    def along_y(self, step, over=0):
        return {"dp": lax.rem(self.d + over, 2), "expert": self.x * 4 + lax.rem(self.y + step, 4)}

    def other_dp(self):
        return {"dp": 1 - self.d}

    def in_group(self, step):
        return {"group": lax.rem(self.g + step, 4)}

    def other_core(self):
        return {"group": self.g + 1 - 2 * lax.rem(self.g, 2)}


def hail(partners):
    barrier = pltpu.get_barrier_semaphore()
    for partner in partners:
        pl.semaphore_signal(barrier, inc=1, device_id=partner, device_id_type=MESH)


def await_hails(partners):
    pl.semaphore_wait(pltpu.get_barrier_semaphore(), len(partners))


PEERS = ((0, 1), (1, 0), (3, 0), (1, 1), (3, 1), (2, 0), (2, 1))


def ring_partners(place):
    return (
        [place.along_x(*peer) for peer in PEERS]
        + [place.along_y(step) for step in (1, 2, 3)]
        + [place.along_y(step, 1) for step in (1, 2, 3)]
    )


class Gather:
    def __init__(self, links, place, whole, h, p1, p2, near1, near2, at, share=None):
        self.links, self.whole, self.h, self.at, self.d, self.place = links, whole, h, at, place.d, place
        self.p1, self.p2, self.near1, self.near2, self.share = p1, p2, near1, near2, share
        self.shared = []

    def push(self, k1, k2, dp, to):
        c, x = self.at(lax.rem(k1, 4), lax.rem(k2, 4))
        ref = self.whole.at[c, slice(None) if dp is None else dp, x, self.h]
        return self.links.send(ref, ref, to)

    def give(self, k1, k2):
        if self.share is not None:
            self.shared.append(self.push(k1, k2, None, self.share))

    def start(self):
        p1, p2, d = self.p1, self.p2, self.d
        self.over_dp = self.push(p1, p2, d, self.place.other_dp())
        self.own = [self.push(p1, p2, d, self.near1(1)), self.push(p1, p2, d, self.near1(3))]

    def ring_one(self):
        p1, p2, d = self.p1, self.p2, self.d
        self.over_dp.wait_recv()
        self.own += [self.push(p1, p2, 1 - d, self.near1(1)), self.push(p1, p2, 1 - d, self.near1(3))]
        self.pushed = [(p1, self.push(p1, p2, None, self.near2(1)), self.push(p1, p2, None, self.near2(3)))]
        self.give(p1, p2)
        for copy in self.own:
            copy.wait_recv()
        self.passed = [self.push(p1 + 3, p2, 0, self.near1(1)), self.push(p1 + 1, p2, 1, self.near1(3))]
        for k1 in (p1 + 3, p1 + 1):
            self.pushed.append((k1, self.push(k1, p2, None, self.near2(1)), self.push(k1, p2, None, self.near2(3))))
            self.give(k1, p2)

    def ring_two(self):
        p1, p2 = self.p1, self.p2
        for copy in self.passed:
            copy.wait_recv()
        k1 = p1 + 2
        self.pushed.append((k1, self.push(k1, p2, None, self.near2(1)), self.push(k1, p2, None, self.near2(3))))
        self.give(k1, p2)
        self.last = []
        for k1, right, left in self.pushed:
            right.wait_recv()
            self.last.append((k1, self.push(k1, p2 + 3, 0, self.near2(1))))
            self.give(k1, p2 + 3)
            left.wait_recv()
            self.last.append((k1, self.push(k1, p2 + 1, 1, self.near2(3))))
            self.give(k1, p2 + 1)

    def end(self):
        for n, (k1, copy) in enumerate(self.last):
            copy.wait_recv()
            if n % 2:
                self.give(k1, self.p2 + 2)
        for copy in self.shared:
            copy.wait_recv()


def run_gather(parts):
    for stage in ("ring_one", "ring_two", "end"):
        for part in parts:
            getattr(part, stage)()


def gather_parts(links, place, whole):
    by_x = lambda kx, ky: (ky, kx)
    by_y = lambda ky, kx: (ky, kx)
    first = Gather(links, place, whole, 0, place.x, place.y, place.along_x, place.along_y, by_x)
    second = Gather(links, place, whole, 1, place.y, place.x, place.along_y, place.along_x, by_y)
    return first, second


class RingSum:
    def __init__(self, links, near1, near2, p1, p2, d, term, far, near, mid, box):
        self.links, self.near1, self.near2, self.p1, self.p2, self.d = links, near1, near2, p1, p2, d
        self.term, self.far, self.near, self.mid, self.box = term, far, near, mid, box
        self.steps = (2, 1, 3, 0)
        self.far_copies, self.direct, self.summed, self.over = [], [], [], []

    def get(self, k, dp, i):
        return self.term(lax.rem(self.p1 + k, 4), dp, lax.rem(self.p2 + self.steps[i], 4))

    def send_far(self, i):
        self.far_copies.append([
            self.links.send(self.get(2, 1, i), self.far.at[0, i], self.near1(1)),
            self.links.send(self.get(2, 0, i), self.far.at[1, i], self.near1(3)),
        ])

    def send_direct(self, i):
        self.direct.append([
            self.links.send(self.get(1, 0, i), self.near.at[0, 0, i], self.near1(1)),
            self.links.send(self.get(3, 1, i), self.near.at[1, 1, i], self.near1(3)),
        ])

    def middle(self, i):
        out = []
        for side, step, dp in ((0, 1, 1), (1, 3, 0)):
            self.far_copies[i][side].wait_recv()
            self.far[side, i] = (self.far[side, i].astype(F32) + self.get(step, dp, i)[...].astype(F32)).astype(BF16)
            out.append(self.links.send(self.far.at[side, i], self.near.at[side, dp, i], self.near1(step)))
        self.summed.append(out)

    def finish(self, i):
        for copy in self.direct[i] + self.summed[i]:
            copy.wait_recv()
        mine = self.d * 4 + self.p2
        for dp in range(2):
            self.mid[i, dp] = (
                self.get(0, dp, i)[...].astype(F32)
                + self.near[0, dp, i].astype(F32)
                + self.near[1, dp, i].astype(F32)
            ).astype(BF16)
        step = self.steps[i]
        for over in (0, 1):
            src = self.mid.at[i, lax.rem(self.d + over, 2)]
            if step or over:
                self.over.append(self.links.send(src, self.box.at[mine], self.near2(step, over)))
            else:
                self.box[mine] = self.mid[i, self.d]

    def total(self):
        for copy in self.over:
            copy.wait_recv()
        value = self.box[0].astype(F32)
        for k in range(1, 8):
            value = value + self.box[k].astype(F32)
        return value


def add_over(links, own, box, position, size, reach):
    box[position] = own
    copies = [links.send(box.at[position], box.at[position], reach(step)) for step in range(1, size)]

    def finish():
        for copy in copies:
            copy.wait_recv()
        total = box[0]
        for k in range(1, size):
            total = total + box[k]
        return total

    return finish


HALF_SCRATCH = [
    VMEM((2, 4, 48, 768), BF16), VMEM((2, 2, 4, 48, 768), BF16), VMEM((4, 2, 48, 768), BF16), VMEM((8, 48, 768), BF16)
]
REDUCE_SCRATCH = HALF_SCRATCH * 2 + [VMEM((4, 24, 768), F32), VMEM((4, 24, 768), F32), VMEM((2, 24, 768), F32)]
REDUCE_COPIES = 2 * (24 + 7) + 7
GATHER_COPIES = 2 * (1 + 4 + 2 + 8 + 8)


def reduce_all(links, place, grads, extra, scratch, between=None):
    box_x, box_y, box_z = scratch[8:]
    first = RingSum(
        links, place.along_y, place.along_x, place.y, place.x, place.d,
        lambda k, dp, j: grads.at[k, dp, j, 0], *scratch[:4],
    )
    second = RingSum(
        links, place.along_x, place.along_y, place.x, place.y, place.d,
        lambda k, dp, j: grads.at[j, dp, k, 1], *scratch[4:8],
    )
    parts = (first, second)
    for i in range(4):
        for part in parts:
            part.send_far(i)
    extra_x = add_over(links, extra, box_x, place.x, 4, place.along_x)
    for i in range(4):
        for part in parts:
            part.send_direct(i)
        for part in parts:
            part.middle(i)
        if between is not None:
            between(i)
        if i == 1:
            extra_y = add_over(links, extra_x(), box_y, place.y, 4, place.along_y)
        if i == 3:
            extra_z = add_over(links, extra_y(), box_z, place.d, 2, lambda step: place.other_dp())
    for i in range(4):
        for part in parts:
            part.finish(i)
    return [part.total() for part in parts], extra_z()


EPS_NORM = 1e-06
BETA_ONE = 0.9
BETA_TWO = 0.95
ADAM_EPS = 1e-08
DECAY = 0.1
OUTER_RATE = 0.7
OUTER_MOMENTUM = 0.9
REPLAY_WEIGHT = 0.25
RATES = (0.6, 0.04, 0.3, 0.03, 0.04, 0.02)
HEADS = 12
LEN = 128
STEPS = 2
STEP = 10


def entry_kernel(p_in, mv_in, e_in, whole, p_out, mv_out, pe_out, mve_out, e_out, p_box, mv_box, sends, recvs):
    place = Place()
    partners = ring_partners(place) + [place.other_core()]
    hail(partners)
    await_hails(partners)
    links = Links(sends, recvs)
    x, y, d = place.x, place.y, place.d
    h = lax.rem(place.g, 2)
    masters = [links.send(p_in.at[lax.rem(y + k, 4)], p_box.at[y], place.along_y(k)) for k in (1, 2, 3)]
    e_out[d, x, y] = e_in[...]
    mine = e_out.at[d, x, y]
    extra_z = links.send(mine, mine, place.other_dp())
    p_box[y] = p_in[y]
    mv_box[y] = mv_in[y]
    for copy in masters:
        copy.wait_recv()
    folded = p_box[...].astype(F32)
    master = jnp.concatenate([folded[:, :24], folded[:, 24:]], axis=2).reshape(2, 48, 768)
    p_out[...] = master

    @pl.when(h == 0)
    def _():
        whole[y, d, x, 0] = master[0].astype(BF16)

    @pl.when(h == 1)
    def _():
        whole[y, d, x, 1] = master[1].astype(BF16)

    def mix(a, b):
        return a * (1 - h) + b * h

    def near1(step, over=0):
        one, two = place.along_x(step, over), place.along_y(step, over)
        return {"dp": one["dp"], "expert": mix(one["expert"], two["expert"])}

    def near2(step):
        one, two = place.along_y(step), place.along_x(step)
        return {"dp": one["dp"], "expert": mix(one["expert"], two["expert"])}

    def at(k1, k2):
        return mix(k2, k1), mix(k1, k2)

    part = Gather(links, place, whole, h, mix(x, y), mix(y, x), near1, near2, at, place.other_core())
    part.start()
    extra_z.wait_recv()
    mine = e_out.at[:, x, y]
    extra_x = [links.send(mine, mine, place.along_x(k)) for k in (1, 2, 3)]
    part.ring_one()
    for copy in extra_x:
        copy.wait_recv()
    mine = e_out.at[:, :, y]
    extra_y = [links.send(mine, mine, place.along_y(k)) for k in (1, 2, 3)]
    part.ring_two()
    moments = [links.send(mv_in.at[lax.rem(y + k, 4)], mv_box.at[y], place.along_y(k)) for k in (1, 2, 3)]
    for copy in extra_y:
        copy.wait_recv()
    turned = e_out[...].reshape(768, 128).T
    pe_out[...] = turned[:24]
    mve_out[0] = turned[24:48]
    mve_out[1] = turned[48:72]
    part.end()
    for copy in moments:
        copy.wait_recv()
    moment = mv_box[...].astype(F32)
    for k in range(2):
        mv_out[k] = moment[:, 24 * k : 24 * k + 24].reshape(2, 48, 768)
    links.finish()


def adam_values(master, first, second, grad, rate, number):
    first = BETA_ONE * first + (1.0 - BETA_ONE) * grad
    second = BETA_TWO * second + (1.0 - BETA_TWO) * grad * grad
    level = second * (1.0 / (1.0 - BETA_TWO**number))
    below = level * lax.rsqrt(jnp.maximum(level, 1e-30)) + ADAM_EPS
    guess = pl.reciprocal(below, approx=True)
    update = first * ((1.0 / (1.0 - BETA_ONE**number)) * rate) * (guess * (2.0 - below * guess))
    return master - (update + (rate * DECAY) * master), first, second


def block_rate(place):
    return jnp.where(place.y == 3, RATES[2], RATES[1]).astype(F32)


def extra_rates():
    row = lax.broadcasted_iota(jnp.int32, (24, 768), 0)
    return jnp.where(row < 17, RATES[3], RATES[0]).astype(F32)


def renew_part(number, place, links, grads, extra, scratch, p_in, mv_in, pe_in, mve_in,
               whole, p_out, mv_out, pe_out, mve_out):
    sums, total = reduce_all(links, place, grads, extra, scratch)
    parts = gather_parts(links, place, whole)
    for h, part in enumerate(parts):
        fresh, first, second = adam_values(p_in[h], mv_in[0, h], mv_in[1, h], sums[h], block_rate(place), number)
        whole[place.y, place.d, place.x, h] = fresh.astype(BF16)
        part.start()
        p_out[h] = fresh
        mv_out[0, h] = first
        mv_out[1, h] = second
    pe_out[...], mve_out[0], mve_out[1] = adam_values(pe_in[...], mve_in[0], mve_in[1], total, extra_rates(), number)
    run_gather(parts)


def outer(begin, moment, mean):
    renewed = OUTER_MOMENTUM * moment + mean
    return begin - OUTER_RATE * (mean + OUTER_MOMENTUM * renewed), renewed


def own_features(place, rows, turned):
    at = 24 * (16 * place.d + 4 * place.x + place.y)
    pick = (lax.broadcasted_iota(jnp.int32, (768, 24), 0) == at + lax.broadcasted_iota(jnp.int32, (768, 24), 1)).astype(BF16)
    total = 0.0
    for _ in range(3):
        part = rows.astype(BF16)
        total = total + (
            lax.dot_general(pick, part, (((0,), (1,)), ((), ())), preferred_element_type=F32) if turned
            else lax.dot_general(part, pick, (((1,), (0,)), ((), ())), preferred_element_type=F32)
        )
        rows = rows - part.astype(F32)
    return total


class ExpertMean:
    def __init__(self, links, place, copies, deltas, own, other, sent, far):
        self.links, self.place, self.deltas = links, place, deltas
        self.own, self.other, self.sent, self.far = own, other, sent, far
        self.core, self.high = lax.rem(place.g, 2), lax.div(place.g, 2)
        self.loads = [copies.start(delta.at[:, self.core], own.at[k]) for k, delta in enumerate(deltas)]

    def start(self):
        self.first = [
            self.links.send(delta.at[:, 1 - self.core], self.other.at[k], self.place.other_core())
            for k, delta in enumerate(self.deltas)
        ]

    def middle(self, k):
        self.loads[k].wait()
        self.first[k].wait_recv()
        self.sent[k] = (
            self.own[k, 1 - self.high].astype(F32) + self.other[k, 1 - self.high].astype(F32)
        ).astype(BF16)
        self.second = getattr(self, "second", [])
        self.second.append(self.links.send(self.sent.at[k], self.far.at[k], self.place.in_group(2)))

    def mean(self, k):
        self.second[k].wait_recv()
        mine = self.own[k, self.high].astype(F32) + self.other[k, self.high].astype(F32)
        return (mine + self.far[k].astype(F32)) * 0.25


def final_part(number, place, links, grads, extra, scratch, experts, p_in, mv_in, pe_in, mve_in, p_start, pe_start,
               turned, flat_out, turned_out, delta, quarters, whole, boxes):
    g, y = place.g, place.y

    def between(i):
        if i >= 2:
            experts.middle(i - 2)

    sums, total = reduce_all(links, place, grads, extra, scratch, between)
    for h in range(2):
        fresh, _, _ = adam_values(p_in[h], mv_in[0, h], mv_in[1, h], sums[h], block_rate(place), number)
        delta[2 * h : 2 * h + 2] = (p_start[h] - fresh).reshape(2, 24, 768)
    summed = [
        links.send(delta.at[lax.rem(g + k, 4)], quarters.at[g], place.in_group(k)) for k in (1, 2, 3)
    ]
    fresh_e, _, _ = adam_values(pe_in[...], mve_in[0], mve_in[1], total, extra_rates(), number)
    sum_e = add_over(links, pe_start[...] - fresh_e, boxes, g, 4, place.in_group)
    quarters[g] = delta[g]
    for copy in summed:
        copy.wait_recv()
    whole[g] = (quarters[0] + quarters[1] + quarters[2] + quarters[3]) * 0.25
    spread = [links.send(whole.at[g], whole.at[g], place.in_group(k)) for k in (1, 2, 3)]
    mean_e = sum_e() * 0.25
    flat_out[...] = own_features(place, mean_e, False)
    turned_out[...] = own_features(place, mean_e, True)
    for copy in spread:
        copy.wait_recv()
    turned[y] = whole[y]
    across = [links.send(whole.at[lax.rem(y + k, 4)], turned.at[y], place.along_y(k)) for k in (1, 2, 3)]
    for copy in across:
        copy.wait_recv()


def semaphores(count):
    return [pltpu.SemaphoreType.DMA((count,)), pltpu.SemaphoreType.DMA((count,))]


ANY = pl.ANY
WHOLE = (4, 2, 4, 2, 48, 768)
BLOCK = (2, 48, 768)
ROW = (128, 768)


def call(kernel, outs, scratch, collective_id, args, limit=60 << 20):
    return pl.pallas_call(
        kernel,
        out_shape=tuple(jax.ShapeDtypeStruct(shape, kind) for _, shape, kind in outs),
        in_specs=[pl.BlockSpec(memory_space=space) for space, _ in args],
        out_specs=tuple(pl.BlockSpec(memory_space=space) for space, _, _ in outs),
        scratch_shapes=scratch,
        compiler_params=pltpu.CompilerParams(
            collective_id=collective_id, has_side_effects=True, vmem_limit_bytes=limit
        ),
    )(*(array for _, array in args))


def entry_call(p_in, mv_in, e_in):
    return call(
        entry_kernel,
        [(VMEM, WHOLE, BF16), (VMEM, BLOCK, F32), (VMEM, (2, *BLOCK), F32), (VMEM, (24, 768), F32),
         (VMEM, (2, 24, 768), F32)],
        [VMEM((2, 4, 4, 24, 128), F32), VMEM((4, 48, 384), BF16), VMEM((4, 48, 768), BF16)]
        + semaphores(3 + 7 + 23 + 3 + 16), 1,
        [(VMEM, p_in), (VMEM, mv_in), (VMEM, e_in)],
    )

CAP = 24
TOK = 128
DIMS = {"nn": (((1,), (0,)), ((), ())), "nt": (((1,), (1,)), ((), ())), "tn": (((0,), (0,)), ((), ()))}


def mm(a, b, form="nn"):
    return lax.dot_general(a, b, DIMS[form], preferred_element_type=F32)


def split_low(values):
    high = values.astype(BF16)
    return high, (values - high.astype(F32)).astype(BF16)


def row_scale(values):
    return lax.rsqrt(jnp.mean(values * values, axis=-1, keepdims=True) + EPS_NORM)


def iota(shape, dim):
    return lax.broadcasted_iota(jnp.int32, shape, dim)


def routing(ids):
    names = [(iota((24, TOK), 0) == ids[k : k + 1]).astype(F32) for k in range(2)]
    either = names[0] + names[1]
    earlier = (iota((TOK, TOK), 0) < iota((TOK, TOK), 1)).astype(BF16)
    slot = mm(either.astype(BF16), earlier).astype(jnp.int32)
    taken = jnp.where(iota((17, CAP, TOK), 1) == slot[:17][:, None, :], 1.0, 0.0)
    return names, taken * either[:17][:, None, :]


def pair_stack(part):
    lane = iota(part.shape, 1)
    zero = jnp.zeros_like(part)
    return jnp.concatenate([jnp.where(lane < 64, part, zero), jnp.where(lane < 64, zero, part)], axis=0)


def side_by_side(stacked):
    return jnp.concatenate([stacked[:TOK], stacked[TOK:]], axis=1)


def flat(whole, c):
    return whole[c].reshape(768, 768)


def cotangent(og_ref, ids_ref):
    factor = jnp.where(ids_ref[2:3] > 0, REPLAY_WEIGHT, 1.0)
    spread = jnp.where(iota((TOK, TOK), 0) == iota((TOK, TOK), 1), factor, 0.0).astype(BF16)
    return mm(spread, og_ref[...])


def front_part(x_ref, og_ref, ids_ref, pe_ref, whole,
               send, frozen, qkv_out, probs_out, mixed_out, middle_out, a1_out, a2_out, weights_out):
    gain = pe_ref[16:24].astype(BF16).astype(F32)
    x = x_ref[...].astype(F32)
    a1 = (x * row_scale(x) * gain[1:2]).astype(BF16)
    a1_out[...] = a1
    for c in range(3):
        qkv_out[c] = mm(a1, flat(whole, c)).astype(BF16)
    row, col = iota((2 * TOK, TOK), 0), iota((2 * TOK, TOK), 1)
    causal = lax.rem(row, TOK) >= col
    for pair in range(6):
        lanes = slice(128 * pair, 128 * pair + 128)
        scores = mm(pair_stack(qkv_out[0, :, lanes]), qkv_out[1, :, lanes], "nt") * 0.125
        scores = jnp.where(causal, scores, -1e30)
        expo = jnp.exp(scores - jnp.max(scores, axis=-1, keepdims=True))
        probs = expo / jnp.sum(expo, axis=-1, keepdims=True)
        probs_out[pair] = probs
        mixed_out[:, lanes] = mm(side_by_side(probs.astype(BF16)), pair_stack(qkv_out[2, :, lanes])).astype(BF16)
    middle = x + mm(mixed_out[...], flat(whole, 3))
    middle_out[...] = middle
    a2 = (middle * row_scale(middle) * gain[2:3]).astype(BF16)
    a2_out[...] = a2
    logits = mm(pe_ref[...].astype(BF16), a2, "nt")
    names, taken = routing(ids_ref[...])
    picked = [jnp.sum(name * logits, axis=0, keepdims=True) for name in names]
    top = jnp.maximum(picked[0], picked[1])
    expo = [jnp.exp(z - top) for z in picked]
    whole_sum = expo[0] + expo[1]
    weights = [e / whole_sum for e in expo]
    weights_out[...] = jnp.concatenate(weights + [jnp.zeros((6, TOK), F32)], axis=0)
    by_expert = names[0] * weights[0] + names[1] * weights[1]
    row_weight = jnp.sum(taken * by_expert[:17][:, None, :], axis=-1, keepdims=True)
    cot = cotangent(og_ref, ids_ref).astype(BF16)
    low = taken.astype(BF16).reshape(17 * CAP, TOK)
    rows = mm(low, a2).reshape(17, CAP, 768)
    grads = mm(low, cot).reshape(17, CAP, 768) * row_weight
    both = jnp.concatenate([rows, grads], axis=1).astype(BF16)
    frozen[...] = both[0]
    send[...] = both[1:]


def back_part(x_ref, og_ref, ids_ref, pe_ref, whole, qkv, probs_ref, mixed, middle_ref, a1, a2,
              weights_ref, ret, frozen, block_out, grad_out, grads, arrived):
    gain = pe_ref[16:24].astype(BF16).astype(F32)
    low_rows = pe_ref[...].astype(BF16)
    cot = cotangent(og_ref, ids_ref)
    names, taken = routing(ids_ref[...])
    weights = [weights_ref[k : k + 1] for k in range(2)]
    by_expert = names[0] * weights[0] + names[1] * weights[1]
    row_weight = jnp.sum(taken * by_expert[:17][:, None, :], axis=-1, keepdims=True)
    low = taken.astype(BF16).reshape(17 * CAP, TOK)
    both = ret[...].astype(F32)
    both = jnp.concatenate([frozen[...][None], both], axis=0)
    results, back = both[:, :CAP], both[:, CAP:].reshape(17 * CAP, 768)
    high, rest = split_low((results * row_weight).reshape(17 * CAP, 768))
    middle = middle_ref[...]
    block_out[...] = (middle + mm(low, high, "tn") + mm(low, rest, "tn")).astype(BF16)
    cot_rows = mm(low, cot.astype(BF16)).reshape(17, CAP, 768)
    grad_row = jnp.sum(cot_rows * results, axis=-1, keepdims=True)
    by_name = jnp.concatenate([jnp.sum(taken * grad_row, axis=1), jnp.zeros((7, TOK), F32)], axis=0)
    grad_w = [jnp.sum(name * by_name, axis=0, keepdims=True) for name in names]
    mean = weights[0] * grad_w[0] + weights[1] * grad_w[1]
    grad_logits = sum(names[k] * (weights[k] * (grad_w[k] - mean)) for k in range(2))
    high, rest = split_low(grad_logits)
    grad_router = mm(high, a2[...]) + mm(rest, a2[...])
    da2 = mm(high, low_rows, "tn") + mm(rest, low_rows, "tn")
    high, rest = split_low(back)
    da2 = da2 + mm(low, high, "tn") + mm(low, rest, "tn")
    scale = row_scale(middle)
    normed = middle * scale
    dg2 = jnp.sum(normed * da2, axis=0, keepdims=True)
    into = da2 * gain[2:3]
    dmiddle = cot + scale * (into - normed * jnp.mean(into * normed, axis=-1, keepdims=True))
    branch = dmiddle.astype(BF16)
    arrived()
    grads[3] = mm(mixed[...], branch, "tn").astype(BF16).reshape(2, 4, 2, 48, 768)
    dmixed = mm(branch, flat(whole, 3), "nt").astype(BF16)
    da1 = jnp.zeros((TOK, 768), F32)
    parts = [[], [], []]
    for pair in range(6):
        lanes = slice(128 * pair, 128 * pair + 128)
        probs = probs_ref[pair]
        dms = pair_stack(dmixed[:, lanes])
        parts[2].append(mm(probs.astype(BF16), dms, "tn").astype(BF16))
        dpb = mm(dms, qkv[2, :, lanes], "nt")
        ds = (probs * (dpb - jnp.sum(probs * dpb, axis=-1, keepdims=True))).astype(BF16)
        parts[0].append((mm(side_by_side(ds), pair_stack(qkv[1, :, lanes])) * 0.125).astype(BF16))
        parts[1].append((mm(ds, pair_stack(qkv[0, :, lanes]), "tn") * 0.125).astype(BF16))
    for c in range(3):
        dqkv = jnp.concatenate(parts[c], axis=1)
        grads[c] = mm(a1[...], dqkv, "tn").astype(BF16).reshape(2, 4, 2, 48, 768)
        da1 = da1 + mm(dqkv, flat(whole, c), "nt")
    x = x_ref[...].astype(F32)
    scale = row_scale(x)
    normed = x * scale
    dg1 = jnp.sum(normed * da1, axis=0, keepdims=True)
    into = da1 * gain[1:2]
    grad_out[...] = dmiddle + scale * (into - normed * jnp.mean(into * normed, axis=-1, keepdims=True))
    return jnp.concatenate([grad_router[:17], dg1, dg2, jnp.zeros((5, 768), F32)], axis=0)


SQRT_HALF = 0.7071067811865476
DENSITY = 0.3989422804014327


def expert_rows(rows, grad, first, second, turned):
    u = mm(rows, first)
    chance = 0.5 + 0.5 * lax.erf(u * SQRT_HALF)
    h = (u * chance).astype(BF16)
    value = mm(h, second, "nt" if turned else "nn")
    slope = chance + u * (jnp.exp(u * u * -0.5) * DENSITY)
    du = (slope * mm(grad, second, "nn" if turned else "nt")).astype(BF16)
    return value, mm(du, first, "nt"), h, du


class Copies:
    def __init__(self, sems):
        self.sems, self.used = sems, 0

    def start(self, src, dst):
        copy = pltpu.make_async_copy(src, dst, self.sems.at[self.used])
        self.used += 1
        copy.start()
        return copy


def grow_experts(first_step, number, copies, rows, grad, h, du, w1, w2, mv1, mv2, starts, news, bufs, between):
    (mv1_buf, mv2_buf, d1_buf, d2_buf, w1_out, w2_out, mv1_out, mv2_out, d1_out, d2_out) = bufs
    tiles = [(0, t) for t in range(6)] + [(1, t) for t in range(6)]

    def cut(which, t):
        return (pl.ds(128 * t, 128), slice(None)) if which == 0 else (slice(None), pl.ds(256 * t, 256))

    def load(n):
        which, t = tiles[n]
        slot = n % 2
        mv, buf = ((mv1, mv1_buf), (mv2, mv2_buf))[which]
        size = (128, 256)[which]
        begun = [copies.start(mv.at[:, pl.ds(size * t, size)], buf.at[slot])]
        if not first_step:
            begun.append(copies.start(starts[which].at[cut(which, t)], (d1_buf, d2_buf)[which].at[slot]))
        return begun

    loads = {0: load(0)}
    stores = {}
    for n, (which, t) in enumerate(tiles):
        slot = n % 2
        if n + 1 < len(tiles):
            loads[n + 1] = load(n + 1)
        for copy in loads[n]:
            copy.wait()
        for copy in stores.get(n - 2, []):
            copy.wait()
        if which == 0:
            value = mm(rows[:, 128 * t : 128 * t + 128], du[...], "tn")
            begin = w1[128 * t : 128 * t + 128].astype(F32)
            moments = mv1_buf
        else:
            value = mm(h[:, 256 * t : 256 * t + 256], grad[...], "tn")
            begin = w2[:, 256 * t : 256 * t + 256].T.astype(F32)
            moments = mv2_buf
        fresh, first, second = adam_values(
            begin, moments[slot, 0].astype(F32), moments[slot, 1].astype(F32), value, RATES[4 + which], number
        )
        here = cut(which, t)
        if first_step:
            low, mv_low = (w1_out, w2_out)[which], (mv1_out, mv2_out)[which]
            low[slot] = fresh.astype(BF16) if which == 0 else fresh.astype(BF16).T
            mv_low[slot, 0] = first.astype(BF16)
            mv_low[slot, 1] = second.astype(BF16)
            size = (128, 256)[which]
            stores[n] = [
                copies.start(low.at[slot], news[which].at[here]),
                copies.start(mv_low.at[slot], news[2 + which].at[:, pl.ds(size * t, size)]),
            ]
        else:
            change = (begin - fresh).astype(BF16)
            since = (d1_buf, d2_buf)[which][slot].astype(F32) - (w1, w2)[which][here].astype(F32)
            out = (d1_out, d2_out)[which]
            out[slot] = (since + (change if which == 0 else change.T).astype(F32)).astype(BF16)
            stores[n] = [copies.start(out.at[slot], news[which].at[here])]
        between(n)
    return stores[len(tiles) - 2] + stores[len(tiles) - 1]


KEPT = [((3, *ROW), BF16), ((6, 256, 128), F32), (ROW, BF16), (ROW, F32), (ROW, BF16), (ROW, BF16), ((8, 128), F32)]


def trade_kernel(first_step, number, *refs):
    (x, og, ids, pe, whole_hbm, both_hbm), refs = refs[:6], refs[6:]
    step = 0 if first_step else 1
    x, og, ids = x.at[step], og.at[step], ids.at[step]
    starts = [both_hbm.at[:, :1536], both_hbm.at[:, 1536:]]
    if first_step:
        w1_hbm, w2_hbm = starts
    else:
        (w1_hbm, w2_hbm), refs = refs[:2], refs[2:]
    (fin_hbm, fout_hbm, mv1, mv2), refs = refs[:4], refs[4:]
    kept_out, refs = refs[:7], refs[7:]
    ret, frozen_out, refs = refs[0], refs[1], refs[2:]
    count = 4 if first_step else 2
    news, refs = refs[:count], refs[count:]
    kept, refs = refs[:7], refs[7:]
    (whole, w1, w2, fin, fout, send, frozen_in, recv, ans, zret, home, rows_all, grad_all, h_all, du_all, local_sems,
     in_send, in_recv, z_send, z_recv, zb_send, zb_recv, home_send, home_recv), bufs = refs[:24], refs[24:]
    copies = Copies(local_sems)
    loads = [
        copies.start(src, dst)
        for src, dst in ((whole_hbm, whole), (w1_hbm, w1), (w2_hbm, w2), (fin_hbm, fin), (fout_hbm, fout))
    ]
    d, e = lax.axis_index("dp"), lax.axis_index("expert")
    partner = {"dp": 1 - d}

    def ahead(k):
        return lax.rem(e + k, 16)

    def behind(k):
        return lax.rem(e + 16 - k, 16)

    barrier = pltpu.get_barrier_semaphore()

    @pl.loop(1, 16)
    def _(k):
        pl.semaphore_signal(barrier, inc=1, device_id={"expert": ahead(k)}, device_id_type=MESH)

    pl.semaphore_signal(barrier, inc=1, device_id=partner, device_id_type=MESH)
    loads[0].wait()
    front_part(x, og, ids, pe, whole, send, frozen_in, *kept)
    pl.semaphore_wait(barrier, 16)

    def remote(src, dst, sends, recvs, k, to):
        return pltpu.make_async_remote_copy(
            src_ref=src, dst_ref=dst, send_sem=sends.at[k], recv_sem=recvs.at[k], device_id=to, device_id_type=MESH
        )

    def to_expert(k):
        return remote(send.at[ahead(k)], recv.at[0, e], in_send, in_recv, k, {"expert": ahead(k)})

    def to_partner(k):
        return remote(recv.at[0, behind(k)], recv.at[1, behind(k)], z_send, z_recv, k, partner)

    def from_partner(k):
        return remote(ans.at[1, behind(k)], zret.at[behind(k)], zb_send, zb_recv, k, partner)

    def to_home(k):
        return remote(home.at[behind(k)], ret.at[e], home_send, home_recv, k, {"expert": behind(k)})

    @pl.loop(1, 16)
    def _(k):
        to_expert(k).start()

    recv[0, e] = send[e]
    to_partner(0).start()
    keeps = [copies.start(src, dst) for src, dst in zip(kept, kept_out)]

    @pl.loop(1, 16)
    def _(k):
        to_expert(k).wait_recv()
        to_partner(k).start()

    for copy in loads[1:3]:
        copy.wait()

    @pl.loop(0, 4)
    def _(j):
        other = lax.rem(lax.div(j + 1, 2) + 1, 2)
        half = lax.div(j, 2)

        @pl.when(other == 1)
        def _():
            @pl.loop(0, 8)
            def _(i):
                to_partner(half * 8 + i).wait_recv()

        blocks = [recv[other, behind(half * 8 + i)].astype(F32) for i in range(8)]
        rows = jnp.concatenate([b[:CAP] for b in blocks], axis=0).astype(BF16)
        grad = jnp.concatenate([b[CAP:] for b in blocks], axis=0).astype(BF16)
        value, back, h, du = expert_rows(rows, grad, w1[...], w2[...], True)
        at = pl.ds(pl.multiple_of(j * 192, 192), 192)
        rows_all[at] = rows
        grad_all[at] = grad
        h_all[at] = h
        du_all[at] = du
        for i in range(8):
            part = slice(i * CAP, (i + 1) * CAP)
            ans[other, behind(half * 8 + i)] = jnp.concatenate([value[part], back[part]], axis=0).astype(BF16)

        @pl.when(other == 1)
        def _():
            @pl.loop(0, 8)
            def _(i):
                from_partner(half * 8 + i).start()

    for copy in loads[3:]:
        copy.wait()
    both = frozen_in[...].astype(F32)
    value, back, _, _ = expert_rows(both[:CAP].astype(BF16), both[CAP:].astype(BF16), fin[...], fout[...], False)
    frozen_out[...] = jnp.concatenate([value, back], axis=0)

    def serve(k):
        from_partner(k).wait_recv()
        slot = behind(k)
        total = (ans[0, slot].astype(F32) + zret[slot].astype(F32)).astype(BF16)
        if k == 0:
            ret[e] = total
        else:
            home[slot] = total
            to_home(k).start()

    def between(n):
        for k in range(SERVED[n], SERVED[n + 1]):
            serve(k)

    for k in range(SERVED[0]):
        serve(k)
    left = grow_experts(
        first_step, number, copies, rows_all, grad_all, h_all, du_all, w1, w2, mv1, mv2, starts, news, bufs, between
    )

    @pl.loop(1, 16)
    def _(k):
        to_home(k).wait_recv()
        to_home(k).wait_send()
        to_expert(k).wait_send()

    @pl.loop(0, 16)
    def _(k):
        to_partner(k).wait_send()
        from_partner(k).wait_send()

    for copy in left + keeps:
        copy.wait()


SERVED = (5, 6, 7, 9, 10, 11, 12, 13, 15, 16, 16, 16, 16)


def trade_call(first_step, number, collective_id, small, *large):
    wide = (768, 1536)
    moment_kind = F32 if first_step else BF16
    news = [(ANY, wide, BF16)] * 2 + ([(ANY, (2, 768, 1536), BF16), (ANY, (2, 1536, 768), BF16)] if first_step else [])
    outs = [(ANY, *k) for k in KEPT] + [(VMEM, (16, 48, 768), BF16), (VMEM, (48, 768), F32)] + news
    t1, t2, c1, c2 = (2, 2, 128, 1536), (2, 2, 256, 768), (2, 128, 1536), (2, 768, 256)
    none = (8, 128)
    first = first_step
    bufs = [
        VMEM(t1, moment_kind), VMEM(t2, moment_kind),
        VMEM(none if first else c1, BF16), VMEM(none if first else c2, BF16),
        VMEM(c1 if first else none, BF16), VMEM(c2 if first else none, BF16),
        VMEM(t1 if first else none, BF16), VMEM(t2 if first else none, BF16),
        VMEM(none if first else c1, BF16), VMEM(none if first else c2, BF16),
    ]
    plane = (16, 48, 768)
    scratch = [VMEM(*k) for k in KEPT] + [
        VMEM(WHOLE, BF16), VMEM(wide, BF16), VMEM(wide, BF16), VMEM((768, 3072), BF16), VMEM((3072, 768), BF16),
        VMEM(plane, BF16), VMEM((48, 768), BF16), VMEM((2, *plane), BF16), VMEM((2, *plane), BF16),
        VMEM(plane, BF16), VMEM(plane, BF16),
        VMEM((768, 768), BF16), VMEM((768, 768), BF16), VMEM(wide, BF16), VMEM(wide, BF16),
        pltpu.SemaphoreType.DMA((72,)),
    ] + semaphores(16) * 4 + bufs
    args = [(VMEM, a) for a in small] + [(ANY, a) for a in large]
    return call(functools.partial(trade_kernel, first_step, number), outs, scratch, collective_id, args)


FETCHED = (0, 1, 2, 4)


def back_body(step, refs, scratch, copies, block_out, grad_out, grads, begin):
    (x, og, ids, pe), whole_hbm, kept, ret, frozen = refs[:4], refs[4], list(refs[5:12]), refs[12], refs[13]
    whole, buffers = scratch[0], scratch[1:5]
    loads = [copies.start(whole_hbm, whole)]
    for at, buffer in zip(FETCHED, buffers):
        loads.append(copies.start(kept[at], buffer))
        kept[at] = buffer

    def arrived():
        begin()
        for copy in loads:
            copy.wait()

    return back_part(
        x.at[step], og.at[step], ids.at[step], pe, whole, *kept, ret, frozen, block_out, grad_out, grads, arrived
    )


BACK_SCRATCH = [VMEM(WHOLE, BF16)] + [VMEM(*KEPT[at]) for at in FETCHED] + [VMEM(WHOLE, BF16), pltpu.SemaphoreType.DMA((16,))]


def renew_kernel(number, *refs):
    shared, (p_in, mv_in, pe_in, mve_in), refs = refs[:14], refs[14:18], refs[18:]
    (block_out, grad_out, whole, p_out, mv_out, pe_out, mve_out), refs = refs[:7], refs[7:]
    back_scratch, (grads, sems), refs = refs[:5], refs[5:7], refs[7:]
    scratch, (sends, recvs) = refs[:11], refs[11:]
    place = Place()
    partners = ring_partners(place)
    hail(partners)
    extra = back_body(
        0, shared, back_scratch, Copies(sems), block_out, grad_out, grads, lambda: await_hails(partners)
    )
    links = Links(sends, recvs)
    renew_part(number, place, links, grads, extra, scratch, p_in, mv_in, pe_in, mve_in,
               whole, p_out, mv_out, pe_out, mve_out)
    links.finish()


def final_kernel(number, *refs):
    shared, dense, refs = refs[:14], refs[14:20], refs[20:]
    deltas, refs = refs[:2], refs[2:]
    (block_out, grad_out, mean_out, flat_out, turned_out, expert_out), refs = refs[:6], refs[6:]
    back_scratch, (grads, sems), refs = refs[:5], refs[5:7], refs[7:]
    scratch, boxes, refs = refs[:11], refs[11:15], refs[15:]
    expert_scratch, (sends, recvs) = refs[:4], refs[4:]
    place = Place()
    partners = ring_partners(place) + [place.in_group(k) for k in (1, 2, 3)]
    hail(partners)
    copies, links = Copies(sems), Links(sends, recvs)
    experts = ExpertMean(links, place, copies, deltas, *expert_scratch)

    def begin():
        await_hails(partners)
        experts.start()

    extra = back_body(1, shared, back_scratch, copies, block_out, grad_out, grads, begin)
    final_part(
        number, place, links, grads, extra, scratch, experts, *dense, mean_out, flat_out, turned_out, *boxes
    )
    for k in range(2):
        expert_out[k] = experts.mean(k)
    links.finish()


def finish_kernel(*refs):
    given, refs = refs[:16], refs[16:]
    olds, refs = refs[:4], refs[4:]
    (block, grad, new_qkv, new_proj, new_mom_qkv, new_mom_proj, new_gains, new_router, new_mom_gains, new_mom_router,
     *news), (old_buf, new_buf, sems, *held) = refs[:14], refs[14:]
    copies = Copies(sems)
    rows = [copies.start(src, dst) for src, dst in zip(given, held)]
    loads = [copies.start(src, old_buf.at[n]) for n, src in enumerate(olds)]
    for copy in rows:
        copy.wait()
    (block0, block1, grad0, grad1, mean, flat_e, turned_e, experts,
     w_qkv, w_proj, mom_qkv, mom_proj, gains, router, mom_gains, mom_router) = held
    stores = []
    for k in range(2):
        for copy in loads[2 * k : 2 * k + 2]:
            copy.wait()
        new_buf[2 * k], new_buf[2 * k + 1] = outer(old_buf[2 * k], old_buf[2 * k + 1], experts[k])
        stores += [copies.start(new_buf.at[n], news[n]) for n in (2 * k, 2 * k + 1)]
    for n, (one, all_rows) in enumerate(((block0, block), (block1, block), (grad0, grad), (grad1, grad))):
        all_rows[n % 2] = one[...]
    new_gains[...], new_mom_gains[...] = outer(gains[...], mom_gains[...], flat_e[17:19])
    new_router[...], new_mom_router[...] = outer(router[...], mom_router[...], turned_e[:, :17])
    for c in range(3):
        lanes = slice(768 * c, 768 * c + 768)
        new_qkv[:, lanes], new_mom_qkv[:, lanes] = outer(w_qkv[:, lanes], mom_qkv[:, lanes], mean[c])
    new_proj[...], new_mom_proj[...] = outer(w_proj[...], mom_proj[...], mean[3])
    for copy in stores:
        copy.wait()


def finish_call(small, olds):
    part = (192, 1536)
    outs = [((2, *ROW), BF16), ((2, *ROW), F32), ((24, 2304), F32), ((24, 768), F32), ((24, 2304), F32), ((24, 768), F32),
            ((2, 24), F32), ((24, 17), F32), ((2, 24), F32), ((24, 17), F32)]
    return pl.pallas_call(
        finish_kernel,
        out_shape=tuple(jax.ShapeDtypeStruct(*out) for out in outs + [(part, F32)] * 4),
        in_specs=[pl.BlockSpec(memory_space=ANY)] * (len(small) + 4),
        out_specs=tuple([pl.BlockSpec(memory_space=VMEM)] * 10 + [pl.BlockSpec(memory_space=ANY)] * 4),
        scratch_shapes=[VMEM((4, *part), F32), VMEM((4, *part), F32), pltpu.SemaphoreType.DMA((24,))]
        + [VMEM(array.shape, array.dtype) for array in small],
        compiler_params=pltpu.CompilerParams(vmem_limit_bytes=60 << 20),
    )(*small, *olds)


def back_args(small, whole, kept, ret, frozen):
    args = [(VMEM, a) for a in small] + [(ANY, whole)]
    args += [(ANY if at in FETCHED else VMEM, a) for at, a in enumerate(kept)]
    return args + [(VMEM, ret), (VMEM, frozen)]


def renew_call(number, shared, *args):
    return call(
        functools.partial(renew_kernel, number),
        [(VMEM, ROW, BF16), (VMEM, ROW, F32), (VMEM, WHOLE, BF16), (VMEM, BLOCK, F32), (VMEM, (2, *BLOCK), F32),
         (VMEM, (24, 768), F32), (VMEM, (2, 24, 768), F32)],
        BACK_SCRATCH + REDUCE_SCRATCH + semaphores(REDUCE_COPIES + GATHER_COPIES), 2,
        back_args(*shared) + [(VMEM, a) for a in args],
    )


def final_call(number, shared, dense, deltas):
    box = VMEM((4, 24, 768), F32)
    part = (192, 1536)
    return call(
        functools.partial(final_kernel, number),
        [(VMEM, ROW, BF16), (VMEM, ROW, F32), (VMEM, (4, 24, 768), F32), (VMEM, (24, 24), F32), (VMEM, (24, 24), F32),
         (VMEM, (2, *part), F32)],
        BACK_SCRATCH + REDUCE_SCRATCH + [box] * 4
        + [VMEM((2, 2, *part), BF16), VMEM((2, 2, *part), BF16), VMEM((2, *part), BF16), VMEM((2, *part), BF16)]
        + semaphores(REDUCE_COPIES + 12 + 4),
        3,
        back_args(*shared) + [(VMEM, a) for a in dense] + [(ANY, a) for a in deltas],
    )


def cols_and_square(wide, square):
    return jnp.stack([wide[:, :768], wide[:, 768:1536], wide[:, 1536:], square])


def body(
    tokens,
    out_grad,
    expert_ids,
    replay,
    frozen_in,
    frozen_out,
    gains,
    w_qkv,
    w_proj,
    router,
    exp_in,
    exp_out,
    mom_gains,
    mom_qkv,
    mom_proj,
    mom_router,
    mom_in,
    mom_out,
    state_gains,
    state_qkv,
    state_proj,
    state_router,
    state_in,
    state_out,
):
    both_low = jnp.concatenate([exp_in[0], jnp.swapaxes(exp_out[0], 0, 1)], axis=1).astype(BF16)
    both_low = lax.all_gather(both_low, "group", axis=0, tiled=True)
    low_start = cols_and_square(w_qkv, w_proj).astype(BF16)
    low_start = jnp.concatenate([low_start[:, :, :384], low_start[:, :, 384:]], axis=1)
    moments = jnp.concatenate([cols_and_square(state_qkv[0, k], state_proj[0, k]) for k in range(2)], axis=1).astype(BF16)
    gap = jnp.zeros((24, 5), F32)
    packed = jnp.concatenate(
        [router, gains.T, gap, state_router[0, 0], state_gains[0, 0].T, gap, state_router[0, 1], state_gains[0, 1].T,
         jnp.zeros((24, 61), F32)], axis=1,
    )
    ids = jnp.concatenate([jnp.swapaxes(expert_ids, 1, 2), replay[:, None], jnp.zeros((2, 5, 128), jnp.int32)], axis=1)
    whole, p_start, mv, pe_start, mve = entry_call(low_start, moments, packed)
    frozen_both = (frozen_in[0], frozen_out[0])
    small = (tokens, out_grad, ids, pe_start)
    made = trade_call(
        True, STEP, 4, small, whole, both_low, *frozen_both, state_in[0, :, 0], state_out[0, :, 0]
    )
    shared = (small, whole, made[:7], made[7], made[8])
    block0, grad0, whole, p_now, mv, pe_now, mve = renew_call(STEP, shared, p_start, mv, pe_start, mve)
    small = (tokens, out_grad, ids, pe_now)
    made = trade_call(False, STEP + 1, 5, small, whole, both_low, *made[9:11], *frozen_both, *made[11:13])
    shared = (small, whole, made[:7], made[7], made[8])
    dense = (p_now, mv, pe_now, mve, p_start, pe_start)
    deltas = tuple(delta.reshape(2, 2, 192, 1536) for delta in made[9:11])
    block1, grad1, *means = final_call(STEP + 1, shared, dense, deltas)
    turn = lambda array: jnp.swapaxes(array[0], 0, 1)
    back = lambda array: jnp.swapaxes(array, 0, 1)[None]
    (block, grad, new_qkv, new_proj, new_mom_qkv, new_mom_proj, new_gains, new_router, new_mom_gains, new_mom_router,
     new_in, new_mom_in, new_out, new_mom_out) = finish_call(
        (block0, block1, grad0, grad1, *means, w_qkv, w_proj, mom_qkv, mom_proj, gains, router, mom_gains, mom_router),
        (exp_in[0], mom_in[0], turn(exp_out), turn(mom_out)),
    )
    return (
        block, grad, new_gains, new_qkv, new_proj, new_router, new_in[None], back(new_out),
        new_mom_gains, new_mom_qkv, new_mom_proj, new_mom_router, new_mom_in[None], back(new_mom_out),
    )


def solution(mesh):
    return jax.shard_map(
        body,
        mesh=mesh,
        in_specs=(
            P(None, ("group", "dp", "expert"), None),
            P(None, ("group", "dp", "expert"), None),
            P(None, ("group", "dp", "expert"), None),
            P(None, ("group", "dp", "expert")),
            P(),
            P(),
            P(None, ("dp", "expert")),
            P(("dp", "expert"), None),
            P(("dp", "expert"), None),
            P(("dp", "expert"), None),
            P("expert", "group", "dp"),
            P("expert", "dp", "group"),
            P(None, ("dp", "expert")),
            P(("dp", "expert"), None),
            P(("dp", "expert"), None),
            P(("dp", "expert"), None),
            P("expert", "group", "dp"),
            P("expert", "dp", "group"),
            P("group", None, None, ("dp", "expert")),
            P("group", None, ("dp", "expert"), None),
            P("group", None, ("dp", "expert"), None),
            P("group", None, ("dp", "expert"), None),
            P("group", None, "expert", None, "dp"),
            P("group", None, "expert", "dp", None),
        ),
        out_specs=(
            P(None, ("group", "dp", "expert"), None),
            P(None, ("group", "dp", "expert"), None),
            P(None, ("dp", "expert")),
            P(("dp", "expert"), None),
            P(("dp", "expert"), None),
            P(("dp", "expert"), None),
            P("expert", "group", "dp"),
            P("expert", "dp", "group"),
            P(None, ("dp", "expert")),
            P(("dp", "expert"), None),
            P(("dp", "expert"), None),
            P(("dp", "expert"), None),
            P("expert", "group", "dp"),
            P("expert", "dp", "group"),
        ),
        check_vma=False,
    )
```

time: 540 us -> 399 us (0.74)
  Pallas kernels: 440 us -> 368 us
  local copies, waits for them, and re-layouts: 64.9 us -> 1.5 us
  other arithmetic: 17.2 us -> 4.76 us
    pallas_call x13 -> x6, Pallas kernels: 440 us -> 368 us  [the longest x5 361 us: call(): pl.pallas_call(kernel, out_shape=tuple((jax.ShapeDtypeStruct(shape, kind)...]
    unnamed x165 -> x25, local copies, waits for them, and re-layouts: 55.8 us -> 0.45 us
    sub x3 -> x0, other arithmetic: 5.49 us -> none  [body(): new_params.append(begin - OUTER_RATE * (delta + OUTER_MOMENTUM * renewed))]
  transfers between devices with their start and end apart: 3 -> 1, of which waited for: 0 -> 1; matrix products, arithmetic and copies ran while one was open for 5% -> 1% of each run, Pallas kernels for 28% -> 10%
where the time goes in v3:
time: 399 us; the launch traced here: 393 us
  Pallas kernels  368 us (92%)
  between operations  14.5 us (4%)
  other arithmetic  4.76 us (1%)
  waiting for transfers between devices  4.13 us (1%)
    pallas_call x5, Pallas kernels, call(): pl.pallas_call(kernel, out_shape=tuple((jax.ShapeDtypeStruct(shape, kind)...  361 us
  transfers between devices with their start and end apart: 1, of which 1 were waited for; matrix products, arithmetic and copies ran while one was open for 1% of the time, Pallas kernels for 10%

profile of v3, /device:TPU:1, one launch (start us, length us, event | category | flops | bytes accessed | tf_op | source)
XLA Modules:
  0.0 393.1 jit_solution(1989194066856365199)
XLA Ops:
  7.2 0.0 copy-start
  7.2 0.0 all-gather.2.cloned.1.call-start
  7.2 1.4 bitcast_convert_fusion.1
  8.7 0.1 copy-done
  8.8 0.0 copy-start.8
  8.8 0.0 copy-start.7
  8.8 0.0 copy-start.6
  8.8 0.0 copy-start.3
  8.8 0.1 bitcast_convert_fusion
  8.9 0.0 copy-start.1
  8.9 0.0 copy-start.5
  8.9 0.0 copy-start.2
  8.9 0.0 copy-start.4
  8.9 1.1 pad_maximum_fusion
  10.1 0.0 all-gather.2.cloned.1.call-update
  10.1 0.0 copy-start.9
  10.1 0.0 copy-start.10
  10.1 0.1 pad.18.clone
  10.2 0.0 copy-done.8
  10.2 0.1 copy.42
  10.3 0.1 copy.40
  10.4 0.0 copy-done.7
  10.4 0.1 copy.38
  10.5 0.0 copy-done.6
  10.5 0.1 copy.44
  10.6 0.1 copy.43
  10.7 0.0 copy-done.3
  10.7 0.0 copy-done.1
  10.7 0.0 copy-done.5
  10.7 0.7 concatenate.20.e_in
  11.4 0.0 copy-done.2
  11.5 0.7 pad_maximum_fusion.2.p_in
  12.2 0.0 copy-done.4
  12.3 0.7 maximum_maximum_fusion.mv_in
  13.0 39.0 %shard_map.335 = (bf16[4,2,4,2,48,768]{5,4,3,2,1,0:T(8,128)(2,1)}, f32[2,48,768]{2,1,0:T(8,128)}, f32[2,2,48,768]{3,2,1,0:T(8,128)}, f32[24,768]{1,0:T(8,128)}, f32[2,24,768]{2,1,0:T(8,128)}) custom-call(bf16[4,48,384]{2,1,0:T(8,128)(2,1)} %pad_maximum_fusion.2.p_in, bf16[4,48,768]{2,1,0:T(8,128)(2,1)} %maximum_maximum_fusion.mv_in, f32[24,128]{1,0:T(8,128)} %concatenate.20.e_in), custom_call_target="tpu_custom_call" | custom-call | tf_op jit(solution)/shard_map/pallas_call | solution.py:472
  52.0 0.0 copy-done.9
  52.0 0.0 copy-done.10
  52.0 0.7 add_add_fusion.refs_2_
  52.7 4.1 %all-gather.2.cloned.1.call-done.refs_5_ = bf16[768,3072]{1,0:T(8,128)(2,1)} async-done(((bf16[192,3072]{1,0:T(8,128)(2,1)}), bf16[768,3072]{1,0:T(8,128)(2,1)}) %all-gather.2.cloned.1.call-update) | async-done | bytes 4718608 | tf_op jit(solution)/shard_map/all_gather | solution.py:1083
  56.8 78.0 %shard_map.336 = (bf16[3,128,768]{2,1,0:T(8,128)(2,1)}, f32[6,256,128]{2,1,0:T(8,128)}, bf16[128,768]{1,0:T(8,128)(2,1)}, f32[128,768]{1,0:T(8,128)}, bf16[128,7...) custom-call(bf16[2,128,768]{2,1,0:T(8,128)(2,1)} %refs_0_.7, ...), custom_call_target="tpu_custom_call" | custom-call | tf_op jit(solution)/shard_map/pallas_call | solution.py:472
  134.9 83.3 %shard_map.337 = (bf16[128,768]{1,0:T(8,128)(2,1)}, f32[128,768]{1,0:T(8,128)}, bf16[4,2,4,2,48,768]{5,4,3,2,1,0:T(8,128)(2,1)}, f32[2,48,768]{2,1,0:T(8,128)}, ...) custom-call(bf16[2,128,768]{2,1,0:T(8,128)(2,1)} %refs_0_.7, bf16[2,128,768]{2,1,0:T(8,128)(2,1)} %refs_1_.7, ...), custom_call_target="tpu_custom_call" | custom-call | tf_op jit(solution)/shard_map/pallas_call | solution.py:472
  218.2 76.3 %shard_map.338 = (bf16[3,128,768]{2,1,0:T(8,128)(2,1)}, f32[6,256,128]{2,1,0:T(8,128)}, bf16[128,768]{1,0:T(8,128)(2,1)}, f32[128,768]{1,0:T(8,128)}, bf16[128,7...) custom-call(bf16[2,128,768]{2,1,0:T(8,128)(2,1)} %refs_0_.7, ...), custom_call_target="tpu_custom_call" | custom-call | tf_op jit(solution)/shard_map/pallas_call | solution.py:472
  294.5 84.4 %shard_map.339 = (bf16[128,768]{1,0:T(8,128)(2,1)}, f32[128,768]{1,0:T(8,128)}, f32[4,24,768]{2,1,0:T(8,128)}, f32[24,24]{1,0:T(8,128)}, f32[24,24]{1,0:T(8,128)}, /*index=5*/f32[2,192,1536]{2,1,0:T(8,128)}) custom-call(bf16[2,128,768]{2,1,0:T(8,128)(2,1)} %refs_0_.7, bf16[2,128,768]{2,1,0:T(8,128)(2,1)} %refs_1_.7, s32[2,8,128]{2,1,0:T(8,128)} %add_add_fusion.refs_2_, ...), custom_call_target="tpu_custom_call" | custom-call | tf_op jit(solution)/shard_map/pallas_call | solution.py:472
  378.9 7.1 %shard_map.340 = (bf16[2,128,768]{2,1,0:T(8,128)(2,1)}, f32[2,128,768]{2,1,0:T(8,128)}, f32[24,2304]{1,0:T(8,128)}, f32[24,768]{1,0:T(8,128)}, f32[24,2304]{1,0:...) custom-call(bf16[128,768]{1,0:T(8,128)(2,1)} %get-tuple-element.84.r, ...), custom_call_target="tpu_custom_call" | custom-call | tf_op jit(solution)/shard_map/pallas_call | solution.py:1010
  (14 shorter events, 0.2 us)
Async XLA Ops:
  7.2 1.6 copy-start
  7.2 49.6 %all-gather.2.cloned.1.call-start = ((), (), s32[]{:S(2)}) async-start(), calls=%async_computation | async-start | bytes 5898240 | tf_op jit(solution)/shard_map/all_gather | solution.py:1083
  8.8 1.4 copy-start.8
  8.8 1.6 copy-start.7
  8.8 1.7 copy-start.6
  8.8 1.9 copy-start.3
  8.9 1.8 copy-start.1
  8.9 1.8 copy-start.5
  8.9 2.5 copy-start.2
  8.9 3.3 copy-start.4
  10.1 41.9 %copy-start.9 = (s32[2,128,2]{1,2,0:T(2,128)S(1)}, s32[2,128,2]{1,2,0:T(2,128)}, u32[]{:S(2)}) copy-start(s32[2,128,2]{1,2,0:T(2,128)} %param.26) | copy-start | bytes 6148
  10.1 41.9 %copy-start.10 = (s32[2,128]{1,0:T(2,128)S(1)}, s32[2,128]{1,0:T(2,128)}, u32[]{:S(2)}) copy-start(s32[2,128]{1,0:T(2,128)} %param.27) | copy-start | bytes 3076
Sparse Core Ops, SparseCore 0:
  10.3 46.5 all-gather.1
